TPU v7x, 32 devices: a whole 2x2x4 slice. The times are simulated.
32 devices in a mesh: section: 2 (over x), dp: 4 (over z), seq: 4 (over y, core).
Axes of the slice: x: 2, y: 2, z: 4, core: 2. Of those that a mesh axis runs over, the one named last changes fastest.
Arguments:
- x_in: bfloat16 [2, 2, 4, 1024, 768], P('section', None, 'dp', 'seq'), may hold values from -18 to 18
- segments: int32 [2, 2, 4, 1024], P(None, None, 'dp', 'seq'), may hold values from 0 to 3, as said below
- cotangent: bfloat16 [2, 4, 1024, 768], P(None, 'dp', 'seq'), may hold values from -6 to 6
- attn_in: bfloat16 [2, 768, 2304], P('section'), may hold values from -0.15625 to 0.15625
- attn_out: bfloat16 [2, 768, 768], P('section'), may hold values from -0.625 to 0.625
- attn_bias: float32 [2, 6, 768], P('section'), may hold values from -1 to 1
- gains: float32 [2, 2, 768], P('section'), may hold values from 0.5 to 1.5
- ffn_in: bfloat16 [2, 768, 3072], P('section'), may hold values from -0.21875 to 0.21875
- ffn_bias: float32 [2, 3072], P('section'), may hold values from -1 to 1
- ffn_out: bfloat16 [2, 3072, 768], P('section'), may hold values from -0.109375 to 0.109375
- cross_q: bfloat16 [768, 768], replicated, may hold values from -0.3125 to 0.3125
- cross_kv: bfloat16 [768, 1536], replicated, may hold values from -0.21875 to 0.21875
- cross_out: bfloat16 [768, 768], replicated, may hold values from -0.625 to 0.625
- cross_bias: float32 [4, 768], replicated, may hold values from -1 to 1
- cross_gain: float32 [768], replicated, may hold values from 0.5 to 1.5
Outputs:
- layer_out: bfloat16 [2, 2, 4, 1024, 768], P('section', None, 'dp', 'seq')
- input_grad: bfloat16 [2, 2, 4, 1024, 768], P('section', None, 'dp', 'seq')
- stats: float32 [2, 2], P('section')
- attn_in_grad: float32 [2, 768, 2304], P('section', ('dp', 'seq'))
- attn_out_grad: float32 [2, 768, 768], P('section', ('dp', 'seq'))
- attn_bias_grad: float32 [2, 6, 768], P('section', None, ('dp', 'seq'))
- gains_grad: float32 [2, 2, 768], P('section', None, ('dp', 'seq'))
- ffn_in_grad: float32 [2, 768, 3072], P('section', ('dp', 'seq'))
- ffn_bias_grad: float32 [2, 3072], P('section', ('dp', 'seq'))
- ffn_out_grad: float32 [2, 3072, 768], P('section', ('dp', 'seq'))
- cross_q_grad: float32 [768, 768], P(('section', 'dp', 'seq'))
- cross_kv_grad: float32 [768, 1536], P(('section', 'dp', 'seq'))
- cross_out_grad: float32 [768, 768], P(('section', 'dp', 'seq'))
- cross_bias_grad: float32 [4, 768], P(None, ('section', 'dp', 'seq'))
- cross_gain_grad: float32 [768], P(('section', 'dp', 'seq'))
Inputs may be any that keep to these rules, and one draw needn't show every extreme that they name: `segments`: ids of a row never fall, and each of 0, 1, 2, 3 appears in every row; document k of a target row attends to document k of the source row.
All inputs are finite; a program needn't handle non-finite values.
Results may differ from a plain program's by a relative error of at most 0.025.
Values may be sent and summed in bfloat16 or wider, within the bound.
A program may use at most 384 MiB of HBM per device.

v0:
```python
from functools import partial
import math

import jax
import jax.numpy as jnp
from jax import lax
from jax.sharding import PartitionSpec as P

HEADS = 12
HEAD_DIM = 64


EPSILON = 1e-05
MASKED = -1000000000.0


def for_sending(x):
    return jax.tree.map(lambda a: a.astype(jnp.bfloat16) if a.dtype == jnp.float32 else a, x)


def from_behind(x, axis, by):
    length = lax.axis_size(axis)
    pairs = [(i, i + by) for i in range(length) if 0 <= i + by < length]
    return lax.ppermute(x, axis, pairs)


def norm_apply(tensor, scale_gain, offset):
    average = jnp.mean(tensor, -1, keepdims=True)
    centered = tensor - average
    spread = jnp.mean(centered * centered, -1, keepdims=True)
    return centered * lax.rsqrt(spread + EPSILON) * scale_gain + offset


def exact_gelu(tensor):
    return jax.nn.gelu(tensor, approximate=False)


def project(activation, weight, offset):
    return jnp.dot(activation, weight, preferred_element_type=jnp.float32) + offset


def project_back(gradient, weight):
    return jnp.einsum("rsj,ij->rsi", gradient, weight, preferred_element_type=jnp.float32)


def weight_grad(activation, gradient):
    return jnp.einsum("rsi,rsj->ij", activation, gradient, preferred_element_type=jnp.float32)


def column_total(gradient):
    return jnp.sum(gradient.astype(jnp.float32), axis=(0, 1))


def pick_row(stacked, position):
    return lax.dynamic_index_in_dim(stacked, position, 0, keepdims=False)


def masked_scores(queries, key_rows, ids_query, ids_key, query_pos, key_pos, causal):
    row_count, length = (queries.shape[0], queries.shape[1])
    key_count = key_rows.shape[1]
    query_heads = queries.reshape(row_count, length, HEADS, HEAD_DIM)
    key_heads = key_rows.reshape(row_count, key_count, HEADS, HEAD_DIM)
    raw_scores = jnp.einsum(
        "rqhd,rkhd->rhqk", query_heads, key_heads, preferred_element_type=jnp.float32
    ) * (1.0 / math.sqrt(HEAD_DIM))
    before = (key_pos[None, :] <= query_pos[:, None]) | jnp.logical_not(causal)
    allowed = (ids_query[:, :, None] == ids_key[:, None, :]) & before[None]
    return jnp.where(allowed[:, None], raw_scores, MASKED)


def attend_forward(queries, key_rows, value_rows, ids_query, ids_key, query_pos, causal):
    key_pos = jnp.arange(key_rows.shape[1])
    scores = masked_scores(queries, key_rows, ids_query, ids_key, query_pos, key_pos, causal)
    row_peak = jnp.max(scores, -1, keepdims=True)
    log_total = row_peak + jnp.log(jnp.sum(jnp.exp(scores - row_peak), -1, keepdims=True))
    weights = jnp.exp(scores - log_total).astype(jnp.bfloat16)
    row_count, length = (queries.shape[0], queries.shape[1])
    value_heads = value_rows.reshape(row_count, value_rows.shape[1], HEADS, HEAD_DIM)
    mixed_heads = jnp.einsum(
        "rhqk,rkhd->rqhd", weights, value_heads, preferred_element_type=jnp.float32
    )
    return (
        mixed_heads.reshape(row_count, length, HEADS * HEAD_DIM).astype(jnp.bfloat16),
        log_total,
    )


def attend_back(
    queries, key_rows, value_rows, mixed_grad, log_total, ids_query, ids_key, query_pos, causal
):
    key_pos = jnp.arange(key_rows.shape[1])
    scores = masked_scores(queries, key_rows, ids_query, ids_key, query_pos, key_pos, causal)
    prob_rows = jnp.exp(scores - log_total)
    row_count, length = (queries.shape[0], queries.shape[1])
    key_count = key_rows.shape[1]
    query_heads = queries.reshape(row_count, length, HEADS, HEAD_DIM)
    key_heads = key_rows.reshape(row_count, key_count, HEADS, HEAD_DIM)
    value_heads = value_rows.reshape(row_count, key_count, HEADS, HEAD_DIM)
    grad_heads = mixed_grad.reshape(row_count, length, HEADS, HEAD_DIM)
    prob_grad = jnp.einsum(
        "rqhd,rkhd->rhqk", grad_heads, value_heads, preferred_element_type=jnp.float32
    )
    score_grad = (
        prob_rows * (prob_grad - jnp.sum(prob_rows * prob_grad, -1, keepdims=True))
    ).astype(jnp.bfloat16)
    scale_factor = 1.0 / math.sqrt(HEAD_DIM)
    query_grad = (
        jnp.einsum("rhqk,rkhd->rqhd", score_grad, key_heads, preferred_element_type=jnp.float32)
        * scale_factor
    )
    key_grad = (
        jnp.einsum("rhqk,rqhd->rkhd", score_grad, query_heads, preferred_element_type=jnp.float32)
        * scale_factor
    )
    value_grad = jnp.einsum(
        "rhqk,rqhd->rkhd",
        prob_rows.astype(jnp.bfloat16),
        grad_heads,
        preferred_element_type=jnp.float32,
    )
    width = HEADS * HEAD_DIM
    return (
        query_grad.reshape(row_count, length, width),
        key_grad.reshape(row_count, key_count, width),
        value_grad.reshape(row_count, key_count, width),
    )


def share_keys(key_local, value_local):
    return (
        lax.all_gather(for_sending(key_local), "seq", axis=1, tiled=True).astype(key_local.dtype),
        lax.all_gather(for_sending(value_local), "seq", axis=1, tiled=True).astype(
            value_local.dtype
        ),
    )


def return_key_grads(key_term, value_term):
    return (
        lax.psum_scatter(
            key_term.astype(jnp.bfloat16), "seq", scatter_dimension=1, tiled=True
        ).astype(jnp.float32),
        lax.psum_scatter(
            value_term.astype(jnp.bfloat16), "seq", scatter_dimension=1, tiled=True
        ).astype(jnp.float32),
    )


def per_device(
    x_in,
    segments,
    cotangent,
    attn_in,
    attn_out,
    attn_bias,
    gains,
    ffn_in,
    ffn_bias,
    ffn_out,
    cross_q,
    cross_kv,
    cross_out,
    cross_bias,
    cross_gain,
):
    section = lax.axis_index("section")
    seq_index = lax.axis_index("seq")
    decoder = section.astype(jnp.float32)
    causal = section == 1
    micro = x_in.shape[1]
    row_count = x_in.shape[2]
    shard_len = x_in.shape[3]
    width = x_in.shape[4]
    query_pos = seq_index * shard_len + jnp.arange(shard_len)
    whole_ids = lax.all_gather(segments, "seq", axis=3, tiled=True)
    own_ids_all = lax.dynamic_index_in_dim(whole_ids, section, 0, keepdims=False)
    source_ids_all = whole_ids[0]
    local_ids_all = lax.dynamic_index_in_dim(segments, section, 0, keepdims=False)
    inputs_all = x_in[0]
    w_qkv = attn_in[0]
    w_mix = attn_out[0]
    bias_rows = attn_bias[0]
    gain_rows = gains[0]
    w_inner = ffn_in[0]
    b_inner = ffn_bias[0]
    w_outer = ffn_out[0]
    zeros_row = jnp.zeros_like(bias_rows[0])
    qkv_bias = jnp.concatenate([bias_rows[0], zeros_row, bias_rows[1]])
    pair_bias = jnp.concatenate([zeros_row, cross_bias[1]])

    def layer_forward(inputs, memory, ids_local, ids_own, ids_source):
        qkv_rows = project(inputs, w_qkv, qkv_bias).astype(jnp.bfloat16)
        queries, key_local, value_local = jnp.split(qkv_rows, 3, axis=-1)
        key_rows, value_rows = share_keys(key_local, value_local)
        mixed, log_self = attend_forward(
            queries, key_rows, value_rows, ids_local, ids_own, query_pos, causal
        )
        branch = project(mixed, w_mix, bias_rows[2])
        summed = inputs.astype(jnp.float32) + branch
        hidden = norm_apply(summed, gain_rows[0], bias_rows[4])
        cross_query = project(hidden.astype(jnp.bfloat16), cross_q, cross_bias[0]).astype(
            jnp.bfloat16
        )
        pair_rows = project(memory, cross_kv, pair_bias).astype(jnp.bfloat16)
        cross_key_local, cross_value_local = jnp.split(pair_rows, 2, axis=-1)
        cross_keys, cross_values = share_keys(cross_key_local, cross_value_local)
        cross_mixed, log_cross = attend_forward(
            cross_query, cross_keys, cross_values, ids_local, ids_source, query_pos, False
        )
        cross_branch = project(cross_mixed, cross_out, cross_bias[2])
        cross_sum = hidden + cross_branch
        cross_normed = norm_apply(cross_sum, cross_gain, cross_bias[3])
        middle = hidden + decoder * (cross_normed - hidden)
        inner_act = project(middle.astype(jnp.bfloat16), w_inner, b_inner)
        activation = exact_gelu(inner_act).astype(jnp.bfloat16)
        ffn_branch = project(activation, w_outer, bias_rows[3])
        final_sum = middle + ffn_branch
        result = norm_apply(final_sum, gain_rows[1], bias_rows[5])
        kept_tick = {
            "inputs": inputs,
            "queries": queries,
            "key_local": key_local,
            "value_local": value_local,
            "log_self": log_self,
            "mixed": mixed,
            "summed": summed,
            "hidden": hidden,
            "cross_query": cross_query,
            "memory": memory,
            "cross_key_local": cross_key_local,
            "cross_value_local": cross_value_local,
            "log_cross": log_cross,
            "cross_mixed": cross_mixed,
            "cross_sum": cross_sum,
            "middle": middle,
            "inner_act": inner_act,
            "activation": activation,
            "final_sum": final_sum,
        }
        kept_tick["key_rows"] = key_rows
        kept_tick["value_rows"] = value_rows
        kept_tick["cross_keys"] = cross_keys
        kept_tick["cross_values"] = cross_values
        squares = jnp.stack([jnp.sum(summed * summed), jnp.sum(branch * branch)])
        return (result, kept_tick, squares)

    def forward_tick(state_pair, tick_index):
        memory, square_sums = state_pair
        micro_index = tick_index - section
        is_valid = ((micro_index >= 0) & (micro_index < micro)).astype(jnp.float32)
        safe_index = jnp.clip(micro_index, 0, micro - 1)
        inputs = pick_row(inputs_all, safe_index)
        result, kept_tick, squares = layer_forward(
            inputs,
            memory,
            pick_row(local_ids_all, safe_index),
            pick_row(own_ids_all, safe_index),
            pick_row(source_ids_all, safe_index),
        )
        sent_rows = result.astype(jnp.bfloat16)
        arrived = from_behind(sent_rows, "section", 1)
        return ((arrived, square_sums + is_valid * squares), (sent_rows, kept_tick))

    start_state = (
        jnp.zeros((row_count, shard_len, width), jnp.bfloat16),
        jnp.zeros((2,), jnp.float32),
    )
    (_, square_sums), (outputs_all, kept_all) = lax.scan(
        forward_tick, start_state, jnp.arange(micro + 1)
    )

    def layer_backward(kept_tick, out_grad, ids_local, ids_own, ids_source):
        key_rows, value_rows = (kept_tick["key_rows"], kept_tick["value_rows"])
        cross_keys, cross_values = (kept_tick["cross_keys"], kept_tick["cross_values"])
        _, back_final = jax.vjp(norm_apply, kept_tick["final_sum"], gain_rows[1], bias_rows[5])
        final_grad, gain_final, shift_final = back_final(out_grad)
        ffn_grad = final_grad.astype(jnp.bfloat16)
        grad_outer = weight_grad(kept_tick["activation"], ffn_grad)
        grad_b2 = column_total(ffn_grad)
        act_grad = project_back(ffn_grad, w_outer)
        _, back_gelu = jax.vjp(exact_gelu, kept_tick["inner_act"])
        inner_grad = back_gelu(act_grad)[0].astype(jnp.bfloat16)
        grad_inner = weight_grad(kept_tick["middle"].astype(jnp.bfloat16), inner_grad)
        grad_b1 = column_total(inner_grad)
        middle_grad = final_grad + project_back(inner_grad, w_inner)
        normed_grad = decoder * middle_grad
        hidden_grad = middle_grad - normed_grad
        _, back_cross = jax.vjp(norm_apply, kept_tick["cross_sum"], cross_gain, cross_bias[3])
        cross_sum_grad, grad_cgain, grad_cshift = back_cross(normed_grad)
        hidden_grad = hidden_grad + cross_sum_grad
        cross_branch_grad = cross_sum_grad.astype(jnp.bfloat16)
        grad_cout = weight_grad(kept_tick["cross_mixed"], cross_branch_grad)
        grad_cbo = column_total(cross_branch_grad)
        cross_mixed_grad = project_back(cross_branch_grad, cross_out).astype(jnp.bfloat16)
        cq_grad, ck_term, cv_term = attend_back(
            kept_tick["cross_query"],
            cross_keys,
            cross_values,
            cross_mixed_grad,
            kept_tick["log_cross"],
            ids_local,
            ids_source,
            query_pos,
            False,
        )
        ck_grad, cv_grad = return_key_grads(ck_term, cv_term)
        pair_grad = jnp.concatenate([ck_grad, cv_grad], -1).astype(jnp.bfloat16)
        cq_grad = cq_grad.astype(jnp.bfloat16)
        grad_cq = weight_grad(kept_tick["hidden"].astype(jnp.bfloat16), cq_grad)
        grad_cbq = column_total(cq_grad)
        hidden_grad = hidden_grad + project_back(cq_grad, cross_q)
        grad_ckv = weight_grad(kept_tick["memory"], pair_grad)
        grad_cbv = column_total(pair_grad)[width:]
        memory_grad = project_back(pair_grad, cross_kv)
        _, back_first = jax.vjp(norm_apply, kept_tick["summed"], gain_rows[0], bias_rows[4])
        summed_grad, gain_first, shift_first = back_first(hidden_grad)
        branch_grad = summed_grad.astype(jnp.bfloat16)
        grad_mix = weight_grad(kept_tick["mixed"], branch_grad)
        grad_bo = column_total(branch_grad)
        mixed_grad = project_back(branch_grad, w_mix).astype(jnp.bfloat16)
        q_grad, k_term, v_term = attend_back(
            kept_tick["queries"],
            key_rows,
            value_rows,
            mixed_grad,
            kept_tick["log_self"],
            ids_local,
            ids_own,
            query_pos,
            causal,
        )
        k_grad, v_grad = return_key_grads(k_term, v_term)
        qkv_grad = jnp.concatenate([q_grad, k_grad, v_grad], -1).astype(jnp.bfloat16)
        grad_qkv = weight_grad(kept_tick["inputs"], qkv_grad)
        qkv_total = column_total(qkv_grad)
        input_grad = summed_grad + project_back(qkv_grad, w_qkv)
        bias_grad = jnp.stack(
            [qkv_total[:width], qkv_total[2 * width :], grad_bo, grad_b2, shift_first, shift_final]
        )
        gain_grad = jnp.stack([gain_first, gain_final])
        cross_bias_grad = jnp.stack([grad_cbq, grad_cbv, grad_cbo, grad_cshift])
        grads = (
            grad_qkv,
            grad_mix,
            bias_grad,
            gain_grad,
            grad_inner,
            grad_b1,
            grad_outer,
            grad_cq,
            grad_ckv,
            grad_cout,
            cross_bias_grad,
            grad_cgain,
        )
        return (input_grad, memory_grad, grads)

    def backward_tick(state_pair, tick_index):
        arrived, totals = state_pair
        micro_index = tick_index - 1 + section
        is_valid = ((micro_index >= 0) & (micro_index < micro)).astype(jnp.float32)
        safe_index = jnp.clip(micro_index, 0, micro - 1)
        saved_at = jnp.clip(micro_index + section, 0, micro)
        kept_tick = jax.tree.map(partial(pick_row, position=saved_at), kept_all)
        from_cotangent = pick_row(cotangent, safe_index).astype(jnp.float32)
        out_grad = jnp.where(causal, from_cotangent, arrived.astype(jnp.float32)) * is_valid
        input_grad, memory_grad, grads = layer_backward(
            kept_tick,
            out_grad,
            pick_row(local_ids_all, safe_index),
            pick_row(own_ids_all, safe_index),
            pick_row(source_ids_all, safe_index),
        )
        sent_grad = memory_grad.astype(jnp.bfloat16)
        returned = from_behind(sent_grad, "section", -1)
        return ((returned, jax.tree.map(jnp.add, totals, grads)), input_grad.astype(jnp.bfloat16))

    grad_zeros = (
        jnp.zeros(w_qkv.shape, jnp.float32),
        jnp.zeros(w_mix.shape, jnp.float32),
        jnp.zeros((6, width), jnp.float32),
        jnp.zeros((2, width), jnp.float32),
        jnp.zeros(w_inner.shape, jnp.float32),
        jnp.zeros(b_inner.shape, jnp.float32),
        jnp.zeros(w_outer.shape, jnp.float32),
        jnp.zeros(cross_q.shape, jnp.float32),
        jnp.zeros(cross_kv.shape, jnp.float32),
        jnp.zeros(cross_out.shape, jnp.float32),
        jnp.zeros((4, width), jnp.float32),
        jnp.zeros((width,), jnp.float32),
    )
    back_start = (jnp.zeros((row_count, shard_len, width), jnp.bfloat16), grad_zeros)
    (_, totals), grads_in = lax.scan(backward_tick, back_start, jnp.arange(micro + 1))
    section_part = (
        lax.psum_scatter(totals[0][None], ("dp", "seq"), scatter_dimension=1, tiled=True),
        lax.psum_scatter(totals[1][None], ("dp", "seq"), scatter_dimension=1, tiled=True),
        lax.psum_scatter(totals[2][None], ("dp", "seq"), scatter_dimension=2, tiled=True),
        lax.psum_scatter(totals[3][None], ("dp", "seq"), scatter_dimension=2, tiled=True),
        lax.psum_scatter(totals[4][None], ("dp", "seq"), scatter_dimension=1, tiled=True),
        lax.psum_scatter(totals[5][None], ("dp", "seq"), scatter_dimension=1, tiled=True),
        lax.psum_scatter(totals[6][None], ("dp", "seq"), scatter_dimension=1, tiled=True),
    )
    cross_part = (
        lax.psum_scatter(totals[7], ("section", "dp", "seq"), scatter_dimension=0, tiled=True),
        lax.psum_scatter(totals[8], ("section", "dp", "seq"), scatter_dimension=0, tiled=True),
        lax.psum_scatter(totals[9], ("section", "dp", "seq"), scatter_dimension=0, tiled=True),
        lax.psum_scatter(totals[10], ("section", "dp", "seq"), scatter_dimension=1, tiled=True),
        lax.psum_scatter(totals[11], ("section", "dp", "seq"), scatter_dimension=0, tiled=True),
    )
    moments = lax.psum(square_sums, ("dp", "seq"))
    count = micro * row_count * lax.axis_size("dp") * shard_len * lax.axis_size("seq") * width
    stats = jnp.sqrt(moments / count)[None]
    layer_out = lax.dynamic_slice_in_dim(outputs_all, section, micro, 0)[None]
    input_grad = lax.dynamic_slice_in_dim(grads_in, 1 - section, micro, 0)[None]
    return (
        layer_out,
        input_grad,
        stats,
        section_part[0],
        section_part[1],
        section_part[2],
        section_part[3],
        section_part[4],
        section_part[5],
        section_part[6],
        cross_part[0],
        cross_part[1],
        cross_part[2],
        cross_part[3],
        cross_part[4],
    )


def solution(mesh):
    return jax.shard_map(
        per_device,
        mesh=mesh,
        in_specs=(
            P("section", None, "dp", "seq", None),
            P(None, None, "dp", "seq"),
            P(None, "dp", "seq", None),
            P("section", None, None),
            P("section", None, None),
            P("section", None, None),
            P("section", None, None),
            P("section", None, None),
            P("section", None),
            P("section", None, None),
            P(),
            P(),
            P(),
            P(),
            P(),
        ),
        out_specs=(
            P("section", None, "dp", "seq", None),
            P("section", None, "dp", "seq", None),
            P("section", None),
            P("section", ("dp", "seq"), None),
            P("section", ("dp", "seq"), None),
            P("section", None, ("dp", "seq")),
            P("section", None, ("dp", "seq")),
            P("section", ("dp", "seq"), None),
            P("section", ("dp", "seq")),
            P("section", ("dp", "seq"), None),
            P(("section", "dp", "seq"), None),
            P(("section", "dp", "seq"), None),
            P(("section", "dp", "seq"), None),
            P(None, ("section", "dp", "seq")),
            P(("section", "dp", "seq")),
        ),
        check_vma=False,
    )
```

profile of v0, /device:TPU:0, one launch (start us, length us, event | category | flops | bytes accessed | tf_op | source)
XLA Modules:
  0.0 1868.3 jit_solution(10089169057505979234)
XLA Ops:
  23.1 389.8 %while.94 = (s32[]{:T(128)}, bf16[1,256,768]{2,1,0:T(8,128)(2,1)S(1)}, f32[2]{0:T(128)S(1)}, bf16[3,1,256,768]{3,2,1,0:T(8,128)(2,1)}, bf16[3,1,256,3072]{3,2,1,...) while((s32[]{:T(128)}, ...), condition=%wide.region_13.14_spmd.clone, body=%wide.region_0.13_spmd.clone.sunk | while | flops 6582562304 | bytes 387940640 | solution.py:268
  35.9 14.1 all-gather.9.cloned.1.call-done
  59.2 12.6 all-gather.7.cloned.1.call-done
  188.5 12.5 all-gather.7.cloned.1.call-done
  296.6 11.7 all-gather.9.cloned.1.call-done
  317.5 12.5 all-gather.7.cloned.1.call-done
  414.6 551.9 %while.95 = (s32[]{:T(128)}, bf16[1,256,768]{2,1,0:T(8,128)(2,1)S(1)}, f32[768,2304]{1,0:T(8,128)}, f32[768,768]{1,0:T(8,128)}, f32[6,768]{1,0:T(8,128)}, /*inde...) while((s32[]{:T(128)}, ...), condition=%wide.region_46.47_spmd.clone, body=%wide.region_14.46_spmd.clone.sunk | while | flops 13903286272 | bytes 772435520 | solution.py:393
  469.6 12.3 multiply_reduce_fusion.32
  526.3 12.2 multiply_reduce_fusion.35
  646.4 12.2 multiply_reduce_fusion.32
  702.3 12.3 multiply_reduce_fusion.35
  827.5 12.0 multiply_reduce_fusion.32
  883.7 12.3 multiply_reduce_fusion.35
  978.4 32.5 %psum.7 = f32[2]{0:T(128)S(1)} all-reduce(f32[2]{0:T(128)S(1)} %copy-done.90), channel_id=1, replica_groups=mesh['section'=2,'dp'=4,'seq'=4] {'dp','seq'}, use_global_device_ids=true, to_apply=%region_47.48 | all-reduce | flops 2 | bytes 16 | tf_op jit(solution)/shard_map/psum | solution.py:410
  1010.9 37.1 %all-reduce.3 = (f32[4,768]{1,0:T(4,128)S(1)}, f32[768]{0:T(1024)S(1)}) all-reduce(f32[4,768]{1,0:T(4,128)S(1)} %copy-done.59, f32[768]{0:T(1024)S(1)} %copy-done.82), channel_id=16, replica_groups=mesh['section'=2,'dp'=4,'seq'=4] {'section','dp','seq'}, use_global_device_ids=true, to_apply=%region_58.59.clone | all-reduce | flops 3840 | bytes 30720
  1052.4 36.2 %reduce-scatter.40.cloned.1.call-done = f32[192,1]{1,0:T(8,128)} async-done(((f32[3072,1]{1,0:T(8,128)}), f32[192,1]{1,0:T(8,128)}) %reduce-scatter.40.cloned.1.call-update) | async-done | bytes 784
  1090.1 56.4 %reduce-scatter.36.cloned.1.call-done = f32[48,6]{1,0:T(8,128)} async-done(((f32[768,6]{1,0:T(8,128)}), f32[48,6]{1,0:T(8,128)}) %reduce-scatter.36.cloned.1.call-update) | async-done | bytes 1168
  1148.1 103.1 %reduce-scatter.30.cloned.1.call-done = f32[24,768]{1,0:T(8,128)} async-done(((f32[768,768]{1,0:T(8,128)}), f32[24,768]{1,0:T(8,128)}) %reduce-scatter.30.cloned.1.call-update) | async-done | bytes 73744 | tf_op jit(solution)/shard_map/reduce_scatter | solution.py:404
  1251.2 103.8 %reduce-scatter.34.cloned.1.call-done = f32[24,768]{1,0:T(8,128)} async-done(((f32[768,768]{1,0:T(8,128)}), f32[24,768]{1,0:T(8,128)}) %reduce-scatter.34.cloned.1.call-update) | async-done | bytes 73744 | tf_op jit(solution)/shard_map/reduce_scatter | solution.py:406
  1355.0 66.8 %reduce-scatter.24.cloned.1.call-done = f32[1,48,768]{2,1,0:T(8,128)} async-done(((f32[1,768,768]{2,1,0:T(8,128)}), f32[1,48,768]{2,1,0:T(8,128)}) %reduce-scatter.24.cloned.1.call-update) | async-done | bytes 147472 | tf_op jit(solution)/shard_map/reduce_scatter | solution.py:396
  1421.8 111.8 %reduce-scatter.32.cloned.1.call-done = f32[24,1536]{1,0:T(8,128)} async-done(((f32[768,1536]{1,0:T(8,128)}), f32[24,1536]{1,0:T(8,128)}) %reduce-scatter.32.cloned.1.call-update) | async-done | bytes 147472 | tf_op jit(solution)/shard_map/reduce_scatter | solution.py:405
  1533.6 93.8 %reduce-scatter.22.cloned.1.call-done = f32[1,48,2304]{2,1,0:T(8,128)} async-done(((f32[1,768,2304]{2,1,0:T(8,128)}), f32[1,48,2304]{2,1,0:T(8,128)}) %reduce-scatter.22.cloned.1.call-update) | async-done | bytes 442384 | tf_op jit(solution)/shard_map/reduce_scatter | solution.py:395
  1627.3 116.2 %reduce-scatter.26.cloned.1.call-done = f32[1,48,3072]{2,1,0:T(8,128)} async-done(((f32[1,768,3072]{2,1,0:T(8,128)}), f32[1,48,3072]{2,1,0:T(8,128)}) %reduce-scatter.26.cloned.1.call-update) | async-done | bytes 589840 | tf_op jit(solution)/shard_map/reduce_scatter | solution.py:399
  1743.5 117.1 %reduce-scatter.28.cloned.1.call-done = f32[1,192,768]{2,1,0:T(8,128)} async-done(((f32[1,3072,768]{2,1,0:T(8,128)}), f32[1,192,768]{2,1,0:T(8,128)}) %reduce-scatter.28.cloned.1.call-update) | async-done | bytes 589840 | tf_op jit(solution)/shard_map/reduce_scatter | solution.py:401
  (1214 shorter events, 819.2 us)
Async XLA Ops:
  29.2 64.5 %all-gather.11.cloned.1.call-start = ((), (), s32[]{:S(2)}) async-start(), calls=%async_computation.27 | async-start | bytes 1966080 | tf_op jit(solution)/shard_map/while/body/eval_jaxpr/all_gather | solution.py:131
  32.7 82.7 %all-gather.5.cloned.1.call-start = ((), (), s32[]{:S(2)}) async-start(), calls=%async_computation.24 | async-start | bytes 1966080 | tf_op jit(solution)/shard_map/while/body/eval_jaxpr/all_gather | solution.py:132
  164.4 80.2 %all-gather.5.cloned.1.call-start = ((), (), s32[]{:S(2)}) async-start(), calls=%async_computation.24 | async-start | bytes 1966080 | tf_op jit(solution)/shard_map/while/body/eval_jaxpr/all_gather | solution.py:132
  293.4 80.1 %all-gather.5.cloned.1.call-start = ((), (), s32[]{:S(2)}) async-start(), calls=%async_computation.24 | async-start | bytes 1966080 | tf_op jit(solution)/shard_map/while/body/eval_jaxpr/all_gather | solution.py:132
  423.2 151.3 %reduce-scatter.42.cloned.1.call-start = ((), (), s32[]{:S(2)}) async-start(), calls=%async_computation.28 | async-start | bytes 1966080 | tf_op jit(solution)/shard_map/while/body/eval_jaxpr/reduce_scatter | solution.py:143
  466.8 107.7 %reduce-scatter.44.cloned.1.call-start = ((), (), s32[]{:S(2)}) async-start(), calls=%async_computation.29 | async-start | bytes 1966080 | tf_op jit(solution)/shard_map/while/body/eval_jaxpr/reduce_scatter | solution.py:140
  493.7 86.5 %reduce-scatter.46.cloned.1.call-start = ((), (), s32[]{:S(2)}) async-start(), calls=%async_computation.30 | async-start | bytes 1966080 | tf_op jit(solution)/shard_map/while/body/eval_jaxpr/reduce_scatter | solution.py:143
  599.8 158.1 %reduce-scatter.42.cloned.1.call-start = ((), (), s32[]{:S(2)}) async-start(), calls=%async_computation.28 | async-start | bytes 1966080 | tf_op jit(solution)/shard_map/while/body/eval_jaxpr/reduce_scatter | solution.py:143
  643.4 114.5 %reduce-scatter.44.cloned.1.call-start = ((), (), s32[]{:S(2)}) async-start(), calls=%async_computation.29 | async-start | bytes 1966080 | tf_op jit(solution)/shard_map/while/body/eval_jaxpr/reduce_scatter | solution.py:140
  670.2 93.5 %reduce-scatter.46.cloned.1.call-start = ((), (), s32[]{:S(2)}) async-start(), calls=%async_computation.30 | async-start | bytes 1966080 | tf_op jit(solution)/shard_map/while/body/eval_jaxpr/reduce_scatter | solution.py:143
  781.2 157.9 %reduce-scatter.42.cloned.1.call-start = ((), (), s32[]{:S(2)}) async-start(), calls=%async_computation.28 | async-start | bytes 1966080 | tf_op jit(solution)/shard_map/while/body/eval_jaxpr/reduce_scatter | solution.py:143
  824.7 114.3 %reduce-scatter.44.cloned.1.call-start = ((), (), s32[]{:S(2)}) async-start(), calls=%async_computation.29 | async-start | bytes 1966080 | tf_op jit(solution)/shard_map/while/body/eval_jaxpr/reduce_scatter | solution.py:140
  851.4 93.6 %reduce-scatter.46.cloned.1.call-start = ((), (), s32[]{:S(2)}) async-start(), calls=%async_computation.30 | async-start | bytes 1966080 | tf_op jit(solution)/shard_map/while/body/eval_jaxpr/reduce_scatter | solution.py:143
  881.8 64.6 %reduce-scatter.48.cloned.1.call-start = ((), (), s32[]{:S(2)}) async-start(), calls=%async_computation.31 | async-start | bytes 1966080 | tf_op jit(solution)/shard_map/while/body/eval_jaxpr/reduce_scatter | solution.py:140
  966.5 84.5 %reduce-scatter.38.cloned.1.call-start = ((), (), s32[]{:S(2)}) async-start(), calls=%async_computation.22 | async-start | bytes 417792
  968.2 120.4 %reduce-scatter.40.cloned.1.call-start = ((), (), s32[]{:S(2)}) async-start(), calls=%async_computation.23 | async-start | bytes 1671168
  970.6 175.9 %reduce-scatter.36.cloned.1.call-start = ((), (), s32[]{:S(2)}) async-start(), calls=%async_computation.21 | async-start | bytes 417792
  973.6 277.5 %reduce-scatter.30.cloned.1.call-start = ((), (), s32[]{:S(2)}) async-start(), calls=%async_computation.18 | async-start | bytes 2433024 | tf_op jit(solution)/shard_map/reduce_scatter | solution.py:404
  974.4 380.6 %reduce-scatter.34.cloned.1.call-start = ((), (), s32[]{:S(2)}) async-start(), calls=%async_computation.20 | async-start | bytes 2433024 | tf_op jit(solution)/shard_map/reduce_scatter | solution.py:406
  975.1 446.7 %reduce-scatter.24.cloned.1.call-start = ((), (), s32[]{:S(2)}) async-start(), calls=%async_computation.15 | async-start | bytes 2506752 | tf_op jit(solution)/shard_map/reduce_scatter | solution.py:396
  975.9 557.7 %reduce-scatter.32.cloned.1.call-start = ((), (), s32[]{:S(2)}) async-start(), calls=%async_computation.19 | async-start | bytes 4866048 | tf_op jit(solution)/shard_map/reduce_scatter | solution.py:405
  976.5 650.9 %reduce-scatter.22.cloned.1.call-start = ((), (), s32[]{:S(2)}) async-start(), calls=%async_computation.14 | async-start | bytes 7520256 | tf_op jit(solution)/shard_map/reduce_scatter | solution.py:395
  977.1 766.5 %reduce-scatter.26.cloned.1.call-start = ((), (), s32[]{:S(2)}) async-start(), calls=%async_computation.16 | async-start | bytes 10027008 | tf_op jit(solution)/shard_map/reduce_scatter | solution.py:399
  977.6 882.9 %reduce-scatter.28.cloned.1.call-start = ((), (), s32[]{:S(2)}) async-start(), calls=%async_computation.17 | async-start | bytes 10027008 | tf_op jit(solution)/shard_map/reduce_scatter | solution.py:401
  (315 other events, 2628.1 us)
Sparse Core Ops, SparseCore 0:
  28.6 21.3 all-gather.8
  52.2 19.6 all-gather.6
  74.0 19.6 all-gather.10
  95.7 19.6 all-gather.4
  160.5 18.7 all-gather.8
  181.3 19.6 all-gather.6
  203.2 19.6 all-gather.10
  225.0 19.6 all-gather.4
  289.5 18.7 all-gather.8
  310.3 19.6 all-gather.6
  332.1 19.6 all-gather.10
  353.8 19.6 all-gather.4
  466.9 27.2 reduce-scatter.41
  496.8 28.1 reduce-scatter.43
  527.3 28.1 reduce-scatter.45
  558.1 28.1 reduce-scatter.47
  643.5 28.1 reduce-scatter.41
  674.2 28.1 reduce-scatter.43
  705.0 28.1 reduce-scatter.45
  735.7 28.1 reduce-scatter.47
  824.8 29.0 reduce-scatter.41
  856.6 28.1 reduce-scatter.43
  887.4 28.1 reduce-scatter.45
  918.2 28.1 reduce-scatter.47
Sparse Core Ops, SparseCore 1:
  970.4 55.6 reduce-scatter.37
  1030.1 58.4 reduce-scatter.39
  1091.9 54.5 reduce-scatter.35
  1153.2 97.9 reduce-scatter.29
  1257.1 97.9 reduce-scatter.33
  1359.9 61.9 reduce-scatter.23
  1427.7 105.8 reduce-scatter.31
  1538.6 88.7 reduce-scatter.21
  1631.9 111.6 reduce-scatter.25
  1748.8 111.8 reduce-scatter.27
where the time goes:
time: 1870 us
  waiting for transfers between devices  943 us (50%)
  matrix products  467 us (25%)
  local copies, waits for them, and re-layouts  183 us (10%)
  other arithmetic  146 us (8%)
  blocking collectives  75.9 us (4%)
  loops' own time  21.4 us (1%)
    reduce_scatter x1, waiting for transfers between devices, per_device(): lax.psum_scatter(totals[6][None], ('dp', 'seq'), scatter_dimension=1, til...  117 us
    reduce_scatter x1, waiting for transfers between devices, per_device(): lax.psum_scatter(totals[4][None], ('dp', 'seq'), scatter_dimension=1, til...  116 us
    dot_general x21, matrix products, weight_grad(): jnp.einsum('rsi,rsj->ij', activation, gradient, preferred_element_type=jn...  112 us
    reduce_scatter x1, waiting for transfers between devices, per_device(): lax.psum_scatter(totals[8], ('section', 'dp', 'seq'), scatter_dimension=0...  112 us
    reduce_scatter x1, waiting for transfers between devices, per_device(): lax.psum_scatter(totals[9], ('section', 'dp', 'seq'), scatter_dimension=0...  104 us
    reduce_scatter x1, waiting for transfers between devices, per_device(): lax.psum_scatter(totals[7], ('section', 'dp', 'seq'), scatter_dimension=0...  103 us
    unnamed x13, waiting for transfers between devices  96.9 us
    reduce_scatter x1, waiting for transfers between devices, per_device(): lax.psum_scatter(totals[0][None], ('dp', 'seq'), scatter_dimension=1, til...  93.8 us
  transfers between devices with their start and end apart: 40, of which 24 were waited for; matrix products, arithmetic and copies ran while one was open for 29% of the time, Pallas kernels for 0%

commit v1 on v0

--- a/solution.py
+++ b/solution.py
@@ -144,6 +144,35 @@
             value_term.astype(jnp.bfloat16), "seq", scatter_dimension=1, tiled=True
         ).astype(jnp.float32),
     )
+
+
+def group_sum(parts, axis, members, stride, kind):
+    length = lax.axis_size(axis)
+    mine = (lax.axis_index(axis) // stride) % members
+    total = pick_row(parts, mine).astype(jnp.float32)
+    for step in range(1, members):
+        pairs = []
+        for i in range(length):
+            at = (i // stride) % members
+            pairs.append((i, i + ((at + step) % members - at) * stride))
+        arrived = lax.ppermute(pick_row(parts, (mine + step) % members), axis, pairs)
+        total = total + arrived.astype(jnp.float32)
+    return total.astype(kind)
+
+
+def scatter_sum(total):
+    dp_size = lax.axis_size("dp")
+    chips = lax.axis_size("seq") // 2
+    rows = total.shape[0] // (dp_size * chips * 2)
+    parts = jnp.moveaxis(total.reshape(dp_size, chips, 2, rows, *total.shape[1:]), 2, 0)
+    parts = group_sum(parts, "seq", 2, 1, total.dtype)
+    parts = group_sum(jnp.moveaxis(parts, 1, 0), "seq", chips, 2, total.dtype)
+    return group_sum(parts, "dp", dp_size, 1, jnp.float32)
+
+
+def section_half(total):
+    parts = total.reshape(2, total.shape[0] // 2, *total.shape[1:])
+    return group_sum(parts, "section", 2, 1, total.dtype)
 
 
 def per_device(
@@ -391,23 +420,33 @@
     )
     back_start = (jnp.zeros((row_count, shard_len, width), jnp.bfloat16), grad_zeros)
     (_, totals), grads_in = lax.scan(backward_tick, back_start, jnp.arange(micro + 1))
-    section_part = (
-        lax.psum_scatter(totals[0][None], ("dp", "seq"), scatter_dimension=1, tiled=True),
-        lax.psum_scatter(totals[1][None], ("dp", "seq"), scatter_dimension=1, tiled=True),
-        lax.psum_scatter(totals[2][None], ("dp", "seq"), scatter_dimension=2, tiled=True),
-        lax.psum_scatter(totals[3][None], ("dp", "seq"), scatter_dimension=2, tiled=True),
-        lax.psum_scatter(totals[4][None], ("dp", "seq"), scatter_dimension=1, tiled=True),
-        lax.psum_scatter(totals[5][None], ("dp", "seq"), scatter_dimension=1, tiled=True),
-        lax.psum_scatter(totals[6][None], ("dp", "seq"), scatter_dimension=1, tiled=True),
-    )
-    cross_part = (
-        lax.psum_scatter(totals[7], ("section", "dp", "seq"), scatter_dimension=0, tiled=True),
-        lax.psum_scatter(totals[8], ("section", "dp", "seq"), scatter_dimension=0, tiled=True),
-        lax.psum_scatter(totals[9], ("section", "dp", "seq"), scatter_dimension=0, tiled=True),
-        lax.psum_scatter(totals[10], ("section", "dp", "seq"), scatter_dimension=1, tiled=True),
-        lax.psum_scatter(totals[11], ("section", "dp", "seq"), scatter_dimension=0, tiled=True),
-    )
-    moments = lax.psum(square_sums, ("dp", "seq"))
+    low = jnp.bfloat16
+    ffn_in_part = scatter_sum(totals[4].astype(low))
+    ffn_out_part = scatter_sum(totals[6].astype(low))
+    attn_in_part = scatter_sum(totals[0].astype(low))
+    attn_out_part = scatter_sum(totals[1].astype(low))
+    cross_part = scatter_sum(
+        section_half(jnp.concatenate([totals[7], totals[8], totals[9]], -1).astype(low))
+    )
+    blocks = lax.axis_size("dp") * lax.axis_size("seq")
+    cross_small = section_half(jnp.concatenate([totals[10], totals[11][None]], 0).T)
+    small = jnp.concatenate(
+        [
+            jnp.concatenate([totals[2], totals[3]], 0).T.reshape(blocks, -1),
+            totals[5].reshape(blocks, -1),
+            cross_small.reshape(blocks, -1),
+            jnp.broadcast_to(square_sums[None], (blocks, 2)),
+        ],
+        -1,
+    )
+    small = scatter_sum(small)[0]
+    per = width // blocks
+    half = per // 2
+    section_small = small[: 8 * per].reshape(per, 8).T
+    ffn_bias_part = small[8 * per : 8 * per + b_inner.shape[0] // blocks]
+    rest = small[8 * per + b_inner.shape[0] // blocks :]
+    cross_rows = rest[: 5 * half].reshape(half, 5).T
+    moments = rest[5 * half :]
     count = micro * row_count * lax.axis_size("dp") * shard_len * lax.axis_size("seq") * width
     stats = jnp.sqrt(moments / count)[None]
     layer_out = lax.dynamic_slice_in_dim(outputs_all, section, micro, 0)[None]
@@ -416,18 +455,18 @@
         layer_out,
         input_grad,
         stats,
-        section_part[0],
-        section_part[1],
-        section_part[2],
-        section_part[3],
-        section_part[4],
-        section_part[5],
-        section_part[6],
-        cross_part[0],
-        cross_part[1],
-        cross_part[2],
-        cross_part[3],
-        cross_part[4],
+        attn_in_part[None],
+        attn_out_part[None],
+        section_small[None, :6],
+        section_small[None, 6:],
+        ffn_in_part[None],
+        ffn_bias_part[None],
+        ffn_out_part[None],
+        cross_part[:, :width],
+        cross_part[:, width : 3 * width],
+        cross_part[:, 3 * width :],
+        cross_rows[:4],
+        cross_rows[4],
     )
 
 

time: 1870 us -> 1210 us (0.65); the launches traced: 1870 us -> 1180 us
  waiting for transfers between devices: 943 us -> 210 us
  blocking collectives: 75.9 us -> 6.32 us
  starting transfers between devices: 16.2 us -> 60.8 us
  other arithmetic: 146 us -> 184 us
  local copies, waits for them, and re-layouts: 183 us -> 212 us
    reduce_scatter x7 -> x0, waiting for transfers between devices: 713 us -> none  [the longest x1 117 us: per_device(): lax.psum_scatter(totals[6][None], ('dp', 'seq'), scatter_dimension=1, til...]
    unnamed x13 -> x0, waiting for transfers between devices: 96.9 us -> none
    ppermute x0 -> x32, waiting for transfers between devices: none -> 76.6 us  [group_sum(): lax.ppermute(pick_row(parts, (mine + step) % members), axis, pairs)]
    ppermute x0 -> x32, starting transfers between devices: none -> 45.1 us  [group_sum(): lax.ppermute(pick_row(parts, (mine + step) % members), axis, pairs)]
    unnamed x1 -> x0, blocking collectives: 37.1 us -> none
    psum x1 -> x0, blocking collectives: 32.5 us -> none  [per_device(): moments = lax.psum(square_sums, ('dp', 'seq'))]
    convert_element_type x0 -> x15, other arithmetic: none -> 25.7 us  [the longest x11 10.6 us: group_sum(): return total.astype(kind)]
    dynamic_slice x45 -> x48, local copies, waits for them, and re-layouts: 55.1 us -> 58.1 us  [pick_row(): return lax.dynamic_index_in_dim(stacked, position, 0, keepdims=False)]
  transfers between devices with their start and end apart: 40 -> 62, of which waited for: 24 -> 28; matrix products, arithmetic and copies ran while one was open for 29% -> 51% of each run, Pallas kernels for 0% -> 0%
where the time goes in v1:
time: 1210 us; the launch traced here: 1180 us
  matrix products  466 us (39%)
  local copies, waits for them, and re-layouts  212 us (18%)
  waiting for transfers between devices  210 us (17%)
  other arithmetic  184 us (15%)
  starting transfers between devices  60.8 us (5%)
  loops' own time  27.4 us (2%)
  between operations  15.3 us (1%)
    dot_general x21, matrix products, weight_grad(): jnp.einsum('rsi,rsj->ij', activation, gradient, preferred_element_type=jn...  112 us
    ppermute x32, waiting for transfers between devices, group_sum(): lax.ppermute(pick_row(parts, (mine + step) % members), axis, pairs)  76.6 us
    dot_general x6, matrix products, attend_back(): jnp.einsum('rqhd,rkhd->rhqk', grad_heads, value_heads, preferred_element_...  73.3 us
    all_gather x6, waiting for transfers between devices, share_keys(): lax.all_gather(for_sending(value_local), 'seq', axis=1, tiled=True)  69.3 us
    dot_general x21, matrix products, project(): jnp.dot(activation, weight, preferred_element_type=jnp.float32) + offset  69.2 us
    dot_general x21, matrix products, project_back(): jnp.einsum('rsj,ij->rsi', gradient, weight, preferred_element_type=jnp.fl...  68.1 us
    dynamic_slice x48, local copies, waits for them, and re-layouts, pick_row(): return lax.dynamic_index_in_dim(stacked, position, 0, keepdims=False)  58.1 us
    all_gather x6, waiting for transfers between devices, share_keys(): lax.all_gather(for_sending(key_local), 'seq', axis=1, tiled=True)  52.4 us
  transfers between devices with their start and end apart: 62, of which 28 were waited for; matrix products, arithmetic and copies ran while one was open for 51% of the time, Pallas kernels for 0%

profile of v1, /device:TPU:0, one launch (start us, length us, event | category | flops | bytes accessed | tf_op | source)
XLA Modules:
  0.0 1182.3 jit_solution(5001669622949904541)
XLA Ops:
  22.3 389.6 %while.94 = (s32[]{:T(128)}, bf16[1,256,768]{2,1,0:T(8,128)(2,1)S(1)}, f32[2]{0:T(128)S(1)}, bf16[3,1,256,768]{3,2,1,0:T(8,128)(2,1)}, bf16[3,1,256,3072]{3,2,1,...) while((s32[]{:T(128)}, ...), condition=%wide.region_13.14_spmd.clone, body=%wide.region_0.13_spmd.clone.sunk | while | flops 6582562304 | bytes 387940640 | solution.py:297
  35.1 14.1 %all-gather.9.cloned.1.call-done = bf16[1,1024,768]{2,1,0:T(8,128)(2,1)} async-done(((bf16[1,256,768]{2,1,0:T(8,128)(2,1)}), bf16[1,1024,768]{2,1,0:T(8,128)(2,1)}) %all-gather.9.cloned.1.call-update) | async-done | bytes 1572880 | tf_op jit(solution)/shard_map/while/body/eval_jaxpr/all_gather | solution.py:131
  58.5 12.6 %all-gather.7.cloned.1.call-done = bf16[1,1024,768]{2,1,0:T(8,128)(2,1)} async-done(((bf16[1,256,768]{2,1,0:T(8,128)(2,1)}), bf16[1,1024,768]{2,1,0:T(8,128)(2,1)}) %all-gather.7.cloned.1.call-update) | async-done | bytes 1572880 | tf_op jit(solution)/shard_map/while/body/eval_jaxpr/all_gather | solution.py:132
  104.0 10.5 all-gather.5.cloned.1.call-done
  166.8 11.5 all-gather.9.cloned.1.call-done
  187.5 12.5 %all-gather.7.cloned.1.call-done = bf16[1,1024,768]{2,1,0:T(8,128)(2,1)} async-done(((bf16[1,256,768]{2,1,0:T(8,128)(2,1)}), bf16[1,1024,768]{2,1,0:T(8,128)(2,1)}) %all-gather.7.cloned.1.call-update) | async-done | bytes 1572880 | tf_op jit(solution)/shard_map/while/body/eval_jaxpr/all_gather | solution.py:132
  232.9 10.7 all-gather.5.cloned.1.call-done
  295.6 11.6 all-gather.9.cloned.1.call-done
  316.4 12.5 %all-gather.7.cloned.1.call-done = bf16[1,1024,768]{2,1,0:T(8,128)(2,1)} async-done(((bf16[1,256,768]{2,1,0:T(8,128)(2,1)}), bf16[1,1024,768]{2,1,0:T(8,128)(2,1)}) %all-gather.7.cloned.1.call-update) | async-done | bytes 1572880 | tf_op jit(solution)/shard_map/while/body/eval_jaxpr/all_gather | solution.py:132
  361.8 10.5 all-gather.5.cloned.1.call-done
  413.6 557.4 %while.95 = (s32[]{:T(128)}, bf16[1,256,768]{2,1,0:T(8,128)(2,1)S(1)}, f32[768,2304]{1,0:T(8,128)}, f32[768,768]{1,0:T(8,128)}, f32[6,768]{1,0:T(8,128)}, /*inde...) while((s32[]{:T(128)}, ...), condition=%wide.region_46.47_spmd.clone, body=%wide.region_14.46_spmd.clone.sunk | while | flops 13903286272 | bytes 772435520 | solution.py:422
  435.1 11.5 convert_reduce_fusion.15
  468.7 12.3 %multiply_reduce_fusion.32 = (f32[12,256]{1,0:T(8,128)S(1)}, f32[12,256,1024]{2,1,0:T(8,128)}) fusion(f32[12,256,1024]{2,1,0:T(8,128)} %copy-done, f32[12,256]{1,0:T(8,128)S(1)} %dynamic-slice_bitcast_fusion.33, pred[256,1024]{1,0:T(8,128)(4,1)S(1)} %get-tuple-element.2822, bf16[256,12,64]{0,2,1:T(8,128)(2,1)S(1)} %bitcast.827, ...), kind=kOutput, calls=%fused_computation.121.clone.1 | convolution fusion | flops 418378752 | bytes 27418624 | tf_op jit(solution)/shard_map/while/body/eval_jaxpr/rqhd,rkhd->rhqk/dot_general | solution.py:100
  525.3 12.2 %multiply_reduce_fusion.35 = (f32[12,256]{1,0:T(8,128)S(1)}, f32[12,256,1024]{2,1,0:T(8,128)}) fusion(f32[12,256,1024]{2,1,0:T(8,128)} %copy-done.1, f32[12,256]{1,0:T(8,128)S(1)} %dynamic-slice_bitcast_fusion.34, pred[256,1024]{1,0:T(8,128)(4,1)} %get-tuple-element.2834, bf16[256,12,64]{0,2,1:T(8,128)(2,1)} %bitcast.828, ...), kind=kOutput, calls=%fused_computation.118.clone.1 | convolution fusion | flops 418378752 | bytes 27418624 | tf_op jit(solution)/shard_map/while/body/eval_jaxpr/rqhd,rkhd->rhqk/dot_general | solution.py:100
  611.4 11.5 convert_reduce_fusion.15
  645.1 12.2 %multiply_reduce_fusion.32 = (f32[12,256]{1,0:T(8,128)S(1)}, f32[12,256,1024]{2,1,0:T(8,128)}) fusion(f32[12,256,1024]{2,1,0:T(8,128)} %copy-done, f32[12,256]{1,0:T(8,128)S(1)} %dynamic-slice_bitcast_fusion.33, pred[256,1024]{1,0:T(8,128)(4,1)S(1)} %get-tuple-element.2822, bf16[256,12,64]{0,2,1:T(8,128)(2,1)S(1)} %bitcast.827, ...), kind=kOutput, calls=%fused_computation.121.clone.1 | convolution fusion | flops 418378752 | bytes 27418624 | tf_op jit(solution)/shard_map/while/body/eval_jaxpr/rqhd,rkhd->rhqk/dot_general | solution.py:100
  701.1 12.3 %multiply_reduce_fusion.35 = (f32[12,256]{1,0:T(8,128)S(1)}, f32[12,256,1024]{2,1,0:T(8,128)}) fusion(f32[12,256,1024]{2,1,0:T(8,128)} %copy-done.1, f32[12,256]{1,0:T(8,128)S(1)} %dynamic-slice_bitcast_fusion.34, pred[256,1024]{1,0:T(8,128)(4,1)} %get-tuple-element.2834, bf16[256,12,64]{0,2,1:T(8,128)(2,1)} %bitcast.828, ...), kind=kOutput, calls=%fused_computation.118.clone.1 | convolution fusion | flops 418378752 | bytes 27418624 | tf_op jit(solution)/shard_map/while/body/eval_jaxpr/rqhd,rkhd->rhqk/dot_general | solution.py:100
  737.9 9.9 select_add_fusion.25
  792.7 11.5 convert_reduce_fusion.15
  826.2 12.0 %multiply_reduce_fusion.32 = (f32[12,256]{1,0:T(8,128)S(1)}, f32[12,256,1024]{2,1,0:T(8,128)}) fusion(f32[12,256,1024]{2,1,0:T(8,128)} %copy-done, f32[12,256]{1,0:T(8,128)S(1)} %dynamic-slice_bitcast_fusion.33, pred[256,1024]{1,0:T(8,128)(4,1)S(1)} %get-tuple-element.2822, bf16[256,12,64]{0,2,1:T(8,128)(2,1)S(1)} %bitcast.827, ...), kind=kOutput, calls=%fused_computation.121.clone.1 | convolution fusion | flops 418378752 | bytes 27418624 | tf_op jit(solution)/shard_map/while/body/eval_jaxpr/rqhd,rkhd->rhqk/dot_general | solution.py:100
  882.4 12.3 %multiply_reduce_fusion.35 = (f32[12,256]{1,0:T(8,128)S(1)}, f32[12,256,1024]{2,1,0:T(8,128)}) fusion(f32[12,256,1024]{2,1,0:T(8,128)} %copy-done.1, f32[12,256]{1,0:T(8,128)S(1)} %dynamic-slice_bitcast_fusion.34, pred[256,1024]{1,0:T(8,128)(4,1)} %get-tuple-element.2834, bf16[256,12,64]{0,2,1:T(8,128)(2,1)} %bitcast.828, ...), kind=kOutput, calls=%fused_computation.118.clone.1 | convolution fusion | flops 418378752 | bytes 27418624 | tf_op jit(solution)/shard_map/while/body/eval_jaxpr/rqhd,rkhd->rhqk/dot_general | solution.py:100
  1069.9 15.6 %collective-permute-done.9 = bf16[4,48,2304]{2,1,0:T(8,128)(2,1)S(1)} collective-permute-done((bf16[4,48,2304]{2,1,0:T(8,128)(2,1)S(1)}, bf16[4,48,2304]{2,1,0:T(8,128)(2,1)S(1)}, u32[]{:S(2)}, u32[]{:S(2)}) %collective-permute-start.9) | collective-permute-done | bytes 884768 | tf_op jit(solution)/shard_map/ppermute | solution.py:158
  1115.1 20.9 %collective-permute-done.24 = bf16[4,192,768]{2,1,0:T(8,128)(2,1)S(1)} collective-permute-done((bf16[4,192,768]{2,1,0:T(8,128)(2,1)S(1)}, bf16[4,192,768]{2,1,0:T(8,128)(2,1)S(1)}, u32[]{:S(2)}, u32[]{:S(2)}) %collective-permute-start.24) | collective-permute-done | bytes 1179680 | tf_op jit(solution)/shard_map/ppermute | solution.py:158
  1149.6 10.8 collective-permute-start.32
  (1337 shorter events, 868.2 us)
Async XLA Ops:
  27.7 43.4 %all-gather.7.cloned.1.call-start = ((), (), s32[]{:S(2)}) async-start(), calls=%async_computation.5 | async-start | bytes 1966080 | tf_op jit(solution)/shard_map/while/body/eval_jaxpr/all_gather | solution.py:132
  28.5 64.4 %all-gather.11.cloned.1.call-start = ((), (), s32[]{:S(2)}) async-start(), calls=%async_computation.7 | async-start | bytes 1966080 | tf_op jit(solution)/shard_map/while/body/eval_jaxpr/all_gather | solution.py:131
  31.9 82.7 %all-gather.5.cloned.1.call-start = ((), (), s32[]{:S(2)}) async-start(), calls=%async_computation.4 | async-start | bytes 1966080 | tf_op jit(solution)/shard_map/while/body/eval_jaxpr/all_gather | solution.py:132
  159.4 40.6 %all-gather.7.cloned.1.call-start = ((), (), s32[]{:S(2)}) async-start(), calls=%async_computation.5 | async-start | bytes 1966080 | tf_op jit(solution)/shard_map/while/body/eval_jaxpr/all_gather | solution.py:132
  160.0 61.8 %all-gather.11.cloned.1.call-start = ((), (), s32[]{:S(2)}) async-start(), calls=%async_computation.7 | async-start | bytes 1966080 | tf_op jit(solution)/shard_map/while/body/eval_jaxpr/all_gather | solution.py:131
  163.4 80.2 %all-gather.5.cloned.1.call-start = ((), (), s32[]{:S(2)}) async-start(), calls=%async_computation.4 | async-start | bytes 1966080 | tf_op jit(solution)/shard_map/while/body/eval_jaxpr/all_gather | solution.py:132
  288.9 61.8 %all-gather.11.cloned.1.call-start = ((), (), s32[]{:S(2)}) async-start(), calls=%async_computation.7 | async-start | bytes 1966080 | tf_op jit(solution)/shard_map/while/body/eval_jaxpr/all_gather | solution.py:131
  292.3 80.1 %all-gather.5.cloned.1.call-start = ((), (), s32[]{:S(2)}) async-start(), calls=%async_computation.4 | async-start | bytes 1966080 | tf_op jit(solution)/shard_map/while/body/eval_jaxpr/all_gather | solution.py:132
  422.3 151.2 %reduce-scatter.5.cloned.1.call-start = ((), (), s32[]{:S(2)}) async-start(), calls=%async_computation.8 | async-start | bytes 1966080 | tf_op jit(solution)/shard_map/while/body/eval_jaxpr/reduce_scatter | solution.py:143
  465.8 107.7 %reduce-scatter.7.cloned.1.call-start = ((), (), s32[]{:S(2)}) async-start(), calls=%async_computation.9 | async-start | bytes 1966080 | tf_op jit(solution)/shard_map/while/body/eval_jaxpr/reduce_scatter | solution.py:140
  492.7 86.5 %reduce-scatter.9.cloned.1.call-start = ((), (), s32[]{:S(2)}) async-start(), calls=%async_computation.10 | async-start | bytes 1966080 | tf_op jit(solution)/shard_map/while/body/eval_jaxpr/reduce_scatter | solution.py:143
  523.2 62.0 %reduce-scatter.11.cloned.1.call-start = ((), (), s32[]{:S(2)}) async-start(), calls=%async_computation.11 | async-start | bytes 1966080 | tf_op jit(solution)/shard_map/while/body/eval_jaxpr/reduce_scatter | solution.py:140
  598.6 158.3 %reduce-scatter.5.cloned.1.call-start = ((), (), s32[]{:S(2)}) async-start(), calls=%async_computation.8 | async-start | bytes 1966080 | tf_op jit(solution)/shard_map/while/body/eval_jaxpr/reduce_scatter | solution.py:143
  642.1 114.8 %reduce-scatter.7.cloned.1.call-start = ((), (), s32[]{:S(2)}) async-start(), calls=%async_computation.9 | async-start | bytes 1966080 | tf_op jit(solution)/shard_map/while/body/eval_jaxpr/reduce_scatter | solution.py:140
  669.0 93.7 %reduce-scatter.9.cloned.1.call-start = ((), (), s32[]{:S(2)}) async-start(), calls=%async_computation.10 | async-start | bytes 1966080 | tf_op jit(solution)/shard_map/while/body/eval_jaxpr/reduce_scatter | solution.py:143
  699.2 63.5 %reduce-scatter.11.cloned.1.call-start = ((), (), s32[]{:S(2)}) async-start(), calls=%async_computation.11 | async-start | bytes 1966080 | tf_op jit(solution)/shard_map/while/body/eval_jaxpr/reduce_scatter | solution.py:140
  779.9 157.8 %reduce-scatter.5.cloned.1.call-start = ((), (), s32[]{:S(2)}) async-start(), calls=%async_computation.8 | async-start | bytes 1966080 | tf_op jit(solution)/shard_map/while/body/eval_jaxpr/reduce_scatter | solution.py:143
  823.3 114.3 %reduce-scatter.7.cloned.1.call-start = ((), (), s32[]{:S(2)}) async-start(), calls=%async_computation.9 | async-start | bytes 1966080 | tf_op jit(solution)/shard_map/while/body/eval_jaxpr/reduce_scatter | solution.py:140
  850.1 93.6 %reduce-scatter.9.cloned.1.call-start = ((), (), s32[]{:S(2)}) async-start(), calls=%async_computation.10 | async-start | bytes 1966080 | tf_op jit(solution)/shard_map/while/body/eval_jaxpr/reduce_scatter | solution.py:143
  880.5 64.6 %reduce-scatter.11.cloned.1.call-start = ((), (), s32[]{:S(2)}) async-start(), calls=%async_computation.11 | async-start | bytes 1966080 | tf_op jit(solution)/shard_map/while/body/eval_jaxpr/reduce_scatter | solution.py:140
  978.1 59.6 %collective-permute-start.13 = (bf16[4,2,48,768]{3,2,1,0:T(8,128)(2,1)}, bf16[4,2,48,768]{3,2,1,0:T(8,128)(2,1)}, u32[]{:S(2)}, u32[]{:S(2)}) collective-permute-start(bf16[4,2,48,768]{3,2,1,0:T(8,128)(2,1)} %dynamic-slice_bitcast_fusion.13), channel_id=1, source_target_pairs={{0,1},{1,0},{2,3},{3,2},{4,5},{5,4},{6,7},{7,6},{8,9},{9,8},{10,11... | collective-permute-start | bytes 1769480 | tf_op jit(solution)/shard_map/ppermute | solution.py:158
  986.6 77.7 %collective-permute-start.28 = (bf16[384,3072]{1,0:T(8,128)(2,1)}, bf16[384,3072]{1,0:T(8,128)(2,1)}, u32[]{:S(2)}, u32[]{:S(2)}) collective-permute-start(bf16[384,3072]{1,0:T(8,128)(2,1)} %dynamic-slice_bitcast_fusion.2), channel_id=1, source_target_pairs={{0,16},{16,0},{1,17},{17,1},{2,18},{18,2},{3,19},{19,3},{4,20},{20... | collective-permute-start | bytes 7077896 | tf_op jit(solution)/shard_map/ppermute | solution.py:158
  1068.9 41.8 %collective-permute-start.19 = (bf16[4,48,3072]{2,1,0:T(8,128)(2,1)S(1)}, bf16[4,48,3072]{2,1,0:T(8,128)(2,1)S(1)}, u32[]{:S(2)}, u32[]{:S(2)}) collective-permute-start(bf16[4,48,3072]{2,1,0:T(8,128)(2,1)S(1)} %dynamic-slice_bitcast_fusion.8), channel_id=1, source_target_pairs={{0,2},{1,3},{2,0},{3,1},{4,6},{5,7},{6,4},{7,5},{8,10},{9,11},{10,... | collective-permute-start | bytes 3538952 | tf_op jit(solution)/shard_map/ppermute | solution.py:158
  1094.4 41.5 %collective-permute-start.24 = (bf16[4,192,768]{2,1,0:T(8,128)(2,1)S(1)}, bf16[4,192,768]{2,1,0:T(8,128)(2,1)S(1)}, u32[]{:S(2)}, u32[]{:S(2)}) collective-permute-start(bf16[4,192,768]{2,1,0:T(8,128)(2,1)S(1)} %dynamic-slice_bitcast_fusion.7), channel_id=1, source_target_pairs={{0,2},{1,3},{2,0},{3,1},{4,6},{5,7},{6,4},{7,5},{8,10},{9,11},{10,... | collective-permute-start | bytes 3538952 | tf_op jit(solution)/shard_map/ppermute | solution.py:158
  (350 other events, 2697.1 us)
Sparse Core Ops, SparseCore 0:
  27.8 21.3 all-gather.8
  51.4 19.6 all-gather.6
  73.2 19.6 all-gather.10
  94.9 19.6 all-gather.4
  159.5 18.7 all-gather.8
  180.3 19.6 all-gather.6
  202.1 19.6 all-gather.10
  223.9 19.6 all-gather.4
  288.4 18.7 all-gather.8
  309.2 19.6 all-gather.6
  331.0 19.6 all-gather.10
  352.7 19.6 all-gather.4
  465.9 27.2 reduce-scatter.4
  495.7 28.1 reduce-scatter.6
  526.3 28.1 reduce-scatter.8
  557.0 28.1 reduce-scatter.10
  642.2 28.1 reduce-scatter.4
  672.9 28.1 reduce-scatter.6
  703.7 28.1 reduce-scatter.8
  734.4 28.1 reduce-scatter.10
  823.5 29.0 reduce-scatter.4
  855.3 28.1 reduce-scatter.6
  886.1 28.1 reduce-scatter.8
  916.8 28.1 reduce-scatter.10

commit v2 on v1

v2 whole, which is shorter than its diff:
```python
import functools
import math

import jax
import jax.numpy as jnp
from jax import lax
from jax.experimental import pallas as pl
from jax.experimental.pallas import tpu as pltpu
from jax.sharding import PartitionSpec as P

HEADS = 12
HEAD_DIM = 64
PAIR = 2 * HEAD_DIM
LSE_ROWS = 16
EPSILON = 1e-05
MASKED = -1000000000.0
SCALE = 1.0 / math.sqrt(HEAD_DIM)
VMEM_LIMIT = 40 * 1024 * 1024

F32 = jnp.float32
BF16 = jnp.bfloat16


def mm(a, b):
    return jnp.dot(a, b, preferred_element_type=F32)


def mm_nt(a, b):
    return lax.dot_general(a, b, (((1,), (1,)), ((), ())), preferred_element_type=F32)


def norm_parts(tensor):
    average = jnp.mean(tensor, -1, keepdims=True)
    centered = tensor - average
    spread = jnp.mean(centered * centered, -1, keepdims=True)
    scale = lax.rsqrt(spread + EPSILON)
    return centered * scale, scale


def norm_back(tensor, gain, grad):
    normed, scale = norm_parts(tensor)
    scaled = gain * grad
    product = grad * normed
    first = jnp.mean(scaled, -1, keepdims=True)
    second = jnp.mean(scaled * normed, -1, keepdims=True)
    out = (scaled - first - normed * second) * scale
    return out, jnp.sum(product, 0, keepdims=True), jnp.sum(grad, 0, keepdims=True)


def column_sum(tensor):
    return jnp.sum(tensor.astype(F32), 0, keepdims=True)


def gelu_pair(x):
    bell = jnp.exp(-0.5 * x * x)
    t = 1.0 / (1.0 + (0.3275911 / math.sqrt(2.0)) * jnp.abs(x))
    poly = t * (
        0.5 * 0.254829592
        + t
        * (
            0.5 * -0.284496736
            + t * (0.5 * 1.421413741 + t * (0.5 * -1.453152027 + t * (0.5 * 1.061405429)))
        )
    )
    tail = poly * bell
    cdf = jnp.where(x < 0, tail, 1.0 - tail)
    return x * cdf, cdf + x * bell * (1.0 / math.sqrt(2.0 * math.pi))


def row_blocks(count, body):
    step = min(256, count)

    def run(i, carry):
        body(pl.ds(pl.multiple_of(i * step, step), step))
        return carry

    lax.fori_loop(0, count // step, run, 0)


def head_halves(rows):
    lane = lax.broadcasted_iota(jnp.int32, (rows, PAIR), 1)
    return lane < HEAD_DIM, lane >= HEAD_DIM


def attend_forward(q_ref, k_ref, v_ref, bias_ref, mixed_ref, lse_ref):
    length = q_ref.shape[0]
    lse_ref[...] = jnp.zeros_like(lse_ref)

    def pair(p, carry):
        lanes = pl.ds(pl.multiple_of(p * PAIR, PAIR), PAIR)
        keys = k_ref[:, lanes]
        values_t = v_ref[:, lanes].T
        queries = q_ref[:, lanes] * SCALE
        outs = []
        for a, half in enumerate(head_halves(length)):
            own = jnp.where(half, queries, jnp.zeros_like(queries))
            scores = mm_nt(keys, own) + bias_ref[...]
            peak = jnp.max(scores, 0, keepdims=True)
            weights = jnp.exp(scores - peak)
            total = jnp.sum(weights, 0, keepdims=True)
            lse_ref[pl.ds(2 * p + a, 1), :] = peak + jnp.log(total)
            out = mm(values_t, weights.astype(BF16))
            outs.append(out[a * HEAD_DIM : (a + 1) * HEAD_DIM] * (1.0 / total))
        mixed_ref[:, lanes] = jnp.concatenate(outs, 0).T.astype(BF16)
        return carry

    lax.fori_loop(0, HEADS // 2, pair, 0)


def attend_back(q_ref, k_ref, v_ref, grad_ref, lse_ref, delta_ref, bias_ref, dq_ref, dkv_ref):
    length, width = q_ref.shape

    def pair(p, carry):
        lanes = pl.ds(pl.multiple_of(p * PAIR, PAIR), PAIR)
        value_lanes = pl.ds(pl.multiple_of(width + p * PAIR, PAIR), PAIR)
        keys = k_ref[:, lanes]
        values = v_ref[:, lanes]
        keys_t = keys.T
        queries = q_ref[:, lanes] * SCALE
        grads = grad_ref[:, lanes]
        key_grad = value_grad = None
        outs = []
        for a, half in enumerate(head_halves(length)):
            own = jnp.where(half, queries, jnp.zeros_like(queries))
            own_grad = jnp.where(half, grads, jnp.zeros_like(grads))
            lse = lse_ref[pl.ds(2 * p + a, 1), :]
            delta = delta_ref[pl.ds(2 * p + a, 1), :]
            weights = jnp.exp(mm_nt(keys, own) + bias_ref[...] - lse)
            weight_grad = mm_nt(values, own_grad)
            score_grad = (weights * (weight_grad - delta)).astype(BF16)
            value_term = mm(weights.astype(BF16), own_grad)
            key_term = mm(score_grad, own)
            value_grad = value_term if value_grad is None else value_grad + value_term
            key_grad = key_term if key_grad is None else key_grad + key_term
            out = mm(keys_t, score_grad)
            outs.append(out[a * HEAD_DIM : (a + 1) * HEAD_DIM] * SCALE)
        dkv_ref[:, lanes] = key_grad.astype(BF16)
        dkv_ref[:, value_lanes] = value_grad.astype(BF16)
        dq_ref[:, lanes] = jnp.concatenate(outs, 0).T.astype(BF16)
        return carry

    lax.fori_loop(0, HEADS // 2, pair, 0)


def head_dots(first, second):
    product = first.astype(F32) * second.astype(F32)
    width = product.shape[1]
    row = lax.broadcasted_iota(jnp.int32, (LSE_ROWS, width), 0)
    column = lax.broadcasted_iota(jnp.int32, (LSE_ROWS, width), 1)
    select = (column // HEAD_DIM == row).astype(F32)
    return lax.dot_general(
        select,
        product,
        (((1,), (1,)), ((), ())),
        precision=lax.Precision.HIGHEST,
        preferred_element_type=F32,
    )


def self_kernel(io, x_ref, w_qkv, w_mix, vec, bias, q_out, k_out, v_out, mixed, lse, summed, hidden, squares):
    length, width = q_out.shape
    io.ready(x_ref, w_qkv, vec)
    x_own = x_ref[0:length, :]
    q_out[...] = (mm(x_own, w_qkv[:, 0:width]) + vec[0:1, :]).astype(BF16)

    def keys(rows):
        x = x_ref[rows, :]
        k_out[rows, :] = mm(x, w_qkv[:, width : 2 * width]).astype(BF16)
        v_out[rows, :] = (mm(x, w_qkv[:, 2 * width : 3 * width]) + vec[1:2, :]).astype(BF16)

    row_blocks(x_ref.shape[0], keys)
    io.done(q_out, k_out, v_out)
    io.ready(bias)
    attend_forward(q_out, k_out, v_out, bias, mixed, lse)
    io.done(mixed, lse)
    io.ready(w_mix)
    branch = mm(mixed[...], w_mix[...]) + vec[2:3, :]
    total = x_own.astype(F32) + branch
    summed[...] = total
    squares[...] = jnp.zeros_like(squares)
    squares[0:1, :] = column_sum(total * total)
    squares[1:2, :] = column_sum(branch * branch)
    hidden[...] = norm_parts(total)[0] * vec[6:7, :] + vec[4:5, :]


def ffn_kernel(io, middle, vec, w_in, b_in, w_out, act, slope, final_sum, low_middle, result):
    width = middle.shape[1]
    chunks = w_in.shape[1] // width
    io.ready(middle, vec)
    mid = middle[...]
    low = mid.astype(BF16)
    low_middle[...] = low
    final_sum[...] = mid + vec[3:4, :]
    io.ready(w_in, b_in, w_out)

    def chunk(j, carry):
        columns = pl.ds(pl.multiple_of(j * width, width), width)
        inner = mm(low, w_in[:, columns]) + b_in[:, columns]
        value, derivative = gelu_pair(inner)
        value = value.astype(BF16)
        act[:, columns] = value
        slope[:, columns] = derivative.astype(BF16)
        final_sum[...] += mm(value, w_out[columns, :])
        return carry

    lax.fori_loop(0, chunks, chunk, 0)
    io.done(act, slope, low_middle, final_sum)
    result[...] = (norm_parts(final_sum[...])[0] * vec[7:8, :] + vec[5:6, :]).astype(BF16)


def ffn_back_kernel(io, grad, final_sum, vec, w_out, slope, w_in, dy, d_inner, d_middle, small):
    width = grad.shape[1]
    chunks = w_in.shape[1] // width
    io.ready(grad, final_sum, vec)
    d_final, d_gain, d_shift = norm_back(final_sum[...], vec[7:8, :], grad[...].astype(F32))
    low = d_final.astype(BF16)
    dy[...] = low
    small[...] = jnp.zeros_like(small)
    small[0:1, :] = d_gain
    small[1:2, :] = d_shift
    small[2:3, :] = column_sum(low)
    d_middle[...] = d_final
    io.done(dy)
    io.ready(w_out, slope, w_in)

    def chunk(j, carry):
        columns = pl.ds(pl.multiple_of(j * width, width), width)
        d_act = mm_nt(low, w_out[columns, :])
        inner = (d_act * slope[:, columns].astype(F32)).astype(BF16)
        d_inner[:, columns] = inner
        small[pl.ds(3 + j, 1), :] = column_sum(inner)
        d_middle[...] += mm_nt(inner, w_in[:, columns])
        return carry

    lax.fori_loop(0, chunks, chunk, 0)


def cross_kernel(
    io, hidden, w_q, vec, memory, w_kv, bias, w_o,
    cq, ck, cv, mixed, lse, summed, middle, low_hidden,
):
    width = hidden.shape[1]
    io.ready(hidden, w_q, vec)
    low = hidden[...].astype(BF16)
    low_hidden[...] = low
    cq[...] = (mm(low, w_q[...]) + vec[0:1, :]).astype(BF16)
    io.ready(memory, w_kv)

    def keys(rows):
        mem = memory[rows, :]
        ck[rows, :] = mm(mem, w_kv[:, 0:width]).astype(BF16)
        cv[rows, :] = (mm(mem, w_kv[:, width : 2 * width]) + vec[1:2, :]).astype(BF16)

    row_blocks(memory.shape[0], keys)
    io.done(cq, ck, cv, low_hidden)
    io.ready(bias)
    attend_forward(cq, ck, cv, bias, mixed, lse)
    io.done(mixed, lse)
    io.ready(w_o)
    total = hidden[...] + mm(mixed[...], w_o[...]) + vec[2:3, :]
    summed[...] = total
    middle[...] = norm_parts(total)[0] * vec[4:5, :] + vec[3:4, :]


def cross_back_kernel(
    io, d_middle, summed, vec, w_o, mixed, cq, ck, bias, lse, cv, w_q, w_kv,
    dyc, dcq, dckv, d_hidden, keep, send, small, d_mixed, delta,
):
    length, width = d_middle.shape
    io.ready(d_middle, summed, vec)
    d_cross, d_gain, d_shift = norm_back(summed[...], vec[4:5, :], d_middle[...])
    low = d_cross.astype(BF16)
    dyc[...] = low
    d_hidden[...] = d_cross
    io.ready(w_o, mixed)
    grads = mm_nt(low, w_o[...]).astype(BF16)
    d_mixed[...] = grads
    delta[...] = head_dots(grads, mixed[...])
    io.ready(cq, ck, bias, lse, cv)
    attend_back(cq, ck, cv, d_mixed, lse, delta, bias, dcq, dckv)
    io.ready(w_q, w_kv)
    for block in range(dckv.shape[0] // length):
        target = keep if block % 2 == 0 else send
        rows = slice(block // 2 * length, (block // 2 + 1) * length)
        target[rows, :] = mm_nt(dckv[block * length : (block + 1) * length, :], w_kv[...]).astype(BF16)
    io.done(send, keep, dyc, dcq, dckv)
    d_hidden[...] += mm_nt(dcq[...], w_q[...])
    small[...] = jnp.zeros_like(small)
    small[0:1, :] = d_gain
    small[1:2, :] = d_shift
    small[2:3, :] = column_sum(low)
    small[3:4, :] = column_sum(dcq[...])
    small[4:5, :] = column_sum(dckv[:, width : 2 * width])


def self_back_kernel(
    io, d_middle, d_hidden, summed, vec, w_mix, mixed, q, k, bias, lse, v, w_qkv,
    dy, dq, dkv, own, keep, send, small, d_mixed, delta,
):
    length, width = q.shape
    io.ready(d_middle, d_hidden, summed, vec)
    grad = jnp.where(io.section() == 0, d_middle[...], d_hidden[...])
    d_sum, d_gain, d_shift = norm_back(summed[...], vec[6:7, :], grad)
    low = d_sum.astype(BF16)
    dy[...] = low
    own[...] = d_sum
    io.ready(w_mix, mixed)
    grads = mm_nt(low, w_mix[...]).astype(BF16)
    d_mixed[...] = grads
    delta[...] = head_dots(grads, mixed[...])
    io.ready(q, k, bias, lse, v)
    attend_back(q, k, v, d_mixed, lse, delta, bias, dq, dkv)
    io.done(dy, dq, dkv)
    io.ready(w_qkv)
    for block in range(dkv.shape[0] // length):
        part = mm_nt(dkv[block * length : (block + 1) * length, :], w_qkv[:, width : 3 * width])
        if block == 0:
            own[...] += part + mm_nt(dq[...], w_qkv[:, 0:width])
            continue
        target = keep if block % 2 == 0 else send
        at = (block - 2) // 2 if block % 2 == 0 else block // 2
        target[at * length : (at + 1) * length, :] = part.astype(BF16)
    io.done(send, keep, own)
    small[...] = jnp.zeros_like(small)
    small[0:1, :] = d_gain
    small[1:2, :] = d_shift
    small[2:3, :] = column_sum(low)
    small[3:4, :] = column_sum(dq[...])
    small[4:5, :] = column_sum(dkv[:, width : 2 * width])


def weight_kernel(plan, io, *refs):
    out = refs[-1]
    for lefts, rights, column in plan:
        inner = refs[lefts[0]].shape[1]
        cols = refs[rights[0]].shape[1]
        step = 256
        wide = min(cols, 1536)
        io.ready(*[refs[i] for i in lefts + rights])

        def tile(i, carry, lefts=lefts, rights=rights, column=column, cols=cols, wide=wide):
            rows = pl.ds(pl.multiple_of(i * step, step), step)
            turned = [refs[l][:, rows].T for l in lefts]
            for start in range(0, cols, wide):
                total = None
                for left, r in zip(turned, rights):
                    term = mm(left, refs[r][:, start : start + wide])
                    total = term if total is None else total + term
                out[rows, column + start : column + start + wide] = total.astype(BF16)
            return carry

        lax.fori_loop(0, inner // step, tile, 0)


def sum_kernel(terms, io, *refs):
    n_out = 1 + max(t[0] for t in terms)
    outs = refs[len(refs) - n_out :]
    io.ready(*refs[: len(refs) - n_out])
    for which, (first, first_row), (second, second_row) in terms:
        out = outs[which]
        rows = out.shape[0]
        one = refs[first][first_row : first_row + rows, :].astype(F32)
        two = refs[second][second_row : second_row + rows, :].astype(F32)
        out[...] = (one + two).astype(out.dtype)
        io.done(out)


class Moves:
    def __init__(self, section, loads, stores):
        self.section_ref, self.loads, self.stores, self.started = section, dict(loads), dict(stores), set()
        self.waited = set()
        for copies in self.loads.values():
            for copy in copies:
                copy.start()

    def section(self):
        return self.section_ref[0]

    def ready(self, *refs):
        for ref in refs:
            if id(ref) not in self.waited:
                self.waited.add(id(ref))
                for copy in self.loads[id(ref)]:
                    copy.wait()

    def done(self, *refs):
        for ref in refs:
            if id(ref) not in self.started:
                self.started.add(id(ref))
                self.stores[id(ref)].start()

    def finish(self, ins, outs):
        self.ready(*ins)
        self.done(*outs)
        for copy in self.stores.values():
            copy.wait()


def call(kernel, outs, operands, *, chain, section, flops, scratch=(), role=None, into=()):
    groups = [list(o) if isinstance(o, (list, tuple)) else [o] for o in operands]
    flat = [a for g in groups for a in g]
    n_in, n_flat, n_out = len(groups), len(flat), len(outs)
    after = [chain[-1]] if chain else []
    n_rest = len(into) + len(after)

    def body(section_ref, *refs):
        hbm_in = refs[:n_flat]
        refs = refs[n_flat + n_rest :]
        hbm_out = refs[:n_out]
        refs = refs[n_out + 1 :]
        ins, vmem_out, rest = refs[:n_in], refs[n_in : n_in + n_out], refs[n_in + n_out :]
        in_sem, out_sem, extra = rest[0], rest[1], rest[2:]

        def run():
            loads, at = [], 0
            for ref, group in zip(ins, groups):
                copies, row = [], 0
                for array in group:
                    target = ref
                    if len(group) > 1:
                        target = ref.at[row : row + array.shape[0]]
                        row += array.shape[0]
                    copies.append(pltpu.make_async_copy(hbm_in[at], target, in_sem.at[at]))
                    at += 1
                loads.append((id(ref), copies))
            stores = [
                (id(ref), pltpu.make_async_copy(ref, hbm_out[i], out_sem.at[i]))
                for i, ref in enumerate(vmem_out)
            ]
            moves = Moves(section_ref, loads, stores)
            kernel(moves, *ins, *vmem_out, *extra)
            moves.finish(ins, vmem_out)

        if role is None:
            run()
        else:
            pl.when(section_ref[0] == role)(run)

    anywhere = pl.BlockSpec(memory_space=pl.ANY)
    in_shapes = [
        pltpu.VMEM((sum(a.shape[0] for a in g), *g[0].shape[1:]), g[0].dtype) for g in groups
    ]
    out_shapes = [pltpu.VMEM(o.shape, o.dtype) for o in outs]
    size = sum(math.prod(o.shape) * o.dtype.itemsize for o in list(outs) + flat)
    results = pl.pallas_call(
        body,
        out_shape=[*outs, jax.ShapeDtypeStruct((8, 128), F32)],
        in_specs=[pl.BlockSpec(memory_space=pltpu.SMEM)] + [anywhere] * (n_flat + n_rest),
        out_specs=[anywhere] * (n_out + 1),
        scratch_shapes=in_shapes
        + out_shapes
        + [pltpu.SemaphoreType.DMA((n_flat,)), pltpu.SemaphoreType.DMA((n_out,))]
        + list(scratch),
        input_output_aliases={1 + n_flat + i: i for i in range(len(into))},
        cost_estimate=pl.CostEstimate(flops=int(flops), bytes_accessed=int(size), transcendentals=0),
        compiler_params=pltpu.CompilerParams(vmem_limit_bytes=VMEM_LIMIT),
        name=getattr(kernel, "func", kernel).__name__,
    )(section, *flat, *into, *after)
    chain.append(results[-1])
    return results[:-1]


def shaped(*shape, kind=F32):
    return jax.ShapeDtypeStruct(shape, kind)


def pick(stacked, position):
    return lax.dynamic_index_in_dim(stacked, position, 0, keepdims=False)


def group_sum(parts, axis, members, stride, kind):
    length = lax.axis_size(axis)
    mine = (lax.axis_index(axis) // stride) % members
    total = pick(parts, mine).astype(F32)
    for step in range(1, members):
        pairs = []
        for i in range(length):
            at = (i // stride) % members
            pairs.append((i, i + ((at + step) % members - at) * stride))
        arrived = lax.ppermute(pick(parts, (mine + step) % members), axis, pairs)
        total = total + arrived.astype(F32)
    return total.astype(kind)


def scatter_sum(total):
    dp_size = lax.axis_size("dp")
    chips = lax.axis_size("seq") // 2
    rows = total.shape[0] // (dp_size * chips * 2)
    parts = jnp.moveaxis(total.reshape(dp_size, chips, 2, rows, *total.shape[1:]), 2, 0)
    parts = group_sum(parts, "seq", 2, 1, total.dtype)
    parts = group_sum(jnp.moveaxis(parts, 1, 0), "seq", chips, 2, total.dtype)
    return group_sum(parts, "dp", dp_size, 1, F32)


def to_encoder_half(total, section):
    half = total.shape[0] // 2
    arrived = lax.ppermute(total[:half], "section", [(1, 0)])
    return jnp.where(section == 0, arrived, total[half:])


def twin(x):
    return lax.ppermute(x, "seq", [(i, i ^ 1) for i in range(lax.axis_size("seq"))])


def chip_shift(x, step):
    length = lax.axis_size("seq")
    return lax.ppermute(x, "seq", [(i, (i + 2 * step) % length) for i in range(length)])


def row_gather(x):
    blocks = [x, twin(x)]
    for step in range(1, lax.axis_size("seq") // 2):
        far = chip_shift(x, -step)
        blocks += [far, twin(far)]
    return blocks


def shard_order():
    me = lax.axis_index("seq")
    length = lax.axis_size("seq")
    order = []
    for step in range(length // 2):
        far = (me + 2 * step) % length
        order += [far, far ^ 1]
    return order


def per_device(
    x_in, segments, cotangent, attn_in, attn_out, attn_bias, gains, ffn_in, ffn_bias, ffn_out,
    cross_q, cross_kv, cross_out, cross_bias, cross_gain,
):
    section = lax.axis_index("section")
    sec = section.astype(jnp.int32).reshape(1)
    micro, length, width = x_in.shape[1], x_in.shape[3], x_in.shape[4]
    seq_size = lax.axis_size("seq")
    tokens = length * seq_size
    hidden_units = ffn_in.shape[2]
    w_qkv, w_mix, w_in, w_out = attn_in[0], attn_out[0], ffn_in[0], ffn_out[0]
    b_in = ffn_bias
    vec = jnp.concatenate([attn_bias[0], gains[0]], 0)
    cross_vec = jnp.concatenate([cross_bias, cross_gain[None], jnp.zeros((3, width), F32)], 0)

    order = shard_order()
    place = jnp.arange(length, dtype=jnp.int32)
    key_place = jnp.concatenate([o * length + place for o in order])
    query_place = order[0] * length + place
    ids = jnp.moveaxis(segments[:, :, 0], 2, 0)
    all_ids = jnp.concatenate(row_gather(ids), 0)

    def allowed_bias(key_ids, query_ids, ordered):
        same = key_ids[:, None] == query_ids[None, :]
        before = (key_place[:, None] <= query_place[None, :]) | jnp.logical_not(ordered)
        return jnp.where(same & before, 0.0, MASKED).astype(F32)

    ticks = range(micro)
    last = micro - 1
    own_ids = pick(jnp.moveaxis(all_ids, 1, 0), section)
    own_queries = own_ids[:length]
    self_bias = [allowed_bias(own_ids[:, m], own_queries[:, m], section == 1) for m in ticks]
    cross_bias_of = [allowed_bias(all_ids[:, 0, m], own_queries[:, m], False) for m in ticks]

    attend_flops = 4 * length * tokens * width
    kv_flops = 4 * tokens * width * width
    square = 2 * length * width * width
    ffn_flops = 4 * length * width * hidden_units
    lw = shaped(length, width)
    lw_low = shaped(length, width, kind=BF16)
    tw_low = shaped(tokens, width, kind=BF16)
    lh_low = shaped(length, hidden_units, kind=BF16)
    pair_low = shaped(tokens, 2 * width, kind=BF16)
    half_low = shaped(tokens // 2, width, kind=BF16)
    rest_low = shaped(tokens // 2 - length, width, kind=BF16)
    lse_shape = shaped(LSE_ROWS, length)
    few = shaped(8, width)
    back_scratch = [pltpu.VMEM((length, width), BF16), pltpu.VMEM((LSE_ROWS, length), F32)]
    chips = seq_size // 2
    chain = []
    run = functools.partial(call, chain=chain, section=sec)

    def run_self(m):
        return run(
            self_kernel,
            [lw_low, tw_low, tw_low, lw_low, lse_shape, lw, lw, few],
            [x_all[m], w_qkv, w_mix, vec, self_bias[m]],
            flops=attend_flops + kv_flops + 2 * square,
        )

    def run_ffn(middle, role, into=()):
        return run(
            ffn_kernel,
            [lh_low, lh_low, lw, lw_low, lw_low],
            [middle, vec, w_in, b_in, w_out],
            flops=ffn_flops,
            role=role,
            into=into,
        )

    def run_ffn_back(grad, forward, role, into=()):
        return run(
            ffn_back_kernel,
            [lw_low, lh_low, lw, few],
            [grad, forward[2], vec, w_out, forward[1], w_in],
            flops=ffn_flops,
            role=role,
            into=into,
        )

    def run_cross(m):
        return run(
            cross_kernel,
            [lw_low, tw_low, tw_low, lw_low, lse_shape, lw, lw, lw_low],
            [selfs[m][6], cross_q, cross_vec, memory[m], cross_kv, cross_bias_of[m], cross_out],
            flops=attend_flops + kv_flops + 2 * square,
            role=1,
        )

    def run_cross_back(m):
        c = crosses[m]
        return run(
            cross_back_kernel,
            [lw_low, lw_low, pair_low, lw, half_low, half_low, few],
            [back[m][2], c[5], cross_vec, cross_out, c[3], c[0], c[1], cross_bias_of[m], c[4], c[2], cross_q, cross_kv],
            flops=3 * attend_flops + kv_flops + 2 * square,
            scratch=back_scratch,
            role=1,
        )

    def run_self_back(m, role, into=()):
        s = selfs[m]
        return run(
            self_back_kernel,
            [lw_low, lw_low, pair_low, lw, rest_low, half_low, few],
            [back[m][2], cross_back[m][3], s[5], vec, w_mix, s[3], s[0], s[1], self_bias[m], s[4], s[2], w_qkv],
            flops=3 * attend_flops + kv_flops + 2 * square,
            scratch=back_scratch,
            role=role,
            into=into,
        )

    def run_weights(products, out, role=None):
        operands, plan, flops = [], [], 0
        for lefts, rights, column in products:
            n, k = len(operands), len(lefts)
            operands += list(lefts) + list(rights)
            plan.append((tuple(range(n, n + k)), tuple(range(n + k, n + 2 * k)), column))
            rows = rights[0].shape[0]
            flops += 2 * k * rows * out.shape[0] * rights[0].shape[1]
        return run(functools.partial(weight_kernel, plan), [out], operands, flops=flops, role=role)[0]

    def run_sum(terms, outs, operands, role=None):
        return run(functools.partial(sum_kernel, terms), outs, operands, flops=0, role=role)

    def core_sums(keep, arrived, first, own_kind, role=None):
        operands = [keep, arrived] if first is None else [first, arrived, keep]
        terms, outs = [], []
        for step in range(chips):
            if first is None:
                mine = (0, step * length)
            else:
                mine = (0, 0) if step == 0 else (2, (step - 1) * length)
            terms.append((step, mine, (1, step * length)))
            outs.append(shaped(length, width, kind=own_kind if step == 0 else BF16))
        return run_sum(terms, outs, operands, role)

    def chip_sums(parts, kind, role=None):
        total = parts[0]
        for step in range(1, chips):
            out = shaped(length, width, kind=kind if step == chips - 1 else F32)
            total = run_sum([(0, (0, 0), (1, 0))], [out], [total, chip_shift(parts[step], step)], role)[0]
        return total

    x_all, selfs, enc_ffn, memory = [], [], [], []
    for m in ticks:
        x_all.append(row_gather(x_in[0, m, 0]))
        selfs.append(run_self(m))
        enc_ffn.append(run_ffn(selfs[m][6], 0))
        memory.append(row_gather(lax.ppermute(enc_ffn[m][4], "section", [(0, 1)])))

    ffn, back, crosses, cross_back, memory_grad, self_back = [], [], [], [], [], []

    def encoder_back(m):
        back[m] = run_ffn_back(memory_grad[m], ffn[m], 0, back[m])

    parts = None
    for m in ticks:
        crosses.append(run_cross(m))
        if parts is not None:
            parts = core_sums(cross_back[m - 1][4], twin(cross_back[m - 1][5]), None, F32, 1)
        ffn.append(run_ffn(crosses[m][6], 1, enc_ffn[m][:4]))
        back.append(run_ffn_back(cotangent[m, 0], ffn[m], 1))
        if parts is not None:
            total = chip_sums(parts, BF16, 1)
            memory_grad.append(lax.ppermute(total, "section", [(1, 0)]))
        cross_back.append(run_cross_back(m))
        if m > 0:
            encoder_back(m - 1)
            self_back.append(run_self_back(m - 1, 0))
        parts = True
    parts = core_sums(cross_back[last][4], twin(cross_back[last][5]), None, F32, 1)
    cross_weights = run_weights(
        [
            ([c[7] for c in crosses], [b[1] for b in cross_back], 0),
            (memory, [b[2] for b in cross_back], width),
            ([c[3] for c in crosses], [b[0] for b in cross_back], 3 * width),
        ],
        shaped(width, 4 * width, kind=BF16),
        role=1,
    )
    memory_grad.append(lax.ppermute(chip_sums(parts, BF16, 1), "section", [(1, 0)]))
    encoder_back(last)
    ffn_out_weights = run_weights(
        [([f[0] for f in ffn], [b[0] for b in back], 0)], shaped(hidden_units, width, kind=BF16)
    )
    ffn_in_weights = run_weights(
        [([f[3] for f in ffn], [b[1] for b in back], 0)], shaped(width, hidden_units, kind=BF16)
    )
    for m in range(last):
        self_back[m] = run_self_back(m, 1, self_back[m])
    self_back.append(run_self_back(last, None))
    attn_weights = run_weights(
        [
            ([x_in[0, m, 0] for m in ticks], [b[1] for b in self_back], 0),
            (x_all, [b[2] for b in self_back], width),
            ([s[3] for s in selfs], [b[0] for b in self_back], 3 * width),
        ],
        shaped(width, 4 * width, kind=BF16),
    )

    ffn_out_part = scatter_sum(ffn_out_weights)
    ffn_in_part = scatter_sum(ffn_in_weights)
    cross_part = scatter_sum(to_encoder_half(cross_weights, section))
    attn_part = scatter_sum(attn_weights)
    inputs_back = jnp.stack(
        [chip_sums(core_sums(b[4], twin(b[5]), b[3], F32), BF16) for b in self_back]
    )

    squares = sum(s[7] for s in selfs)
    f_small = sum(b[3] for b in back)
    s_small = sum(b[6] for b in self_back)
    c_small = sum(b[6] for b in cross_back)
    blocks = lax.axis_size("dp") * seq_size
    per = width // blocks
    half = per // 2
    per_hidden = hidden_units // blocks
    section_rows = jnp.stack(
        [s_small[3], s_small[4], s_small[2], f_small[2], s_small[1], f_small[1], s_small[0], f_small[0]]
    )
    cross_rows = jnp.stack([c_small[3], c_small[4], c_small[2], c_small[1], c_small[0]])
    cross_half = to_encoder_half(cross_rows.T, section)
    small = jnp.concatenate(
        [
            section_rows.T.reshape(blocks, 8 * per),
            f_small[3 : 3 + hidden_units // width].reshape(blocks, per_hidden),
            cross_half.reshape(blocks, 5 * half),
            jnp.broadcast_to(jnp.sum(squares[:2], 1)[None], (blocks, 2)),
        ],
        -1,
    )
    small = scatter_sum(small)[0]
    section_small = small[: 8 * per].reshape(per, 8).T
    ffn_bias_part = small[8 * per : 8 * per + per_hidden]
    rest = small[8 * per + per_hidden :]
    cross_small = rest[: 5 * half].reshape(half, 5).T
    count = micro * lax.axis_size("dp") * tokens * width
    stats = jnp.sqrt(rest[5 * half :] / count)[None]
    results = jnp.stack([jnp.where(section == 0, e[4], f[4]) for e, f in zip(enc_ffn, ffn)])
    return (
        results[None, :, None],
        inputs_back[None, :, None],
        stats,
        attn_part[None, :, : 3 * width],
        attn_part[None, :, 3 * width :],
        section_small[None, :6],
        section_small[None, 6:],
        ffn_in_part[None],
        ffn_bias_part[None],
        ffn_out_part[None],
        cross_part[:, :width],
        cross_part[:, width : 3 * width],
        cross_part[:, 3 * width :],
        cross_small[:4],
        cross_small[4],
    )


def solution(mesh):
    return jax.shard_map(
        per_device,
        mesh=mesh,
        in_specs=(
            P("section", None, "dp", "seq", None),
            P(None, None, "dp", "seq"),
            P(None, "dp", "seq", None),
            P("section", None, None),
            P("section", None, None),
            P("section", None, None),
            P("section", None, None),
            P("section", None, None),
            P("section", None),
            P("section", None, None),
            P(),
            P(),
            P(),
            P(),
            P(),
        ),
        out_specs=(
            P("section", None, "dp", "seq", None),
            P("section", None, "dp", "seq", None),
            P("section", None),
            P("section", ("dp", "seq"), None),
            P("section", ("dp", "seq"), None),
            P("section", None, ("dp", "seq")),
            P("section", None, ("dp", "seq")),
            P("section", ("dp", "seq"), None),
            P("section", ("dp", "seq")),
            P("section", ("dp", "seq"), None),
            P(("section", "dp", "seq"), None),
            P(("section", "dp", "seq"), None),
            P(("section", "dp", "seq"), None),
            P(None, ("section", "dp", "seq")),
            P(("section", "dp", "seq")),
        ),
        check_vma=False,
    )
```

time: 1210 us -> 625 us (0.52)
  the two profiles are of different devices: /device:TPU:0 before, /device:TPU:2 now
where the time goes in v2:
time: 625 us; the launch traced here: 615 us
  Pallas kernels  217 us (35%)
  waiting for transfers between devices  186 us (30%)
  local copies, waits for them, and re-layouts  127 us (20%)
  starting transfers between devices  61 us (10%)
  other arithmetic  19.8 us (3%)
    pallas_call x29, Pallas kernels, call(): pl.pallas_call(body, out_shape=[*outs, jax.ShapeDtypeStruct((8, 128), F32...  217 us
    ppermute x25, waiting for transfers between devices, group_sum(): arrived = lax.ppermute(pick(parts, (mine + step) % members), axis, pairs)  120 us
    unnamed x452, local copies, waits for them, and re-layouts  103 us
    ppermute x25, starting transfers between devices, group_sum(): arrived = lax.ppermute(pick(parts, (mine + step) % members), axis, pairs)  36.5 us
    ppermute x2, waiting for transfers between devices, per_device(): memory.append(row_gather(lax.ppermute(enc_ffn[m][4], 'section', [(0, 1)])))  33.9 us
    ppermute x9, waiting for transfers between devices, chip_shift(): lax.ppermute(x, 'seq', [(i, (i + 2 * step) % length) for i in range(lengt...  23.2 us
  transfers between devices with their start and end apart: 54, of which 19 were waited for; matrix products, arithmetic and copies ran while one was open for 7% of the time, Pallas kernels for 34%

profile of v2, /device:TPU:2, one launch (start us, length us, event | category | flops | bytes accessed | tf_op | source)
XLA Modules:
  0.0 615.1 jit_solution(18256513893868844121)
XLA Ops:
  18.7 16.1 %self_kernel.2 = (bf16[256,768]{1,0:T(8,128)(2,1)S(1)}, bf16[1024,768]{1,0:T(8,128)(2,1)S(1)}, bf16[1024,768]{1,0:T(8,128)(2,1)S(1)}, bf16[256,768]{1,0:T(8,128)...) custom-call(s32[1]{0:T(128)} %bitcast.section_ref, ...), custom_call_target="tpu_custom_call" | custom-call | flops 3825205248 | bytes 12910592 | tf_op jit(solution)/shard_map/self_kernel/pallas_call | solution.py:445
  42.6 17.9 %collective-permute-done.6.refs_3_.refs_4_ = bf16[256,768]{1,0:T(8,128)(2,1)S(1)} collective-permute-done((bf16[256,768]{1,0:T(8,128)(2,1)S(1)}, bf16[256,768]{1,0:T(8,128)(2,1)S(1)}, u32[]{:S(2)}, u32[]{:S(2)}) %collective-permute-start.6) | collective-permute-done | bytes 393248 | tf_op jit(solution)/shard_map/ppermute | solution.py:677
  62.9 16.0 %self_kernel.3 = (bf16[256,768]{1,0:T(8,128)(2,1)S(1)}, bf16[1024,768]{1,0:T(8,128)(2,1)S(1)}, bf16[1024,768]{1,0:T(8,128)(2,1)S(1)}, bf16[256,768]{1,0:T(8,128)...) custom-call(s32[1]{0:T(128)} %bitcast.section_ref, ...), custom_call_target="tpu_custom_call" | custom-call | flops 3825205248 | bytes 12910592 | tf_op jit(solution)/shard_map/self_kernel/pallas_call | solution.py:445
  88.9 16.0 %collective-permute-done.13.refs_3_.refs_8_ = bf16[256,768]{1,0:T(8,128)(2,1)} collective-permute-done((bf16[256,768]{1,0:T(8,128)(2,1)S(1)}, bf16[256,768]{1,0:T(8,128)(2,1)}, u32[]{:S(2)}, u32[]{:S(2)}) %collective-permute-start.13) | collective-permute-done | bytes 393248 | tf_op jit(solution)/shard_map/ppermute | solution.py:677
  114.9 16.3 %cross_kernel.2 = (bf16[256,768]{1,0:T(8,128)(2,1)S(1)}, bf16[1024,768]{1,0:T(8,128)(2,1)S(1)}, bf16[1024,768]{1,0:T(8,128)(2,1)S(1)}, bf16[256,768]{1,0:T(8,128...) custom-call(s32[1]{0:T(128)} %bitcast.section_ref, ...), custom_call_target="tpu_custom_call" | custom-call | flops 3825205248 | bytes 14065664 | tf_op jit(solution)/shard_map/cross_kernel/pallas_call | solution.py:445
  135.8 9.5 %ffn_kernel.6 = (bf16[256,3072]{1,0:T(8,128)(2,1)S(1)}, bf16[256,3072]{1,0:T(8,128)(2,1)S(1)}, f32[256,768]{1,0:T(8,128)S(1)}, bf16[256,768]{1,0:T(8,128)(2,1)S(...) custom-call(s32[1]{0:T(128)} %bitcast.section_ref, ...), custom_call_target="tpu_custom_call", output_to_operand_aliasing={{0}: (6, {}), {1}: (7, {}), {2}: (8, {}), {3}: (9, {})} | custom-call | flops 2415919104 | bytes 14979072 | tf_op jit(solution)/shard_map/ffn_kernel/pallas_call | solution.py:445
  146.2 8.8 %ffn_back_kernel.4 = (bf16[256,768]{1,0:T(8,128)(2,1)S(1)}, bf16[256,3072]{1,0:T(8,128)(2,1)S(1)}, f32[256,768]{1,0:T(8,128)S(1)}, f32[8,768]{1,0:T(8,128)S(1)}, f32[8,128]{1,0:T(8,128)S(1)}) custom-call(s32[1]{0:T(128)} %bitcast.section_ref, bf16[256,768]{1,0:T(8,128)(2,1)S(1)} %get-tuple-element.357.refs_0_, f32[256,768]{1,0:T(8,128)S(1)} %get-tuple-element.177.refs_1_, ...), custom_call_target="tpu_custom_call" | custom-call | flops 2415919104 | bytes 14991360 | tf_op jit(solution)/shard_map/ffn_back_kernel/pallas_call | solution.py:445
  160.7 17.8 %cross_back_kernel.2 = (bf16[256,768]{1,0:T(8,128)(2,1)S(1)}, bf16[256,768]{1,0:T(8,128)(2,1)S(1)}, bf16[1024,1536]{1,0:T(8,128)(2,1)}, f32[256,768]{1,0:T(8,128...) custom-call(s32[1]{0:T(128)} %bitcast.section_ref, ...), custom_call_target="tpu_custom_call" | custom-call | flops 5435817984 | bytes 17629184 | tf_op jit(solution)/shard_map/cross_back_kernel/pallas_call | solution.py:445
  190.0 16.1 %cross_kernel.3 = (bf16[256,768]{1,0:T(8,128)(2,1)S(1)}, bf16[1024,768]{1,0:T(8,128)(2,1)S(1)}, bf16[1024,768]{1,0:T(8,128)(2,1)S(1)}, bf16[256,768]{1,0:T(8,128...) custom-call(s32[1]{0:T(128)} %bitcast.section_ref, ...), custom_call_target="tpu_custom_call" | custom-call | flops 3825205248 | bytes 14065664 | tf_op jit(solution)/shard_map/cross_kernel/pallas_call | solution.py:445
  212.0 9.3 %ffn_kernel.7 = (bf16[256,3072]{1,0:T(8,128)(2,1)S(1)}, bf16[256,3072]{1,0:T(8,128)(2,1)S(1)}, f32[256,768]{1,0:T(8,128)S(1)}, bf16[256,768]{1,0:T(8,128)(2,1)S(...) custom-call(s32[1]{0:T(128)} %bitcast.section_ref, ...), custom_call_target="tpu_custom_call", output_to_operand_aliasing={{0}: (6, {}), {1}: (7, {}), {2}: (8, {}), {3}: (9, {})} | custom-call | flops 2415919104 | bytes 14979072 | tf_op jit(solution)/shard_map/ffn_kernel/pallas_call | solution.py:445
  221.5 8.7 %ffn_back_kernel.5 = (bf16[256,768]{1,0:T(8,128)(2,1)S(1)}, bf16[256,3072]{1,0:T(8,128)(2,1)S(1)}, f32[256,768]{1,0:T(8,128)S(1)}, f32[8,768]{1,0:T(8,128)S(1)}, f32[8,128]{1,0:T(8,128)S(1)}) custom-call(s32[1]{0:T(128)} %bitcast.section_ref, bf16[256,768]{1,0:T(8,128)(2,1)S(1)} %copy-done.11, f32[256,768]{1,0:T(8,128)S(1)} %get-tuple-element.201.refs_1_, ...), custom_call_target="tpu_custom_call" | custom-call | flops 2415919104 | bytes 14991360 | tf_op jit(solution)/shard_map/ffn_back_kernel/pallas_call | solution.py:445
  238.1 17.7 %cross_back_kernel.3 = (bf16[256,768]{1,0:T(8,128)(2,1)S(1)}, bf16[256,768]{1,0:T(8,128)(2,1)S(1)}, bf16[1024,1536]{1,0:T(8,128)(2,1)}, f32[256,768]{1,0:T(8,128...) custom-call(s32[1]{0:T(128)} %bitcast.section_ref, ...), custom_call_target="tpu_custom_call" | custom-call | flops 5435817984 | bytes 17629184 | tf_op jit(solution)/shard_map/cross_back_kernel/pallas_call | solution.py:445
  278.5 13.0 %weight_kernel.4 = (bf16[768,3072]{1,0:T(8,128)(2,1)}, f32[8,128]{1,0:T(8,128)S(1)}) custom-call(s32[1]{0:T(128)} %bitcast.section_ref, bf16[256,768]{1,0:T(8,128)(2,1)S(1)} %copy-done.171, bf16[256,768]{1,0:T(8,128)(2,1)S(1)} %copy-done.176, bf16[256,768]{1,0:T(8,128)(2,1)S(1)} %copy-done.193, bf16[256,768]{1,0:T(8,128)(2,1)S(1)} %copy-done.197, ...), custom_call_target="tpu_custom_call" | custom-call | flops 6039797760 | bytes 17301504 | tf_op jit(solution)/shard_map/weight_kernel/pallas_call | solution.py:445
  332.3 17.1 %self_back_kernel.4 = (bf16[256,768]{1,0:T(8,128)(2,1)S(1)}, bf16[256,768]{1,0:T(8,128)(2,1)S(1)}, bf16[1024,1536]{1,0:T(8,128)(2,1)S(1)}, f32[256,768]{1,0:T(8,...) custom-call(s32[1]{0:T(128)} %bitcast.section_ref, ...), custom_call_target="tpu_custom_call", output_to_operand_aliasing={{0}: (13, {}), {1}: (14, {}), {2}: (15, {}), {3}: (16, {}),... | custom-call | flops 5435817984 | bytes 18022400 | tf_op jit(solution)/shard_map/self_back_kernel/pallas_call | solution.py:445
  351.0 16.8 %self_back_kernel.5 = (bf16[256,768]{1,0:T(8,128)(2,1)S(1)}, bf16[256,768]{1,0:T(8,128)(2,1)S(1)}, bf16[1024,1536]{1,0:T(8,128)(2,1)S(1)}, f32[256,768]{1,0:T(8,...) custom-call(s32[1]{0:T(128)} %bitcast.section_ref, ...), custom_call_target="tpu_custom_call" | custom-call | flops 5435817984 | bytes 18022400 | tf_op jit(solution)/shard_map/self_back_kernel/pallas_call | solution.py:445
  387.5 13.6 %weight_kernel.7 = (bf16[768,3072]{1,0:T(8,128)(2,1)}, f32[8,128]{1,0:T(8,128)S(1)}) custom-call(s32[1]{0:T(128)} %bitcast.section_ref, bf16[256,768]{1,0:T(8,128)(2,1)S(1)} %copy-done.48, bf16[256,768]{1,0:T(8,128)(2,1)S(1)} %copy-done.50, bf16[256,768]{1,0:T(8,128)(2,1)S(1)} %copy-done.144, bf16[256,768]{1,0:T(8,128)(2,1)S(1)} %copy-done.189, ...), custom_call_target="tpu_custom_call" | custom-call | flops 6039797760 | bytes 17301504 | tf_op jit(solution)/shard_map/weight_kernel/pallas_call | solution.py:445
  426.5 7.8 %collective-permute-done.24.refs_1_ = bf16[256,768]{1,0:T(8,128)(2,1)S(1)} collective-permute-done((bf16[256,768]{1,0:T(8,128)(2,1)}, bf16[256,768]{1,0:T(8,128)(2,1)S(1)}, u32[]{:S(2)}, u32[]{:S(2)}) %collective-permute-start.24) | collective-permute-done | bytes 393248 | tf_op jit(solution)/shard_map/ppermute | solution.py:507
  440.8 8.6 %collective-permute-done.26.refs_1_ = bf16[256,768]{1,0:T(8,128)(2,1)S(1)} collective-permute-done((bf16[256,768]{1,0:T(8,128)(2,1)S(1)}, bf16[256,768]{1,0:T(8,128)(2,1)S(1)}, u32[]{:S(2)}, u32[]{:S(2)}) %collective-permute-start.26) | collective-permute-done | bytes 393248 | tf_op jit(solution)/shard_map/ppermute | solution.py:507
  461.0 57.8 %collective-permute-done.50 = bf16[4,24,3072]{2,1,0:T(8,128)(2,1)S(1)} collective-permute-done((bf16[4,24,3072]{2,1,0:T(8,128)(2,1)S(1)}, bf16[4,24,3072]{2,1,0:T(8,128)(2,1)S(1)}, u32[]{:S(2)}, u32[]{:S(2)}) %collective-permute-start.50) | collective-permute-done | bytes 589856 | tf_op jit(solution)/shard_map/ppermute | solution.py:480
  540.5 11.1 %collective-permute-done.34 = bf16[4,48,3072]{2,1,0:T(8,128)(2,1)S(1)} collective-permute-done((bf16[4,48,3072]{2,1,0:T(8,128)(2,1)S(1)}, bf16[4,48,3072]{2,1,0:T(8,128)(2,1)S(1)}, u32[]{:S(2)}, u32[]{:S(2)}) %collective-permute-start.34) | collective-permute-done | bytes 1179680 | tf_op jit(solution)/shard_map/ppermute | solution.py:480
  556.5 7.5 %collective-permute-done.35 = bf16[48,3072]{1,0:T(8,128)(2,1)S(1)} collective-permute-done((bf16[48,3072]{1,0:T(8,128)(2,1)S(1)}, bf16[48,3072]{1,0:T(8,128)(2,1)S(1)}, u32[]{:S(2)}, u32[]{:S(2)}) %collective-permute-start.35) | collective-permute-done | bytes 294944 | tf_op jit(solution)/shard_map/ppermute | solution.py:480
  564.0 13.9 %collective-permute-start.46 = (bf16[192,768]{1,0:T(8,128)(2,1)S(1)}, bf16[192,768]{1,0:T(8,128)(2,1)S(1)}, u32[]{:S(2)}, u32[]{:S(2)}) collective-permute-start(bf16[192,768]{1,0:T(8,128)(2,1)S(1)} %get-tuple-element.349), channel_id=1, source_target_pairs={{0,8},{4,12},{8,0},{12,4},{1,9},{5,13},{9,1},{13,5},{2,10},{6,14},... | collective-permute-start | bytes 884744 | tf_op jit(solution)/shard_map/ppermute | solution.py:480
  579.1 15.3 %collective-permute-done.36 = bf16[48,3072]{1,0:T(8,128)(2,1)S(1)} collective-permute-done((bf16[48,3072]{1,0:T(8,128)(2,1)S(1)}, bf16[48,3072]{1,0:T(8,128)(2,1)S(1)}, u32[]{:S(2)}, u32[]{:S(2)}) %collective-permute-start.36) | collective-permute-done | bytes 294944 | tf_op jit(solution)/shard_map/ppermute | solution.py:480
  602.4 11.3 %collective-permute-done.41 = bf16[48,3072]{1,0:T(8,128)(2,1)S(1)} collective-permute-done((bf16[48,3072]{1,0:T(8,128)(2,1)S(1)}, bf16[48,3072]{1,0:T(8,128)(2,1)S(1)}, u32[]{:S(2)}, u32[]{:S(2)}) %collective-permute-start.41) | collective-permute-done | bytes 294944 | tf_op jit(solution)/shard_map/ppermute | solution.py:480
  (664 shorter events, 247.6 us)
Async XLA Ops:
  4.9 37.4 %collective-permute-start.11 = (bf16[256,768]{1,0:T(8,128)(2,1)S(1)}, bf16[256,768]{1,0:T(8,128)(2,1)}, u32[]{:S(2)}, u32[]{:S(2)}) collective-permute-start(bf16[256,768]{1,0:T(8,128)(2,1)S(1)} %get-tuple-element.359.refs_0_.refs_1_.refs_8_), channel_id=1, source_target_pairs={{0,2},{1,3},{2,0},{3,1},{4,6},{5,7},{6,4},{7,5},{8,10},{9,11},{10,... | collective-permute-start | bytes 1179656 | tf_op jit(solution)/shard_map/ppermute | solution.py:507
  40.5 20.0 %collective-permute-start.6 = (bf16[256,768]{1,0:T(8,128)(2,1)S(1)}, bf16[256,768]{1,0:T(8,128)(2,1)S(1)}, u32[]{:S(2)}, u32[]{:S(2)}) collective-permute-start(bf16[256,768]{1,0:T(8,128)(2,1)S(1)} %get-tuple-element.164), channel_id=1, source_target_pairs={{0,16},{1,17},{2,18},{3,19},{4,20},{5,21},{6,22},{7,23},{8,24},{9,... | collective-permute-start | bytes 1179656 | tf_op jit(solution)/shard_map/ppermute | solution.py:677
  60.5 27.0 %collective-permute-start.8 = (bf16[256,768]{1,0:T(8,128)(2,1)S(1)}, bf16[256,768]{1,0:T(8,128)(2,1)S(1)}, u32[]{:S(2)}, u32[]{:S(2)}) collective-permute-start(bf16[256,768]{1,0:T(8,128)(2,1)S(1)} %collective-permute-done.6.refs_3_.refs_4_), channel_id=1, source_target_pairs={{0,2},{1,3},{2,0},{3,1},{4,6},{5,7},{6,4},{7,5},{8,10},{9,11},{10,... | collective-permute-start | bytes 1179656 | tf_op jit(solution)/shard_map/ppermute | solution.py:507
  104.8 77.4 %collective-permute-start.15 = (bf16[256,768]{1,0:T(8,128)(2,1)}, bf16[256,768]{1,0:T(8,128)(2,1)}, u32[]{:S(2)}, u32[]{:S(2)}) collective-permute-start(bf16[256,768]{1,0:T(8,128)(2,1)} %collective-permute-done.13.refs_3_.refs_8_), channel_id=1, source_target_pairs={{0,2},{1,3},{2,0},{3,1},{4,6},{5,7},{6,4},{7,5},{8,10},{9,11},{10,... | collective-permute-start | bytes 1179656 | tf_op jit(solution)/shard_map/ppermute | solution.py:507
  181.8 25.6 %collective-permute-start.17 = (bf16[512,768]{1,0:T(8,128)(2,1)}, bf16[512,768]{1,0:T(8,128)(2,1)}, u32[]{:S(2)}, u32[]{:S(2)}) collective-permute-start(bf16[512,768]{1,0:T(8,128)(2,1)} %get-tuple-element.195), channel_id=1, source_target_pairs={{0,1},{1,0},{2,3},{3,2},{4,5},{5,4},{6,7},{7,6},{8,9},{9,8},{10,11... | collective-permute-start | bytes 2359304 | tf_op jit(solution)/shard_map/ppermute | solution.py:502
  210.0 21.8 %collective-permute-start.18 = (bf16[256,768]{1,0:T(8,128)(2,1)S(1)}, bf16[256,768]{1,0:T(8,128)(2,1)S(1)}, u32[]{:S(2)}, u32[]{:S(2)}) collective-permute-start(bf16[256,768]{1,0:T(8,128)(2,1)S(1)} %get-tuple-element.200), channel_id=1, source_target_pairs={{0,2},{1,3},{2,0},{3,1},{4,6},{5,7},{6,4},{7,5},{8,10},{9,11},{10,... | collective-permute-start | bytes 1179656 | tf_op jit(solution)/shard_map/ppermute | solution.py:507
  232.9 25.4 %collective-permute-start.19 = (bf16[256,768]{1,0:T(8,128)(2,1)}, bf16[256,768]{1,0:T(8,128)(2,1)}, u32[]{:S(2)}, u32[]{:S(2)}) collective-permute-start(bf16[256,768]{1,0:T(8,128)(2,1)} %get-tuple-element.205), channel_id=1, source_target_pairs={{16,0},{17,1},{18,2},{19,3},{20,4},{21,5},{22,6},{23,7},{24,8},{25... | collective-permute-start | bytes 1179656 | tf_op jit(solution)/shard_map/ppermute | solution.py:693
  268.0 23.6 %collective-permute-start.21 = (bf16[256,768]{1,0:T(8,128)(2,1)S(1)}, bf16[256,768]{1,0:T(8,128)(2,1)S(1)}, u32[]{:S(2)}, u32[]{:S(2)}) collective-permute-start(bf16[256,768]{1,0:T(8,128)(2,1)S(1)} %get-tuple-element.241), channel_id=1, source_target_pairs={{0,2},{1,3},{2,0},{3,1},{4,6},{5,7},{6,4},{7,5},{8,10},{9,11},{10,... | collective-permute-start | bytes 1179656 | tf_op jit(solution)/shard_map/ppermute | solution.py:507
  292.1 20.0 %collective-permute-start.22 = (bf16[256,768]{1,0:T(8,128)(2,1)S(1)}, bf16[256,768]{1,0:T(8,128)(2,1)S(1)}, u32[]{:S(2)}, u32[]{:S(2)}) collective-permute-start(bf16[256,768]{1,0:T(8,128)(2,1)S(1)} %get-tuple-element.252), channel_id=1, source_target_pairs={{16,0},{17,1},{18,2},{19,3},{20,4},{21,5},{22,6},{23,7},{24,8},{25... | collective-permute-start | bytes 1179656 | tf_op jit(solution)/shard_map/ppermute | solution.py:709
  306.2 132.1 %collective-permute-start.48 = (bf16[384,3072]{1,0:T(8,128)(2,1)}, bf16[384,3072]{1,0:T(8,128)(2,1)}, u32[]{:S(2)}, u32[]{:S(2)}) collective-permute-start(bf16[384,3072]{1,0:T(8,128)(2,1)} %slice.176), channel_id=1, source_target_pairs={{16,0},{17,1},{18,2},{19,3},{20,4},{21,5},{22,6},{23,7},{24,8},{25... | collective-permute-start | bytes 7077896 | tf_op jit(solution)/shard_map/ppermute | solution.py:497
  374.3 28.6 %collective-permute-start.28 = (f32[4,2,1,698]{3,2,1,0:T(1,128)S(1)}, f32[4,2,1,698]{3,2,1,0:T(1,128)S(1)}, u32[]{:S(2)}, u32[]{:S(2)}) collective-permute-start(f32[4,2,1,698]{3,2,1,0:T(1,128)S(1)} %dynamic-slice_bitcast_fusion.16), channel_id=1, source_target_pairs={{0,1},{1,0},{2,3},{3,2},{4,5},{5,4},{6,7},{7,6},{8,9},{9,8},{10,11... | collective-permute-start | bytes 67016 | tf_op jit(solution)/shard_map/ppermute | solution.py:480
  418.1 32.7 %collective-permute-start.43 = (bf16[4,2,192,768]{3,2,0,1:T(8,128)(2,1)}, bf16[4,2,192,768]{3,2,0,1:T(8,128)(2,1)}, u32[]{:S(2)}, u32[]{:S(2)}) collective-permute-start(bf16[4,2,192,768]{3,2,0,1:T(8,128)(2,1)} %bitcast.172), channel_id=1, source_target_pairs={{0,1},{1,0},{2,3},{3,2},{4,5},{5,4},{6,7},{7,6},{8,9},{9,8},{10,11... | collective-permute-start | bytes 7077896 | tf_op jit(solution)/shard_map/ppermute | solution.py:480
  418.6 35.1 %collective-permute-start.38 = (bf16[4,2,48,3072]{3,2,0,1:T(8,128)(2,1)}, bf16[4,2,48,3072]{3,2,0,1:T(8,128)(2,1)}, u32[]{:S(2)}, u32[]{:S(2)}) collective-permute-start(bf16[4,2,48,3072]{3,2,0,1:T(8,128)(2,1)} %bitcast.173), channel_id=1, source_target_pairs={{0,1},{1,0},{2,3},{3,2},{4,5},{5,4},{6,7},{7,6},{8,9},{9,8},{10,11... | collective-permute-start | bytes 7077896 | tf_op jit(solution)/shard_map/ppermute | solution.py:480
  434.3 25.7 %collective-permute-start.33 = (bf16[4,2,48,3072]{3,2,0,1:T(8,128)(2,1)}, bf16[4,2,48,3072]{3,2,0,1:T(8,128)(2,1)S(1)}, u32[]{:S(2)}, u32[]{:S(2)}) collective-permute-start(bf16[4,2,48,3072]{3,2,0,1:T(8,128)(2,1)} %bitcast.225), channel_id=1, source_target_pairs={{0,1},{1,0},{2,3},{3,2},{4,5},{5,4},{6,7},{7,6},{8,9},{9,8},{10,11... | collective-permute-start | bytes 7077896 | tf_op jit(solution)/shard_map/ppermute | solution.py:480
  453.1 83.1 %collective-permute-start.44 = (bf16[4,192,768]{2,1,0:T(8,128)(2,1)S(1)}, bf16[4,192,768]{2,1,0:T(8,128)(2,1)S(1)}, u32[]{:S(2)}, u32[]{:S(2)}) collective-permute-start(bf16[4,192,768]{2,1,0:T(8,128)(2,1)S(1)} %dynamic-slice_bitcast_fusion), channel_id=1, source_target_pairs={{0,2},{1,3},{2,0},{3,1},{4,6},{5,7},{6,4},{7,5},{8,10},{9,11},{10,... | collective-permute-start | bytes 3538952 | tf_op jit(solution)/shard_map/ppermute | solution.py:480
  457.4 98.6 %collective-permute-start.39 = (bf16[4,48,3072]{2,1,0:T(8,128)(2,1)S(1)}, bf16[4,48,3072]{2,1,0:T(8,128)(2,1)S(1)}, u32[]{:S(2)}, u32[]{:S(2)}) collective-permute-start(bf16[4,48,3072]{2,1,0:T(8,128)(2,1)S(1)} %dynamic-slice_bitcast_fusion.1), channel_id=1, source_target_pairs={{0,2},{1,3},{2,0},{3,1},{4,6},{5,7},{6,4},{7,5},{8,10},{9,11},{10,... | collective-permute-start | bytes 3538952 | tf_op jit(solution)/shard_map/ppermute | solution.py:480
  458.5 60.2 %collective-permute-start.50 = (bf16[4,24,3072]{2,1,0:T(8,128)(2,1)S(1)}, bf16[4,24,3072]{2,1,0:T(8,128)(2,1)S(1)}, u32[]{:S(2)}, u32[]{:S(2)}) collective-permute-start(bf16[4,24,3072]{2,1,0:T(8,128)(2,1)S(1)} %dynamic-slice_bitcast_fusion.3), channel_id=1, source_target_pairs={{0,2},{1,3},{2,0},{3,1},{4,6},{5,7},{6,4},{7,5},{8,10},{9,11},{10,... | collective-permute-start | bytes 1769480 | tf_op jit(solution)/shard_map/ppermute | solution.py:480
  527.7 24.0 %collective-permute-start.34 = (bf16[4,48,3072]{2,1,0:T(8,128)(2,1)S(1)}, bf16[4,48,3072]{2,1,0:T(8,128)(2,1)S(1)}, u32[]{:S(2)}, u32[]{:S(2)}) collective-permute-start(bf16[4,48,3072]{2,1,0:T(8,128)(2,1)S(1)} %dynamic-slice_bitcast_fusion.2), channel_id=1, source_target_pairs={{0,2},{1,3},{2,0},{3,1},{4,6},{5,7},{6,4},{7,5},{8,10},{9,11},{10,... | collective-permute-start | bytes 3538952 | tf_op jit(solution)/shard_map/ppermute | solution.py:480
  536.6 58.7 %collective-permute-start.45 = (bf16[192,768]{1,0:T(8,128)(2,1)S(1)}, bf16[192,768]{1,0:T(8,128)(2,1)S(1)}, u32[]{:S(2)}, u32[]{:S(2)}) collective-permute-start(bf16[192,768]{1,0:T(8,128)(2,1)S(1)} %get-tuple-element.347), channel_id=1, source_target_pairs={{0,4},{4,8},{8,12},{12,0},{1,5},{5,9},{9,13},{13,1},{2,6},{6,10},{... | collective-permute-start | bytes 884744 | tf_op jit(solution)/shard_map/ppermute | solution.py:480
  536.7 59.3 %collective-permute-start.47 = (bf16[192,768]{1,0:T(8,128)(2,1)S(1)}, bf16[192,768]{1,0:T(8,128)(2,1)S(1)}, u32[]{:S(2)}, u32[]{:S(2)}) collective-permute-start(bf16[192,768]{1,0:T(8,128)(2,1)S(1)} %get-tuple-element.348), channel_id=1, source_target_pairs={{0,12},{4,0},{8,4},{12,8},{1,13},{5,1},{9,5},{13,9},{2,14},{6,2},{... | collective-permute-start | bytes 884744 | tf_op jit(solution)/shard_map/ppermute | solution.py:480
  552.2 25.7 %collective-permute-start.37 = (bf16[48,3072]{1,0:T(8,128)(2,1)S(1)}, bf16[48,3072]{1,0:T(8,128)(2,1)S(1)}, u32[]{:S(2)}, u32[]{:S(2)}) collective-permute-start(bf16[48,3072]{1,0:T(8,128)(2,1)S(1)} %get-tuple-element.354), channel_id=1, source_target_pairs={{0,12},{4,0},{8,4},{12,8},{1,13},{5,1},{9,5},{13,9},{2,14},{6,2},{... | collective-permute-start | bytes 884744 | tf_op jit(solution)/shard_map/ppermute | solution.py:480
  556.0 38.3 %collective-permute-start.36 = (bf16[48,3072]{1,0:T(8,128)(2,1)S(1)}, bf16[48,3072]{1,0:T(8,128)(2,1)S(1)}, u32[]{:S(2)}, u32[]{:S(2)}) collective-permute-start(bf16[48,3072]{1,0:T(8,128)(2,1)S(1)} %get-tuple-element.355), channel_id=1, source_target_pairs={{0,8},{4,12},{8,0},{12,4},{1,9},{5,13},{9,1},{13,5},{2,10},{6,14},... | collective-permute-start | bytes 884744 | tf_op jit(solution)/shard_map/ppermute | solution.py:480
  564.0 36.6 %collective-permute-start.46 = (bf16[192,768]{1,0:T(8,128)(2,1)S(1)}, bf16[192,768]{1,0:T(8,128)(2,1)S(1)}, u32[]{:S(2)}, u32[]{:S(2)}) collective-permute-start(bf16[192,768]{1,0:T(8,128)(2,1)S(1)} %get-tuple-element.349), channel_id=1, source_target_pairs={{0,8},{4,12},{8,0},{12,4},{1,9},{5,13},{9,1},{13,5},{2,10},{6,14},... | collective-permute-start | bytes 884744 | tf_op jit(solution)/shard_map/ppermute | solution.py:480
  577.9 23.7 %collective-permute-start.40 = (bf16[48,3072]{1,0:T(8,128)(2,1)S(1)}, bf16[48,3072]{1,0:T(8,128)(2,1)S(1)}, u32[]{:S(2)}, u32[]{:S(2)}) collective-permute-start(bf16[48,3072]{1,0:T(8,128)(2,1)S(1)} %get-tuple-element.350), channel_id=1, source_target_pairs={{0,4},{4,8},{8,12},{12,0},{1,5},{5,9},{9,13},{13,1},{2,6},{6,10},{... | collective-permute-start | bytes 884744 | tf_op jit(solution)/shard_map/ppermute | solution.py:480
  (254 other events, 2236.9 us)

commit v3 on v2

v3 whole, which is shorter than its diff:
```python
import enum
import functools
import math

import jax
import jax.numpy as jnp
from jax import lax
from jax.experimental import pallas as pl
from jax.experimental.pallas import tpu as pltpu
from jax.sharding import PartitionSpec as P

HEADS = 12
HEAD_DIM = 64
PAIR = 2 * HEAD_DIM
EPSILON = 1e-05
MASKED = -1000000000.0
SCALE = 1.0 / math.sqrt(HEAD_DIM)
VMEM_LIMIT = 58 * 1024 * 1024

F32 = jnp.float32
BF16 = jnp.bfloat16


def mm(a, b):
    return jnp.dot(a, b, preferred_element_type=F32)


def mm_nt(a, b):
    return lax.dot_general(a, b, (((1,), (1,)), ((), ())), preferred_element_type=F32)


def norm_parts(tensor):
    average = jnp.mean(tensor, -1, keepdims=True)
    centered = tensor - average
    spread = jnp.mean(centered * centered, -1, keepdims=True)
    scale = lax.rsqrt(spread + EPSILON)
    return centered * scale, scale


def norm_back(tensor, gain, grad):
    normed, scale = norm_parts(tensor)
    scaled = gain * grad
    product = grad * normed
    first = jnp.mean(scaled, -1, keepdims=True)
    second = jnp.mean(scaled * normed, -1, keepdims=True)
    out = (scaled - first - normed * second) * scale
    return out, jnp.sum(product, 0, keepdims=True), jnp.sum(grad, 0, keepdims=True)


def column_sum(tensor):
    return jnp.sum(tensor.astype(F32), 0, keepdims=True)


def gelu_pair(x):
    bell = jnp.exp(-0.5 * x * x)
    t = 1.0 / (1.0 + (0.3275911 / math.sqrt(2.0)) * jnp.abs(x))
    poly = t * (
        0.5 * 0.254829592
        + t
        * (
            0.5 * -0.284496736
            + t * (0.5 * 1.421413741 + t * (0.5 * -1.453152027 + t * (0.5 * 1.061405429)))
        )
    )
    tail = poly * bell
    cdf = jnp.where(x < 0, tail, 1.0 - tail)
    return x * cdf, cdf + x * bell * (1.0 / math.sqrt(2.0 * math.pi))


def row_blocks(count, body):
    step = min(256, count)

    def run(i, carry):
        body(pl.ds(pl.multiple_of(i * step, step), step))
        return carry

    lax.fori_loop(0, count // step, run, 0, unroll=True)


def head_halves(rows):
    lane = lax.broadcasted_iota(jnp.int32, (rows, PAIR), 1)
    return lane < HEAD_DIM, lane >= HEAD_DIM


def attend_forward(q_ref, k_ref, v_ref, bias_ref, mixed_ref, lse_ref):
    query_halves, key_halves = head_halves(q_ref.shape[0]), head_halves(k_ref.shape[0])

    def pair(p, carry):
        lanes = pl.ds(pl.multiple_of(p * PAIR, PAIR), PAIR)
        keys, values = k_ref[:, lanes], v_ref[:, lanes]
        queries = q_ref[:, lanes] * SCALE
        outs, peaks = [], []
        for a in range(2):
            own = jnp.where(query_halves[a], queries, jnp.zeros_like(queries))
            scores = mm_nt(own, keys) + bias_ref[...]
            peak = jnp.max(scores, 1, keepdims=True)
            weights = jnp.exp(scores - peak).astype(BF16)
            outs.append(mm(weights, jnp.where(key_halves[a], values, jnp.ones_like(values))))
            peaks.append(peak)
        first = query_halves[0]
        total = pltpu.roll(jnp.where(first, outs[1], outs[0]), HEAD_DIM, 1)
        lse_ref[p] = jnp.where(first, peaks[0], peaks[1]) + jnp.log(total)
        mixed_ref[:, lanes] = (jnp.where(first, outs[0], outs[1]) * (1.0 / total)).astype(BF16)
        return carry

    lax.fori_loop(0, HEADS // 2, pair, 0, unroll=2)


def attend_back(q_ref, k_ref, v_ref, grad_ref, mixed_ref, lse_ref, bias_ref, dq_ref, dkv_ref):
    length, width = q_ref.shape
    halves = head_halves(length)

    def pair(p, carry):
        lanes = pl.ds(pl.multiple_of(p * PAIR, PAIR), PAIR)
        value_lanes = pl.ds(pl.multiple_of(width + p * PAIR, PAIR), PAIR)
        keys, values = k_ref[:, lanes], v_ref[:, lanes]
        queries = q_ref[:, lanes] * SCALE
        grads = grad_ref[:, lanes]
        product = grads.astype(F32) * mixed_ref[:, lanes].astype(F32)
        queries_t, grads_t = queries.T, grads.T
        outs, key_grads, value_grads = [], [], []
        for a, half in enumerate(halves):
            own = jnp.where(half, queries, jnp.zeros_like(queries))
            own_grad = jnp.where(half, grads, jnp.zeros_like(grads))
            rows = slice(a * HEAD_DIM, (a + 1) * HEAD_DIM)
            lse = lse_ref[p, :, a * HEAD_DIM : a * HEAD_DIM + 1]
            delta = jnp.sum(jnp.where(half, product, 0.0), 1, keepdims=True)
            weights = jnp.exp(mm_nt(own, keys) + bias_ref[...] - lse)
            score_grad = (weights * (mm_nt(own_grad, values) - delta)).astype(BF16)
            outs.append(mm(score_grad, keys))
            key_grads.append(mm(queries_t[rows], score_grad))
            value_grads.append(mm(grads_t[rows], weights.astype(BF16)))
        dkv_ref[:, lanes] = jnp.concatenate(key_grads, 0).astype(BF16).T
        dkv_ref[:, value_lanes] = jnp.concatenate(value_grads, 0).astype(BF16).T
        dq_ref[:, lanes] = (jnp.where(halves[0], outs[0], outs[1]) * SCALE).astype(BF16)
        return carry

    lax.fori_loop(0, HEADS // 2, pair, 0, unroll=2)


def self_kernel(io, x_ref, w_qkv, w_mix, vec, bias, q_out, k_out, v_out, mixed, lse, summed, hidden, squares):
    length, width = q_out.shape
    io.ready(x_ref, w_qkv, vec)
    x_own = x_ref[0:length, :]
    q_out[...] = (mm(x_own, w_qkv[:, 0:width]) + vec[0:1, :]).astype(BF16)

    def keys(rows):
        x = x_ref[rows, :]
        k_out[rows, :] = mm(x, w_qkv[:, width : 2 * width]).astype(BF16)
        v_out[rows, :] = (mm(x, w_qkv[:, 2 * width : 3 * width]) + vec[1:2, :]).astype(BF16)

    row_blocks(x_ref.shape[0], keys)
    io.done(q_out, k_out, v_out)
    io.ready(bias)
    attend_forward(q_out, k_out, v_out, bias, mixed, lse)
    io.done(mixed, lse)
    io.ready(w_mix)
    branch = mm(mixed[...], w_mix[...]) + vec[2:3, :]
    total = x_own.astype(F32) + branch
    summed[...] = total
    squares[...] = jnp.zeros_like(squares)
    squares[0:1, :] = column_sum(total * total)
    squares[1:2, :] = column_sum(branch * branch)
    hidden[...] = norm_parts(total)[0] * vec[6:7, :] + vec[4:5, :]


def ffn_kernel(io, middle, vec, w_in, b_in, w_out, act, slope, final_sum, low_middle, result):
    width = middle.shape[1]
    chunks = w_in.shape[1] // width
    io.ready(middle, vec)
    mid = middle[...]
    low = mid.astype(BF16)
    low_middle[...] = low
    final_sum[...] = mid + vec[3:4, :]
    io.ready(w_in, b_in, w_out)

    def chunk(j, carry):
        columns = pl.ds(pl.multiple_of(j * width, width), width)
        inner = mm(low, w_in[:, columns]) + b_in[:, columns]
        value, derivative = gelu_pair(inner)
        value = value.astype(BF16)
        act[:, columns] = value
        slope[:, columns] = derivative.astype(BF16)
        final_sum[...] += mm(value, w_out[columns, :])
        return carry

    lax.fori_loop(0, chunks, chunk, 0, unroll=True)
    io.done(act, slope, low_middle, final_sum)
    result[...] = (norm_parts(final_sum[...])[0] * vec[7:8, :] + vec[5:6, :]).astype(BF16)


def ffn_norm_kernel(io, grad, final_sum, vec, dy, d_final, small):
    io.ready(grad, final_sum, vec)
    back, d_gain, d_shift = norm_back(final_sum[...], vec[7:8, :], grad[...].astype(F32))
    low = back.astype(BF16)
    dy[...] = low
    d_final[...] = back
    small[...] = jnp.zeros_like(small)
    small[0:1, :] = d_gain
    small[1:2, :] = d_shift
    small[2:3, :] = column_sum(low)


def ffn_rest_kernel(io, dy, d_final, small_in, w_out, slope, w_in, d_inner, d_middle, small):
    width = dy.shape[1]
    chunks = w_in.shape[1] // width
    io.ready(dy, d_final, small_in, w_out, slope, w_in)
    low = dy[...]
    small[...] = small_in[...]
    d_middle[...] = d_final[...]

    def chunk(j, carry):
        columns = pl.ds(pl.multiple_of(j * width, width), width)
        d_act = mm_nt(low, w_out[columns, :])
        inner = (d_act * slope[:, columns].astype(F32)).astype(BF16)
        d_inner[:, columns] = inner
        small[pl.ds(3 + j, 1), :] = column_sum(inner)
        d_middle[...] += mm_nt(inner, w_in[:, columns])
        return carry

    lax.fori_loop(0, chunks, chunk, 0, unroll=True)


def ffn_back_kernel(io, grad, final_sum, vec, w_out, slope, w_in, dy, d_inner, d_middle, small):
    ffn_norm_kernel(io, grad, final_sum, vec, dy, d_middle, small)
    io.done(dy)
    ffn_rest_kernel(io, dy, d_middle, small, w_out, slope, w_in, d_inner, d_middle, small)


def mask_kernel(micro, io, ids, far, *outs):
    io.ready(ids, far)
    length = ids.shape[1]
    section, me, blocks = lax.axis_index("section"), lax.axis_index("seq"), lax.axis_size("seq")
    orders = []
    for k in range(blocks // 2):
        chip = (me + 2 * k) % blocks
        orders += [chip, chip + 1 - 2 * (me % 2)]
    here = lax.broadcasted_iota(jnp.int32, (length, length), 0)
    there = lax.broadcasted_iota(jnp.int32, (length, length), 1)
    for m in range(micro):
        own = jnp.where(section == 0, ids[m : m + 1, :], ids[micro + m : micro + m + 1, :])
        query = jnp.broadcast_to(own.astype(F32), (PAIR, length)).T[:, 0:1]
        for j, order in enumerate(orders):
            block = ids if j == 0 else far.at[j]
            source, target = block[m : m + 1, :], block[micro + m : micro + m + 1, :]
            key = jnp.where(section == 0, source, target).astype(F32)
            late = (there + order * length > here + orders[0] * length) & (section == 1)
            columns = slice(j * length, (j + 1) * length)
            outs[m][:, columns] = jnp.where((query == key) & jnp.logical_not(late), 0.0, MASKED)
            outs[micro + m][:, columns] = jnp.where(query == source.astype(F32), 0.0, MASKED)


def cross_kernel(
    io, hidden, w_q, vec, memory, w_kv, bias, w_o,
    cq, ck, cv, mixed, lse, summed, middle, low_hidden,
):
    width = hidden.shape[1]
    io.ready(hidden, w_q, vec)
    low = hidden[...].astype(BF16)
    low_hidden[...] = low
    cq[...] = (mm(low, w_q[...]) + vec[0:1, :]).astype(BF16)
    io.ready(memory, w_kv)

    def keys(rows):
        mem = memory[rows, :]
        ck[rows, :] = mm(mem, w_kv[:, 0:width]).astype(BF16)
        cv[rows, :] = (mm(mem, w_kv[:, width : 2 * width]) + vec[1:2, :]).astype(BF16)

    row_blocks(memory.shape[0], keys)
    io.done(cq, ck, cv, low_hidden)
    io.ready(bias)
    attend_forward(cq, ck, cv, bias, mixed, lse)
    io.done(mixed, lse)
    io.ready(w_o)
    total = hidden[...] + mm(mixed[...], w_o[...]) + vec[2:3, :]
    summed[...] = total
    middle[...] = norm_parts(total)[0] * vec[4:5, :] + vec[3:4, :]


def cross_back_kernel(
    io, d_middle, summed, vec, w_o, mixed, cq, ck, bias, lse, cv, w_q, w_kv,
    dyc, dcq, dckv, d_hidden, keep, send, small, d_mixed,
):
    length, width = d_middle.shape
    io.ready(d_middle, summed, vec)
    d_cross, d_gain, d_shift = norm_back(summed[...], vec[4:5, :], d_middle[...])
    low = d_cross.astype(BF16)
    dyc[...] = low
    d_hidden[...] = d_cross
    io.ready(w_o, mixed)
    grads = mm_nt(low, w_o[...]).astype(BF16)
    d_mixed[...] = grads
    io.ready(cq, ck, bias, lse, cv)
    attend_back(cq, ck, cv, d_mixed, mixed, lse, bias, dcq, dckv)
    io.ready(w_q, w_kv)
    for block in range(dckv.shape[0] // length):
        target = keep if block % 2 == 0 else send
        rows = slice(block // 2 * length, (block // 2 + 1) * length)
        target[rows, :] = mm_nt(dckv[block * length : (block + 1) * length, :], w_kv[...]).astype(BF16)
    io.done(send, keep, dyc, dcq, dckv)
    d_hidden[...] += mm_nt(dcq[...], w_q[...])
    small[...] = jnp.zeros_like(small)
    small[0:1, :] = d_gain
    small[1:2, :] = d_shift
    small[2:3, :] = column_sum(low)
    small[3:4, :] = column_sum(dcq[...])
    small[4:5, :] = column_sum(dckv[:, width : 2 * width])


def self_back_kernel(
    io, grad, summed, vec, w_mix, mixed, q, k, bias, lse, v, w_qkv,
    dy, dq, dkv, own, keep, send, small, d_mixed,
):
    length, width = q.shape
    io.ready(grad, summed, vec)
    d_sum, d_gain, d_shift = norm_back(summed[...], vec[6:7, :], grad[...])
    low = d_sum.astype(BF16)
    dy[...] = low
    own[...] = d_sum
    io.ready(w_mix, mixed)
    grads = mm_nt(low, w_mix[...]).astype(BF16)
    d_mixed[...] = grads
    io.ready(q, k, bias, lse, v)
    attend_back(q, k, v, d_mixed, mixed, lse, bias, dq, dkv)
    io.done(dy, dq, dkv)
    io.ready(w_qkv)
    for block in range(dkv.shape[0] // length):
        part = mm_nt(dkv[block * length : (block + 1) * length, :], w_qkv[:, width : 3 * width])
        if block == 0:
            own[...] += part + mm_nt(dq[...], w_qkv[:, 0:width])
            continue
        target = keep if block % 2 == 0 else send
        at = (block - 2) // 2 if block % 2 == 0 else block // 2
        target[at * length : (at + 1) * length, :] = part.astype(BF16)
    io.done(send, keep, own)
    small[...] = jnp.zeros_like(small)
    small[0:1, :] = d_gain
    small[1:2, :] = d_shift
    small[2:3, :] = column_sum(low)
    small[3:4, :] = column_sum(dq[...])
    small[4:5, :] = column_sum(dkv[:, width : 2 * width])


def weight_kernel(plan, regroup, io, *refs):
    out = refs[-1] if regroup == 0 else refs[-2]
    wide_out = out if regroup == 0 else refs[-1]
    for lefts, rights, column in plan:
        inner = refs[lefts[0]].shape[1]
        cols = refs[rights[0]].shape[1]
        step = 256
        wide = min(cols, 1536)
        io.ready(*[refs[i] for i in lefts + rights])

        def tile(i, carry, lefts=lefts, rights=rights, column=column, cols=cols, wide=wide):
            rows = pl.ds(pl.multiple_of(i * step, step), step)
            turned = [refs[l][:, rows].T for l in lefts]
            for start in range(0, cols, wide):
                total = None
                for left, r in zip(turned, rights):
                    term = mm(left, refs[r][:, start : start + wide])
                    total = term if total is None else total + term
                wide_out[rows, column + start : column + start + wide] = total.astype(wide_out.dtype)
            return carry

        lax.fori_loop(0, inner // step, tile, 0, unroll=3)
    if regroup:
        half = out.shape[0] // 2

        def group(i, carry):
            first = wide_out[pl.ds(pl.multiple_of(i * regroup, regroup), regroup), :]
            second = wide_out[pl.ds(pl.multiple_of(half + i * regroup, regroup), regroup), :]
            rows = pl.ds(pl.multiple_of(2 * i * regroup, 2 * regroup), 2 * regroup)
            out[rows, :] = jnp.concatenate([first, second], 0).astype(BF16)
            return carry

        lax.fori_loop(0, half // regroup, group, 0)


def add_kernel(io, *refs):
    out = refs[-1]
    io.ready(*refs[:-1])
    total = refs[0][...].astype(F32)
    for ref in refs[1:-1]:
        total = total + ref[...].astype(F32)
    out[...] = total.astype(out.dtype)


def add_lead_kernel(io, one, many, out):
    io.ready(one, many)
    total = one[...].astype(F32)
    for i in range(many.shape[0]):
        total = total + many[i].astype(F32)
    out[...] = total.astype(out.dtype)


def small_kernel(micro, io, *refs):
    out = refs[-1]
    ins = refs[:-1]
    io.ready(*ins)
    selfs, ffns, squares, crosses = (ins[i * micro : (i + 1) * micro] for i in range(4))
    out[...] = jnp.zeros_like(out)
    for ref in selfs:
        out[0:8, :] += ref[...]
    for ref in squares:
        out[5:7, :] += ref[0:2, :]
    for ref in ffns:
        out[8:16, :] += ref[...]
    for ref in crosses:
        out[16:24, :] += jnp.where(lax.axis_index("section") == 1, ref[...], 0.0)


class Moves:
    def __init__(self, loads, stores):
        self.loads, self.stores = dict(loads), dict(stores)
        self.started, self.waited = set(), set()
        for copies in self.loads.values():
            for copy in copies:
                copy.start()

    def ready(self, *refs):
        for ref in refs:
            if id(ref) not in self.waited:
                self.waited.add(id(ref))
                for copy in self.loads.get(id(ref), ()):
                    copy.wait()

    def done(self, *refs):
        for ref in refs:
            if id(ref) not in self.started:
                self.started.add(id(ref))
                for copy in self.stores[id(ref)]:
                    copy.start()

    def finish(self, ins, outs):
        self.ready(*ins)
        self.done(*outs)
        for copies in self.stores.values():
            for copy in copies:
                copy.wait()


class Held:
    def __init__(self, ref):
        self.ref = ref


class Rows:
    def __init__(self, pieces, shape=None):
        self.pieces = list(pieces)
        rest = self.pieces[0].shape[1:] if shape is None else shape[1:]
        count = sum(p.shape[0] for p in self.pieces) if shape is None else shape[0]
        self.shape, self.dtype = (count, *rest), self.pieces[0].dtype


def as_rows(item):
    return item if isinstance(item, Rows) else Rows([item])


def step(kernel, operands, outs, scratch=()):
    operands = [o if isinstance(o, Held) else as_rows(o) for o in operands]
    moved = [o for o in operands if not isinstance(o, Held)]
    outs = [as_rows(o) for o in outs]
    n_load = sum(len(o.pieces) for o in moved)
    n_store = sum(len(o.pieces) for o in outs)

    def pairs(ref, rows):
        if len(rows.pieces) == 1:
            return [(rows.pieces[0], ref)]
        found, at = [], 0
        for piece in rows.pieces:
            found.append((piece, ref.at[pl.ds(at, piece.shape[0])]))
            at += piece.shape[0]
        return found

    def inner(*refs):
        n_in, n_out = len(moved), len(outs)
        vmem_in, vmem_out = refs[:n_in], refs[n_in : n_in + n_out]
        in_sem, out_sem = refs[n_in + n_out : n_in + n_out + 2]
        extra = refs[n_in + n_out + 2 :]
        loads, at = [], 0
        for ref, rows in zip(vmem_in, moved):
            copies = []
            for hbm, vmem in pairs(ref, rows):
                copies.append(pltpu.make_async_copy(hbm, vmem, in_sem.at[at]))
                at += 1
            loads.append((id(ref), copies))
        stores, at = [], 0
        for ref, rows in zip(vmem_out, outs):
            copies = []
            for hbm, vmem in pairs(ref, rows):
                copies.append(pltpu.make_async_copy(vmem, hbm, out_sem.at[at]))
                at += 1
            stores.append((id(ref), copies))
        moves = Moves(loads, stores)
        left = list(vmem_in)
        ins = [o.ref if isinstance(o, Held) else left.pop(0) for o in operands]
        kernel(moves, *ins, *vmem_out, *extra)
        moves.finish(vmem_in, vmem_out)

    pl.run_scoped(
        inner,
        *[pltpu.VMEM(o.shape, o.dtype) for o in moved],
        *[pltpu.VMEM(o.shape, o.dtype) for o in outs],
        pltpu.SemaphoreType.DMA((max(n_load, 1),)),
        pltpu.SemaphoreType.DMA((max(n_store, 1),)),
        *scratch,
    )


class N(enum.Enum):
    act = enum.auto()
    b_in = enum.auto()
    chip = enum.auto()
    chip_in = enum.auto()
    mid = enum.auto()
    d_final = enum.auto()
    norm_small = enum.auto()
    ids = enum.auto()
    ids_all = enum.auto()
    ck = enum.auto()
    core = enum.auto()
    core_in = enum.auto()
    core_sum = enum.auto()
    cotangent = enum.auto()
    cq = enum.auto()
    cross_bias = enum.auto()
    cross_half = enum.auto()
    cross_kv = enum.auto()
    cross_lse = enum.auto()
    cross_mixed = enum.auto()
    cross_out = enum.auto()
    cross_q = enum.auto()
    cross_small = enum.auto()
    cross_sum = enum.auto()
    cross_vec = enum.auto()
    cv = enum.auto()
    d_inner = enum.auto()
    d_memory = enum.auto()
    d_middle = enum.auto()
    dckv = enum.auto()
    dcq = enum.auto()
    dkv = enum.auto()
    dm = enum.auto()
    dm_chip = enum.auto()
    dm_chip_in = enum.auto()
    dm_core = enum.auto()
    dm_core_in = enum.auto()
    dm_keep = enum.auto()
    dm_send = enum.auto()
    dm_sum = enum.auto()
    dq = enum.auto()
    dx = enum.auto()
    dx_chip = enum.auto()
    dx_chip_in = enum.auto()
    dx_core = enum.auto()
    dx_core_in = enum.auto()
    dx_keep = enum.auto()
    dx_own = enum.auto()
    dx_rest = enum.auto()
    dx_send = enum.auto()
    dx_sum = enum.auto()
    dy = enum.auto()
    dy3 = enum.auto()
    dyc = enum.auto()
    ffn_small = enum.auto()
    final_sum = enum.auto()
    g_attn = enum.auto()
    g_cross = enum.auto()
    g_in = enum.auto()
    g_out = enum.auto()
    hidden = enum.auto()
    hop = enum.auto()
    i = enum.auto()
    input_grad = enum.auto()
    k = enum.auto()
    layer_out = enum.auto()
    low_hidden = enum.auto()
    low_middle = enum.auto()
    lse = enum.auto()
    m = enum.auto()
    memory = enum.auto()
    middle = enum.auto()
    mixed = enum.auto()
    out = enum.auto()
    q = enum.auto()
    row = enum.auto()
    row_in = enum.auto()
    self_bias = enum.auto()
    self_small = enum.auto()
    slope = enum.auto()
    small = enum.auto()
    small_chip = enum.auto()
    small_chip_in = enum.auto()
    small_chip_sum = enum.auto()
    small_core = enum.auto()
    small_core_in = enum.auto()
    small_core_sum = enum.auto()
    small_half = enum.auto()
    small_row = enum.auto()
    small_row_in = enum.auto()
    small_sum = enum.auto()
    squares = enum.auto()
    summed = enum.auto()
    v = enum.auto()
    vec = enum.auto()
    w_in = enum.auto()
    w_mix = enum.auto()
    w_out = enum.auto()
    w_qkv = enum.auto()
    x = enum.auto()
    x_all = enum.auto()


class Wires:
    def __init__(self, send_sem, recv_sem, names, buffers):
        self.send_sem, self.recv_sem, self.names = send_sem, recv_sem, names
        self.like = {(ref.shape, ref.dtype): ref for ref in buffers}
        self.section, self.dp, self.seq = (lax.axis_index(n) for n in ("section", "dp", "seq"))
        self.dp_size, self.seq_size = lax.axis_size("dp"), lax.axis_size("seq")
        self.chips = self.seq_size // 2
        self.core = self.seq % 2
        self.twin = {"seq": self.seq + 1 - 2 * self.core}
        self.across = {"section": 1 - self.section}
        self.open, self.role = [], None

    def chip(self, k):
        return {"seq": (self.seq + 2 * k) % self.seq_size}

    def row(self, k):
        return {"dp": (self.dp + k) % self.dp_size}

    def peers(self, across=True):
        found = [self.twin]
        found += [self.chip(k) for k in range(1, self.chips)]
        found += [self.row(k) for k in range(1, self.dp_size)] if across else []
        return found + ([self.across] if across else [])

    def barrier(self, across=True):
        semaphore = pltpu.get_barrier_semaphore()
        peers = self.peers(across)
        for peer in peers:
            pl.semaphore_signal(semaphore, inc=1, device_id=peer, device_id_type=pl.DeviceIdType.MESH)
        pl.semaphore_wait(semaphore, len(peers))

    def copy(self, name, source, target, device):
        at = self.names.index(name)
        return pltpu.make_async_remote_copy(
            src_ref=source,
            dst_ref=target,
            send_sem=self.send_sem.at[at],
            recv_sem=self.recv_sem.at[at],
            device_id=device,
            device_id_type=pl.DeviceIdType.MESH,
        )

    def start(self, name, moves, whole=None):
        for source, target, device in moves:
            self.copy(name, source, target, device).start()
        if whole is None:
            whole = moves[0][0]
        self.open.append((name, self.like.get((whole.shape, whole.dtype), whole), self.role))

    def arrived(self, name, target):
        self.copy(name, target, target, self.twin).wait_recv()

    def close(self):
        def wait(role):
            for name, whole, of in self.open:
                if of == role:
                    self.copy(name, whole, whole, self.twin).wait_send()

        wait(None)
        for role in (0, 1):
            if any(of == role for _, _, of in self.open):
                pl.when(self.section == role)(functools.partial(wait, role))

    def only(self, role):
        def run(body):
            def inner():
                self.role = role
                body()
                self.role = None

            pl.when(self.section == role)(inner)

        return run


def gather_start(wires, name, source, target):
    wires.start((name, N.core), [(source, target.at[1], wires.twin)])
    for k in range(1, wires.chips):
        wires.start((name, N.chip, k), [(source, target.at[2 * (wires.chips - k)], wires.chip(k))])


def gather_pass(wires, name, target):
    for k in range(1, wires.chips):
        wires.arrived((name, N.chip, k), target.at[2 * (wires.chips - k)])
        wires.start((name, N.hop, k), [(target.at[2 * (wires.chips - k)], target.at[2 * (wires.chips - k) + 1], wires.twin)])


def gather_end(wires, name, target):
    wires.arrived((name, N.core), target.at[1])
    for k in range(1, wires.chips):
        wires.arrived((name, N.hop, k), target.at[2 * (wires.chips - k) + 1])


def gather_names(name, chips):
    return [(name, N.core)] + [(name, part, k) for part in (N.chip, N.hop) for k in range(1, chips)]


class Sums:
    def __init__(self, wires, refs, key, unit, first, rows, dp_first):
        self.wires, self.key, self.dp_first = wires, key, dp_first
        self.full, self.out = refs[unit], refs[unit, N.out]
        self.first, self.rows, self.block_rows = first, rows, self.out.shape[0]
        self.core_in, self.core_sum = refs[key, N.core_in], refs[key, N.core_sum]
        self.chip_in, self.row_in, self.mid = refs[key, N.chip_in], refs[key, N.row_in], refs[key, N.mid]
        self.count, self.columns = self.core_in.shape[0], self.core_in.shape[2]

    def block(self, pair, core):
        at = (2 * pair + core) * self.block_rows + self.first
        return self.full.at[pl.ds(pl.multiple_of(at, 16), self.rows)]

    def core_start(self):
        w = self.wires
        moves = [(self.block(i, 1 - w.core), self.core_in.at[i], w.twin) for i in range(self.count)]
        w.start((self.key, N.core), moves, self.core_in)

    def core_add(self):
        w = self.wires
        w.arrived((self.key, N.core), self.core_in)
        own = Rows([self.block(i, w.core) for i in range(self.count)], (self.count * self.rows, self.columns))
        arrived = Rows([self.core_in.at[i] for i in range(self.count)], own.shape)
        sums = Rows([self.core_sum.at[i] for i in range(self.count)], own.shape)
        step(add_kernel, [own, arrived], [sums])
        if self.dp_first:
            moves = []
            for k in range(1, w.dp_size):
                source = self.core_sum.at[pl.ds((w.dp + k) % w.dp_size * w.chips, w.chips)]
                moves.append((source, self.row_in.at[k - 1], w.row(k)))
            w.start((self.key, N.row), moves, self.row_in)
            return
        for k in range(1, w.chips):
            there = (w.seq // 2 + k) % w.chips
            target = self.chip_in.at[k - 1]
            moves = [
                (self.core_sum.at[d * w.chips + there], target.at[d], w.chip(k)) for d in range(w.dp_size)
            ]
            w.start((self.key, N.chip, k), moves, target)

    def second_add(self):
        w = self.wires
        mine = w.seq // 2
        if self.dp_first:
            w.arrived((self.key, N.row), self.row_in)
            terms = [self.core_sum.at[pl.ds(w.dp * w.chips, w.chips)]]
            terms += [self.row_in.at[k] for k in range(w.dp_size - 1)]
            step(add_kernel, terms, [self.mid])
            for k in range(1, w.chips):
                source = self.mid.at[(mine + k) % w.chips]
                w.start((self.key, N.chip, k), [(source, self.chip_in.at[k - 1], w.chip(k))])
            return
        shape = (w.dp_size * self.rows, self.columns)
        terms = [Rows([self.core_sum.at[d * w.chips + mine] for d in range(w.dp_size)], shape)]
        for k in range(1, w.chips):
            w.arrived((self.key, N.chip, k), self.chip_in.at[k - 1])
            terms.append(Rows([self.chip_in.at[k - 1, d] for d in range(w.dp_size)], shape))
        step(add_kernel, terms, [Rows([self.mid.at[d] for d in range(w.dp_size)], shape)])
        moves = [
            (self.mid.at[(w.dp + k) % w.dp_size], self.row_in.at[k - 1], w.row(k)) for k in range(1, w.dp_size)
        ]
        w.start((self.key, N.row), moves, self.row_in)

    def third_add(self):
        w = self.wires
        out = self.out.at[pl.ds(self.first, self.rows)]
        if self.dp_first:
            for k in range(1, w.chips):
                w.arrived((self.key, N.chip, k), self.chip_in.at[k - 1])
            step(add_lead_kernel, [self.mid.at[w.seq // 2], self.chip_in], [out])
            return
        w.arrived((self.key, N.row), self.row_in)
        step(add_lead_kernel, [self.mid.at[w.dp], self.row_in], [out])


def sum_pieces(units, devices):
    pieces = []
    for unit, (rows, _) in units.items():
        rows //= devices
        if unit is N.g_out and rows // 2 % 16 == 0:
            pieces.append(((unit, 0), unit, 0, rows // 2, True))
            pieces.append(((unit, 1), unit, rows // 2, rows // 2, False))
        else:
            pieces.append(((unit, 0), unit, 0, rows, unit is N.g_out))
    return pieces


def sum_shapes(key, rows, columns, dp_first, dp_size, chips):
    far_chips, far_rows = max(chips - 1, 1), max(dp_size - 1, 1)
    block = (rows, columns)
    return {
        (key, N.core_in): shaped(dp_size * chips, *block, kind=BF16),
        (key, N.core_sum): shaped(dp_size * chips, *block, kind=BF16),
        (key, N.mid): shaped(chips if dp_first else dp_size, *block, kind=BF16),
        (key, N.chip_in): shaped(far_chips, *(block if dp_first else (dp_size, *block)), kind=BF16),
        (key, N.row_in): shaped(far_rows, *((chips, *block) if dp_first else block), kind=BF16),
    }


def sum_names(key, chips):
    return [(key, N.core), (key, N.row)] + [(key, N.chip, k) for k in range(1, chips)]


def final_body(count, n_in, *refs):
    n_out = 15
    ins, outs, refs = refs[:n_in], refs[n_in : n_in + n_out], refs[n_in + n_out :]
    held, refs = refs[:n_in], refs[n_in:]
    stats, bias_grad, gain_grad, hidden_grad, cross_grad, cross_gain_grad, in_sem, out_sem = refs
    layer_out, input_grad, attn, ffn_in, ffn_out, small, cross_small = held[:7]
    cross = held[7:]
    section = lax.axis_index("section")
    me = lax.axis_index("dp") * lax.axis_size("seq") + lax.axis_index("seq")
    devices = lax.axis_size("dp") * lax.axis_size("seq")
    width = small.shape[1]
    half = outs[6].shape[0]
    loads = [pltpu.make_async_copy(a, v, in_sem.at[i]) for i, (a, v) in enumerate(zip(ins, held))]
    for copy in [*loads[5:7], *loads[:5], *loads[7:]]:
        copy.start()
    moves = []

    def move(source, at):
        moves.append(pltpu.make_async_copy(source, outs[at], out_sem.at[at]))
        return moves[-1]

    loads[5].wait()
    loads[6].wait()

    def columns_of(rows, start, number):
        at = lax.broadcasted_iota(jnp.int32, (width, number), 0)
        column = lax.broadcasted_iota(jnp.int32, (width, number), 1)
        return jnp.dot(
            rows, (at == column + start).astype(F32), precision=lax.Precision.HIGHEST, preferred_element_type=F32
        )

    per, per_hidden = bias_grad.shape[1], hidden_grad.shape[1]
    mine = columns_of(small[...], me * per, per)
    for i, row in enumerate((3, 4, 2, 10, 1, 9)):
        bias_grad[i : i + 1, :] = mine[row : row + 1]
    for i, row in enumerate((0, 8)):
        gain_grad[i : i + 1, :] = mine[row : row + 1]
    place = me * per_hidden
    hidden_rows = columns_of(small[8:16, :], place % width, per_hidden)
    row = lax.broadcasted_iota(jnp.int32, hidden_rows.shape, 0)
    hidden_grad[...] = jnp.sum(jnp.where(row == 3 + place // width, hidden_rows, 0.0), 0, keepdims=True)
    rows = jnp.where(section == 0, cross_small[...], small[16:24, :])
    cross_rows = columns_of(rows, (section * devices + me) * half, half)
    for i, row in enumerate((3, 4, 2, 1)):
        cross_grad[i : i + 1, :] = cross_rows[row : row + 1]
    cross_gain_grad[...] = cross_rows[0:1]
    squares = jnp.sum(small[5:7, :], 1, keepdims=True)
    stats[...] = jnp.sqrt(jnp.concatenate([squares[0:1], squares[1:2]], 1) / count)
    for i, ref in enumerate((stats, bias_grad, gain_grad, hidden_grad, cross_grad, cross_gain_grad)):
        move(ref, 9 + i).start()
    for load, targets in zip(
        loads[:5],
        (
            [(layer_out, 0)],
            [(input_grad, 1)],
            [(attn.at[:, 0 : 3 * width], 2), (attn.at[:, 3 * width : 4 * width], 3)],
            [(ffn_in, 4)],
            [(ffn_out, 5)],
        ),
    ):
        load.wait()
        for source, at in targets:
            move(source, at).start()
    for load in loads[7:]:
        load.wait()
    if len(cross) == 2:
        cross[0][...] = jnp.where(section == 0, cross[0][...], cross[1][half : 2 * half, :])
    for i, (first, end) in enumerate([(0, width), (width, 3 * width), (3 * width, 4 * width)]):
        move(cross[0].at[:, first:end], 6 + i).start()
    for copy in moves:
        copy.wait()


def main_body(micro, pieces, in_names, out_names, wire_names, held_names, *refs):
    refs = list(refs)
    hbm = {n: refs.pop(0) for n in in_names + out_names}
    held_refs = {n: refs.pop(0) for n in held_names}
    send_sem, recv_sem, held_sem = refs
    wires = Wires(send_sem, recv_sem, wire_names, hbm.values())
    chips, dp_size = wires.chips, wires.dp_size
    length, width = hbm[N.x].shape[1:]
    hidden_units = hbm[N.w_in].shape[1]
    held_copies = {
        n: pltpu.make_async_copy(hbm[n], held_refs[n], held_sem.at[i]) for i, n in enumerate(held_names)
    }
    for copy in held_copies.values():
        copy.start()
    held = {n: Held(r) for n, r in held_refs.items()}
    vec, cross_vec = held[N.vec], held[N.cross_vec]
    ticks, last = range(micro), micro - 1
    back_scratch = (pltpu.VMEM((length, width), BF16),)

    def b(name, m):
        return hbm[(name, m)]

    def inputs(m):
        blocks = b(N.x_all, m)
        return Rows([hbm[N.x].at[m]] + [blocks.at[i] for i in range(1, wires.seq_size)])

    def memory(m):
        arrived = b(N.memory, m)
        return Rows([arrived.at[i] for i in range(wires.seq_size)])

    def self_forward(m):
        step(
            self_kernel,
            [inputs(m), held[N.w_qkv], held[N.w_mix], vec, b(N.self_bias, m)],
            [b(n, m) for n in (N.q, N.k, N.v, N.mixed, N.lse, N.summed, N.hidden, N.squares)],
        )

    def ffn_forward(m, middle):
        step(
            ffn_kernel,
            [b(middle, m), vec, held[N.w_in], held[N.b_in], held[N.w_out]],
            [b(n, m) for n in (N.act, N.slope, N.final_sum, N.low_middle)] + [hbm[N.layer_out].at[m]],
        )

    def ffn_back(m, grad):
        step(
            ffn_back_kernel,
            [grad, b(N.final_sum, m), vec, held[N.w_out], b(N.slope, m), held[N.w_in]],
            [b(n, m) for n in (N.dy3, N.d_inner, N.d_middle, N.ffn_small)],
        )

    def cross_forward(m):
        step(
            cross_kernel,
            [b(N.hidden, m), held[N.cross_q], cross_vec, memory(m), held[N.cross_kv], b(N.cross_bias, m), held[N.cross_out]],
            [b(n, m) for n in (N.cq, N.ck, N.cv, N.cross_mixed, N.cross_lse, N.cross_sum, N.middle, N.low_hidden)],
        )

    def cross_back(m):
        step(
            cross_back_kernel,
            [b(N.d_middle, m), b(N.cross_sum, m), cross_vec, held[N.cross_out], b(N.cross_mixed, m), b(N.cq, m), b(N.ck, m),
             b(N.cross_bias, m), b(N.cross_lse, m), b(N.cv, m), held[N.cross_q], held[N.cross_kv]],
            [b(n, m) for n in (N.dyc, N.dcq, N.dckv, N.d_middle, N.dm_keep, N.dm_send, N.cross_small)],
            back_scratch,
        )

    def self_back(m):
        step(
            self_back_kernel,
            [b(N.d_middle, m), b(N.summed, m), vec, held[N.w_mix], b(N.mixed, m), b(N.q, m), b(N.k, m), b(N.self_bias, m),
             b(N.lse, m), b(N.v, m), held[N.w_qkv]],
            [b(n, m) for n in (N.dy, N.dq, N.dkv, N.dx_own, N.dx_keep, N.dx_send, N.self_small)],
            back_scratch,
        )
        wires.start((N.dx_core, m), [(b(N.dx_send, m), b(N.dx_core_in, m), wires.twin)])

    def dx_core(m):
        wires.arrived((N.dx_core, m), b(N.dx_core_in, m))
        arrived, rest = b(N.dx_core_in, m), (chips - 1) * length
        step(add_kernel, [b(N.dx_own, m), arrived.at[0:length]], [b(N.dx_sum, m)])
        step(add_kernel, [b(N.dx_keep, m), arrived.at[pl.ds(length, rest)]], [b(N.dx_rest, m)])
        for k in range(1, chips):
            source = b(N.dx_rest, m).at[pl.ds((k - 1) * length, length)]
            wires.start((N.dx_chip, k, m), [(source, b(N.dx_chip_in, m).at[k - 1], wires.chip(k))])

    def dx_end(m):
        for k in range(1, chips):
            wires.arrived((N.dx_chip, k, m), b(N.dx_chip_in, m).at[k - 1])
        step(add_lead_kernel, [b(N.dx_sum, m), b(N.dx_chip_in, m)], [hbm[N.input_grad].at[m]])

    def dm_start(m):
        wires.start((N.dm_core, m), [(b(N.dm_send, m), b(N.dm_core_in, m), wires.twin)])

    def dm_core(m):
        wires.arrived((N.dm_core, m), b(N.dm_core_in, m))
        step(add_kernel, [b(N.dm_keep, m), b(N.dm_core_in, m)], [b(N.dm_sum, m)])
        for k in range(1, chips):
            source = b(N.dm_sum, m).at[pl.ds(k * length, length)]
            wires.start((N.dm_chip, k, m), [(source, b(N.dm_chip_in, m).at[k - 1], wires.chip(k))])

    def dm_chip(m):
        for k in range(1, chips):
            wires.arrived((N.dm_chip, k, m), b(N.dm_chip_in, m).at[k - 1])
        step(add_lead_kernel, [b(N.dm_sum, m).at[0:length], b(N.dm_chip_in, m)], [b(N.dm, m)])
        wires.start((N.dm, m), [(b(N.dm, m), b(N.d_memory, m), wires.across)])

    def memory_start(m):
        arrived = b(N.memory, m)
        wires.arrived((N.m, m), arrived.at[0])
        gather_start(wires, (N.m, m), arrived.at[0], arrived)

    def weights(products, out, regroup=0):
        operands, plan = [], []
        for lefts, rights, column in products:
            n, count = len(operands), len(lefts)
            operands += list(lefts) + list(rights)
            plan.append((tuple(range(n, n + count)), tuple(range(n + count, n + 2 * count)), column))
        scratch = (pltpu.VMEM(out.shape, F32),) if regroup else ()
        step(functools.partial(weight_kernel, plan, regroup), operands, [out], scratch)

    def all_b(name):
        return [b(name, m) for m in ticks]

    def cross_weights():
        regroup = width // 2 // (dp_size * wires.seq_size) if pieces else 0
        weights(
            [
                (all_b(N.low_hidden), all_b(N.dcq), 0),
                ([memory(m) for m in ticks], all_b(N.dckv), width),
                (all_b(N.cross_mixed), all_b(N.dyc), 3 * width),
            ],
            hbm[N.g_cross],
            regroup,
        )

    def out_weights():
        weights([(all_b(N.act), all_b(N.dy3), 0)], hbm[N.g_out])

    def in_weights():
        weights([(all_b(N.low_middle), all_b(N.d_inner), 0)], hbm[N.g_in])

    def attn_weights():
        weights(
            [
                ([hbm[N.x].at[m] for m in ticks], all_b(N.dq), 0),
                ([inputs(m) for m in ticks], all_b(N.dkv), width),
                (all_b(N.mixed), all_b(N.dy), 3 * width),
            ],
            hbm[N.g_attn],
        )

    units = {}
    for piece in pieces:
        units.setdefault(piece[1], []).append(Sums(wires, hbm, *piece))

    def stage(unit, which):
        for sums in units.get(unit, ()):
            which(sums)

    wires.barrier()
    gather_start(wires, N.i, hbm[N.ids], hbm[N.ids_all])
    gather_start(wires, (N.x, 0), hbm[N.x].at[0], b(N.x_all, 0))
    gather_pass(wires, N.i, hbm[N.ids_all])
    gather_end(wires, N.i, hbm[N.ids_all])
    step(
        functools.partial(mask_kernel, micro),
        [hbm[N.ids], hbm[N.ids_all]],
        all_b(N.self_bias) + all_b(N.cross_bias),
    )
    gather_pass(wires, (N.x, 0), b(N.x_all, 0))
    for m in range(1, micro):
        gather_start(wires, (N.x, m), hbm[N.x].at[m], b(N.x_all, m))
    for n in (N.vec, N.w_qkv, N.w_mix):
        held_copies[n].wait()
    gather_end(wires, (N.x, 0), b(N.x_all, 0))
    self_forward(0)
    for n in held_names:
        if n not in (N.vec, N.w_qkv, N.w_mix):
            held_copies[n].wait()
    for m in range(1, micro):
        gather_pass(wires, (N.x, m), b(N.x_all, m))

    @wires.only(0)
    def _():
        for m in ticks:
            ffn_forward(m, N.hidden)
            wires.start((N.m, m), [(hbm[N.layer_out].at[m], b(N.memory, m).at[0], wires.across)])
            if m < last:
                gather_end(wires, (N.x, m + 1), b(N.x_all, m + 1))
                self_forward(m + 1)
        for m in ticks:
            wires.arrived((N.dm, m), b(N.d_memory, m))
            if m < last:
                ffn_back(m, b(N.d_memory, m))
                self_back(m)
                dx_core(m)
        step(
            ffn_norm_kernel,
            [b(N.d_memory, last), b(N.final_sum, last), vec],
            [b(N.dy3, last), hbm[N.d_final], hbm[N.norm_small]],
        )

    @wires.only(1)
    def _():
        for m in range(1, micro):
            gather_end(wires, (N.x, m), b(N.x_all, m))
            self_forward(m)
        memory_start(0)
        gather_pass(wires, (N.m, 0), b(N.memory, 0))
        for m in ticks:
            gather_end(wires, (N.m, m), b(N.memory, m))
            cross_forward(m)
            if m < last:
                memory_start(m + 1)
            if m > 0:
                dm_core(m - 1)
            ffn_forward(m, N.middle)
            if m < last:
                gather_pass(wires, (N.m, m + 1), b(N.memory, m + 1))
            ffn_back(m, hbm[N.cotangent].at[m])
            if m > 0:
                dm_chip(m - 1)
            cross_back(m)
            dm_start(m)
        dm_core(last)
        cross_weights()
        dm_chip(last)
        stage(N.g_cross, Sums.core_start)

    out_weights()
    stage(N.g_out, Sums.core_start)

    @wires.only(0)
    def _():
        step(
            ffn_rest_kernel,
            [b(N.dy3, last), hbm[N.d_final], hbm[N.norm_small], held[N.w_out], b(N.slope, last), held[N.w_in]],
            [b(N.d_inner, last), b(N.d_middle, last), b(N.ffn_small, last)],
        )

    @wires.only(1)
    def _():
        stage(N.g_cross, Sums.core_add)

    stage(N.g_out, Sums.core_add)
    in_weights()
    stage(N.g_in, Sums.core_start)

    @wires.only(1)
    def _():
        for m in range(last):
            self_back(m)

    stage(N.g_in, Sums.core_add)

    @wires.only(1)
    def _():
        for m in range(last):
            dx_core(m)
        stage(N.g_cross, Sums.second_add)

    self_back(last)
    attn_weights()
    stage(N.g_attn, Sums.core_start)
    step(
        functools.partial(small_kernel, micro),
        all_b(N.self_small) + all_b(N.ffn_small) + all_b(N.squares) + all_b(N.cross_small),
        [hbm[N.small]],
    )
    wires.start(N.small_core, [(hbm[N.small], hbm[N.small_core_in], wires.twin)])
    stage(N.g_attn, Sums.core_add)
    stage(N.g_out, Sums.second_add)
    dx_core(last)
    wires.arrived(N.small_core, hbm[N.small_core_in])
    step(add_kernel, [hbm[N.small], hbm[N.small_core_in]], [hbm[N.small_core_sum]])
    for k in range(1, chips):
        wires.start((N.small_chip, k), [(hbm[N.small_core_sum], hbm[N.small_chip_in].at[k - 1], wires.chip(k))])

    @wires.only(1)
    def _():
        stage(N.g_cross, Sums.third_add)
        if pieces:
            half = width // 2 // (dp_size * wires.seq_size)
            wires.start(N.cross_half, [(hbm[N.g_cross, N.out].at[0:half], hbm[N.cross_half], wires.across)])

    stage(N.g_in, Sums.second_add)
    for k in range(1, chips):
        wires.arrived((N.small_chip, k), hbm[N.small_chip_in].at[k - 1])
    step(add_lead_kernel, [hbm[N.small_core_sum], hbm[N.small_chip_in]], [hbm[N.small_chip_sum]])
    moves = [(hbm[N.small_chip_sum], hbm[N.small_row_in].at[k - 1], wires.row(k)) for k in range(1, dp_size)]
    wires.start(N.small_row, moves, hbm[N.small_row_in])
    for m in range(last):
        dx_end(m)
    stage(N.g_out, Sums.third_add)
    stage(N.g_attn, Sums.second_add)
    dx_end(last)
    wires.arrived(N.small_row, hbm[N.small_row_in])
    step(add_lead_kernel, [hbm[N.small_chip_sum], hbm[N.small_row_in]], [hbm[N.small_sum]])

    @wires.only(1)
    def _():
        wires.start(N.small_half, [(hbm[N.small_sum].at[16:24], hbm[N.small_half], wires.across)])

    stage(N.g_in, Sums.third_add)
    stage(N.g_attn, Sums.third_add)

    @wires.only(0)
    def _():
        wires.arrived(N.small_half, hbm[N.small_half])
        if pieces:
            wires.arrived(N.cross_half, hbm[N.cross_half])

    wires.close()


def shaped(*shape, kind=F32):
    return jax.ShapeDtypeStruct(shape, kind)


def pick(stacked, position):
    return lax.dynamic_index_in_dim(stacked, position, 0, keepdims=False)


def section_permute(x, axis, pairs, only):
    if only is None:
        return lax.ppermute(x, axis, pairs)
    first = only * lax.axis_size(axis)
    return lax.ppermute(x, ("section", axis), [(first + i, first + j) for i, j in pairs])


def group_permute(x, axis, members, stride, step, only=None):
    pairs = []
    for i in range(lax.axis_size(axis)):
        at = (i // stride) % members
        pairs.append((i, i + ((at + step) % members - at) * stride))
    return section_permute(x, axis, pairs, only)


def place_in(axis, members, stride):
    return (lax.axis_index(axis) // stride) % members


class Scatter:
    def __init__(self, parts, only=None):
        self.dp, self.chips = lax.axis_size("dp"), lax.axis_size("seq") // 2
        self.only, self.kind = only, parts.dtype
        self.parts = jnp.moveaxis(parts, 2, 0)
        self.stages = [("seq", 2, 1), ("seq", self.chips, 2), ("dp", self.dp, 1)]

    def send(self):
        axis, members, stride = self.stages[0]
        mine = place_in(axis, members, stride)
        self.keep = pick(self.parts, mine)
        return [pick(self.parts, (mine + step) % members) for step in range(1, members)]

    def arrive(self, sent):
        axis, members, stride = self.stages.pop(0)
        total = self.keep.astype(F32)
        for step in range(1, members):
            total = total + group_permute(sent[step - 1], axis, members, stride, step, self.only).astype(F32)
        if not self.stages:
            return total
        total = total.astype(self.kind)
        self.parts = jnp.moveaxis(total, 1, 0) if len(self.stages) == 2 else total
        return None

    def finish(self, sent=None):
        while self.stages:
            total = self.arrive(self.send() if sent is None else sent)
            sent = None
        return total


def by_device(total):
    dp_size, seq_size = lax.axis_size("dp"), lax.axis_size("seq")
    return total.reshape(dp_size, seq_size // 2, 2, total.shape[0] // (dp_size * seq_size), *total.shape[1:])


def to_encoder_half(total, section):
    half = total.shape[0] // 2
    arrived = lax.ppermute(total[:half], "section", [(1, 0)])
    return jnp.where(section == 0, arrived, total[half:])


def kernel_call(body, outs, operands, scratch, collective_id, flops, name):
    anywhere = pl.BlockSpec(memory_space=pltpu.HBM)
    size = sum(math.prod(o.shape) * o.dtype.itemsize for o in list(outs) + list(operands))
    return pl.pallas_call(
        body,
        out_shape=list(outs),
        in_specs=[anywhere] * len(operands),
        out_specs=[anywhere] * len(outs),
        scratch_shapes=scratch,
        cost_estimate=pl.CostEstimate(flops=int(flops), bytes_accessed=int(size), transcendentals=0),
        compiler_params=pltpu.CompilerParams(
            vmem_limit_bytes=VMEM_LIMIT, collective_id=collective_id, has_side_effects=True
        ),
        name=name,
    )(*operands)


def per_device(
    x_in, segments, cotangent, attn_in, attn_out, attn_bias, gains, ffn_in, ffn_bias, ffn_out,
    cross_q, cross_kv, cross_out, cross_bias, cross_gain,
):
    section = lax.axis_index("section")
    micro, length, width = x_in.shape[1], x_in.shape[3], x_in.shape[4]
    dp_size, seq_size = lax.axis_size("dp"), lax.axis_size("seq")
    chips = seq_size // 2
    devices = dp_size * seq_size
    tokens = length * seq_size
    hidden_units = ffn_in.shape[2]
    fused = width // devices % 16 == 0
    ticks = range(micro)
    x = x_in[0, :, 0]
    vec = jnp.concatenate([attn_bias[0], gains[0]], 0)
    cross_vec = jnp.concatenate([cross_bias, cross_gain[None], jnp.zeros((3, width), F32)], 0)

    ids = segments[:, :, 0].reshape(2 * micro, length)
    ids = jnp.concatenate([ids, jnp.zeros((-2 * micro % 8, length), ids.dtype)], 0)
    arrays = {
        N.x: x,
        N.ids: ids,
        N.cotangent: cotangent[:, 0],
        N.w_qkv: attn_in[0],
        N.w_mix: attn_out[0],
        N.w_in: ffn_in[0],
        N.w_out: ffn_out[0],
        N.b_in: ffn_bias,
        N.vec: vec,
        N.cross_q: cross_q,
        N.cross_kv: cross_kv,
        N.cross_out: cross_out,
        N.cross_vec: cross_vec,
    }
    lw, lw_low = shaped(length, width), shaped(length, width, kind=BF16)
    tw_low = shaped(tokens, width, kind=BF16)
    lh_low = shaped(length, hidden_units, kind=BF16)
    pair_low = shaped(tokens, 2 * width, kind=BF16)
    half_low = shaped(tokens // 2, width, kind=BF16)
    rest_low = shaped(max(tokens // 2 - length, length), width, kind=BF16)
    far_low = shaped(max(chips - 1, 1), length, width, kind=BF16)
    seq_low = shaped(seq_size, length, width, kind=BF16)
    mask = shaped(length, tokens)
    lse_shape, few = shaped(HEADS // 2, length, PAIR), shaped(8, width)
    kinds = {
        N.q: lw_low, N.k: tw_low, N.v: tw_low, N.mixed: lw_low, N.lse: lse_shape, N.summed: lw, N.hidden: lw, N.squares: few,
        N.act: lh_low, N.slope: lh_low, N.final_sum: lw, N.low_middle: lw_low,
        N.dy3: lw_low, N.d_inner: lh_low, N.d_middle: lw, N.ffn_small: few,
        N.cq: lw_low, N.ck: tw_low, N.cv: tw_low, N.cross_mixed: lw_low, N.cross_lse: lse_shape, N.cross_sum: lw,
        N.middle: lw, N.low_hidden: lw_low,
        N.dyc: lw_low, N.dcq: lw_low, N.dckv: pair_low, N.dm_keep: half_low, N.dm_send: half_low,
        N.cross_small: few, N.dm_core_in: half_low, N.dm_sum: half_low, N.dm_chip_in: far_low, N.dm: lw_low, N.d_memory: lw_low,
        N.dy: lw_low, N.dq: lw_low, N.dkv: pair_low, N.dx_own: lw, N.dx_keep: rest_low, N.dx_send: half_low, N.self_small: few,
        N.dx_core_in: half_low, N.dx_sum: lw, N.dx_rest: rest_low, N.dx_chip_in: far_low,
        N.x_all: seq_low, N.memory: seq_low, N.self_bias: mask, N.cross_bias: mask,
    }
    outs = {(n, m): kind for m in ticks for n, kind in kinds.items()}
    for n in (N.layer_out, N.input_grad):
        outs[n] = shaped(micro, length, width, kind=BF16)
    outs[N.ids_all] = shaped(seq_size, *ids.shape, kind=ids.dtype)
    outs[N.d_final], outs[N.norm_small] = lw, few
    small_shape = shaped(24, width)
    for n in (N.small, N.small_core_in, N.small_core_sum, N.small_chip_sum, N.small_sum):
        outs[n] = small_shape
    outs[N.small_chip_in] = shaped(max(chips - 1, 1), 24, width)
    outs[N.small_row_in] = shaped(max(dp_size - 1, 1), 24, width)
    outs[N.small_half] = few
    totals = {
        N.g_cross: (width, 4 * width), N.g_out: (hidden_units, width), N.g_in: (width, hidden_units), N.g_attn: (width, 4 * width),
    }
    wire_names = [N.small_core, N.small_row, N.small_half] + [(N.small_chip, k) for k in range(1, chips)]
    for m in ticks:
        wire_names += gather_names((N.m, m), chips) + gather_names((N.x, m), chips)
        wire_names += [(N.m, m), (N.dm, m), (N.dm_core, m), (N.dx_core, m)]
        wire_names += [(n, k, m) for n in (N.dm_chip, N.dx_chip) for k in range(1, chips)]
    pieces = sum_pieces(totals, devices) if fused else []
    for n, total in totals.items():
        outs[n] = shaped(*total, kind=BF16)
        if fused:
            outs[n, N.out] = shaped(total[0] // devices, total[1])
    for key, n, _, rows, dp_first in pieces:
        outs.update(sum_shapes(key, rows, totals[n][1], dp_first, dp_size, chips))
        wire_names += sum_names(key, chips)
    if fused:
        outs[N.cross_half] = shaped(width // 2 // devices, 4 * width)
        wire_names.append(N.cross_half)
    wire_names += gather_names(N.i, chips)
    held_names = [N.vec, N.w_qkv, N.w_mix, N.w_in, N.b_in, N.w_out, N.cross_vec, N.cross_q, N.cross_kv, N.cross_out]
    scratch = [pltpu.VMEM(arrays[n].shape, arrays[n].dtype) for n in held_names]
    scratch += [pltpu.SemaphoreType.DMA((len(wire_names),))] * 2 + [pltpu.SemaphoreType.DMA((len(held_names),))]
    results = kernel_call(
        functools.partial(main_body, micro, pieces, list(arrays), list(outs), wire_names, held_names),
        list(outs.values()),
        list(arrays.values()),
        scratch,
        0,
        6 * micro * length * width * (12 * width + 2 * hidden_units),
        "layers",
    )
    results = dict(zip(outs, results))

    if fused:
        cross_part = None
        attn_part, ffn_in_part, ffn_out_part = (results[n, N.out] for n in (N.g_attn, N.g_in, N.g_out))
        cross_parts = [results[N.cross_half], results[N.g_cross, N.out]]
    else:
        halves = results[N.g_cross].reshape(2, width // 2, 4 * width)
        halves = jnp.stack([by_device(halves[0]), by_device(halves[1])], 3)
        cross_part = Scatter(halves, 1).finish()
        cross_part = jnp.where(
            section == 0, lax.ppermute(cross_part[0], "section", [(1, 0)]), cross_part[1]
        )
        attn_part, ffn_in_part, ffn_out_part = (
            Scatter(by_device(results[n])).finish() for n in (N.g_attn, N.g_in, N.g_out)
        )
        cross_parts = [cross_part]
    per, half, per_hidden = width // devices, width // 2 // devices, hidden_units // devices
    operands = [
        results[N.layer_out], results[N.input_grad], attn_part, ffn_in_part, ffn_out_part,
        results[N.small_sum], results[N.small_half], *cross_parts,
    ]
    final_shapes = [
        shaped(micro, length, width, kind=BF16),
        shaped(micro, length, width, kind=BF16),
        shaped(per, 3 * width),
        shaped(per, width),
        shaped(per, hidden_units),
        shaped(per_hidden, width),
        shaped(half, width),
        shaped(half, 2 * width),
        shaped(half, width),
        shaped(1, 2),
        shaped(6, per),
        shaped(2, per),
        shaped(1, per_hidden),
        shaped(4, half),
        shaped(1, half),
    ]
    anywhere = pl.BlockSpec(memory_space=pltpu.HBM)
    finals = pl.pallas_call(
        functools.partial(final_body, micro * dp_size * tokens * width, len(operands)),
        out_shape=final_shapes,
        in_specs=[anywhere] * len(operands),
        out_specs=[anywhere] * len(final_shapes),
        scratch_shapes=[pltpu.VMEM(o.shape, o.dtype) for o in operands + final_shapes[9:]]
        + [pltpu.SemaphoreType.DMA((len(operands),)), pltpu.SemaphoreType.DMA((len(final_shapes),))],
    )(*operands)
    (layer_out, input_grad, attn_in_grad, attn_out_grad, ffn_in_grad, ffn_out_grad, cross_q_grad, cross_kv_grad,
     cross_out_grad, stats, attn_bias_grad, gains_grad, ffn_bias_grad, cross_bias_grad, cross_gain_grad) = finals
    return (
        layer_out[None, :, None],
        input_grad[None, :, None],
        stats,
        attn_in_grad[None],
        attn_out_grad[None],
        attn_bias_grad[None],
        gains_grad[None],
        ffn_in_grad[None],
        ffn_bias_grad,
        ffn_out_grad[None],
        cross_q_grad,
        cross_kv_grad,
        cross_out_grad,
        cross_bias_grad,
        cross_gain_grad[0],
    )


def solution(mesh):
    return jax.shard_map(
        per_device,
        mesh=mesh,
        in_specs=(
            P("section", None, "dp", "seq", None),
            P(None, None, "dp", "seq"),
            P(None, "dp", "seq", None),
            P("section", None, None),
            P("section", None, None),
            P("section", None, None),
            P("section", None, None),
            P("section", None, None),
            P("section", None),
            P("section", None, None),
            P(),
            P(),
            P(),
            P(),
            P(),
        ),
        out_specs=(
            P("section", None, "dp", "seq", None),
            P("section", None, "dp", "seq", None),
            P("section", None),
            P("section", ("dp", "seq"), None),
            P("section", ("dp", "seq"), None),
            P("section", None, ("dp", "seq")),
            P("section", None, ("dp", "seq")),
            P("section", ("dp", "seq"), None),
            P("section", ("dp", "seq")),
            P("section", ("dp", "seq"), None),
            P(("section", "dp", "seq"), None),
            P(("section", "dp", "seq"), None),
            P(("section", "dp", "seq"), None),
            P(None, ("section", "dp", "seq")),
            P(("section", "dp", "seq")),
        ),
        check_vma=False,
    )
```

time: 625 us -> 369 us (0.59)
  the two profiles are of different devices: /device:TPU:2 before, /device:TPU:8 now
where the time goes in v3:
time: 369 us; the launch traced here: 363 us
  Pallas kernels  357 us (97%)
    pallas_call x1, Pallas kernels, kernel_call(): pl.pallas_call(body, out_shape=list(outs), in_specs=[anywhere] * len(oper...  353 us

profile of v3, /device:TPU:8, one launch (start us, length us, event | category | flops | bytes accessed | tf_op | source)
XLA Modules:
  0.0 363.4 jit_solution(15433033004023682176)
XLA Ops:
  0.7 0.1 pad.3.clone
  0.7 0.7 broadcast_in_dim.31
  1.4 0.7 reduce
  2.1 0.6 concatenate.9.refs_1_
  2.8 0.7 copy.36
  3.5 1.4 pad_maximum_fusion
  4.9 353.2 %layers.1 = (bf16[256,768]{1,0:T(8,128)(2,1)}, bf16[1024,768]{1,0:T(8,128)(2,1)}, bf16[1024,768]{1,0:T(8,128)(2,1)}, bf16[256,768]{1,0:T(8,128)(2,1)}, f32[6,256...) custom-call(bf16[2,256,768]{2,1,0:T(8,128)(2,1)} %bitcast.30, ...), custom_call_target="tpu_custom_call" | custom-call | flops 36238786560 | bytes 160526336 | tf_op jit(solution)/shard_map/layers/pallas_call | solution.py:1275
  358.1 3.8 %shard_map.262 = (bf16[2,256,768]{2,1,0:T(8,128)(2,1)}, bf16[2,256,768]{2,1,0:T(8,128)(2,1)}, f32[48,2304]{1,0:T(8,128)}, f32[48,768]{1,0:T(8,128)}, f32[48,3072...) custom-call(bf16[2,256,768]{2,1,0:T(8,128)(2,1)} %get-tuple-element., ...), custom_call_target="tpu_custom_call" | custom-call | tf_op jit(solution)/shard_map/pallas_call | solution.py:1428
  361.9 1.3 copy.32
  (2 shorter events, 0.0 us)

commit v4 on v3

--- a/solution.py
+++ b/solution.py
@@ -299,6 +299,7 @@
         target[rows, :] = mm_nt(dckv[block * length : (block + 1) * length, :], w_kv[...]).astype(BF16)
     io.done(send, keep, dyc, dcq, dckv)
     d_hidden[...] += mm_nt(dcq[...], w_q[...])
+    io.sent(send)
     small[...] = jnp.zeros_like(small)
     small[0:1, :] = d_gain
     small[1:2, :] = d_shift
@@ -333,6 +334,7 @@
         at = (block - 2) // 2 if block % 2 == 0 else block // 2
         target[at * length : (at + 1) * length, :] = part.astype(BF16)
     io.done(send, keep, own)
+    io.sent(send)
     small[...] = jnp.zeros_like(small)
     small[0:1, :] = d_gain
     small[1:2, :] = d_shift
@@ -383,6 +385,7 @@
     for ref in refs[1:-1]:
         total = total + ref[...].astype(F32)
     out[...] = total.astype(out.dtype)
+    io.sent(out)
 
 
 def add_lead_kernel(io, one, many, out):
@@ -411,32 +414,44 @@
 
 class Moves:
     def __init__(self, loads, stores):
-        self.loads, self.stores = dict(loads), dict(stores)
-        self.started, self.waited = set(), set()
+        self.loads, self.stores, self.hook = dict(loads), dict(stores), None
+        self.started, self.loaded, self.stored = set(), set(), set()
         for copies in self.loads.values():
             for copy in copies:
                 copy.start()
 
     def ready(self, *refs):
         for ref in refs:
-            if id(ref) not in self.waited:
-                self.waited.add(id(ref))
+            if id(ref) not in self.loaded:
+                self.loaded.add(id(ref))
                 for copy in self.loads.get(id(ref), ()):
                     copy.wait()
+
+    def away(self, ref):
+        self.done(ref)
+        if id(ref) not in self.stored:
+            self.stored.add(id(ref))
+            for copy in self.stores.get(id(ref), ()):
+                copy.wait()
 
     def done(self, *refs):
         for ref in refs:
             if id(ref) not in self.started:
                 self.started.add(id(ref))
-                for copy in self.stores[id(ref)]:
+                for copy in self.stores.get(id(ref), ()):
                     copy.start()
+
+    def sent(self, ref):
+        self.done(ref)
+        if self.hook is not None:
+            self.away(ref)
+            self.hook()
 
     def finish(self, ins, outs):
         self.ready(*ins)
         self.done(*outs)
-        for copies in self.stores.values():
-            for copy in copies:
-                copy.wait()
+        for ref in outs:
+            self.away(ref)
 
 
 class Held:
@@ -457,11 +472,37 @@
 
 
 def step(kernel, operands, outs, scratch=()):
-    operands = [o if isinstance(o, Held) else as_rows(o) for o in operands]
-    moved = [o for o in operands if not isinstance(o, Held)]
-    outs = [as_rows(o) for o in outs]
-    n_load = sum(len(o.pieces) for o in moved)
-    n_store = sum(len(o.pieces) for o in outs)
+    group((kernel, operands, outs, scratch))
+
+
+def group(*parts):
+    made, loads, load_at, outs, owner, scratches, plans = {}, [], {}, [], {}, [], []
+    for part in parts:
+        if callable(part):
+            plans.append(part)
+            continue
+        kernel, operands, results, scratch, hook = (*part, None)[:5]
+        ins = []
+        for o in operands:
+            if isinstance(o, Held):
+                ins.append((0, o.ref))
+            elif id(o) in made:
+                ins.append((2, made[id(o)]))
+            else:
+                if id(o) not in load_at:
+                    load_at[id(o)] = len(loads)
+                    loads.append(as_rows(o))
+                ins.append((1, load_at[id(o)]))
+        first = len(outs)
+        for o in results:
+            made[id(o)] = owner[id(o)] = len(outs)
+            outs.append(o)
+        plans.append((kernel, ins, range(first, len(outs)), range(len(scratches), len(scratches) + len(scratch)), hook))
+        scratches += list(scratch)
+    stored = [owner[id(o)] == i for i, o in enumerate(outs)]
+    rows_out = [as_rows(o) for o in outs]
+    n_load = sum(len(o.pieces) for o in loads)
+    n_store = sum(len(o.pieces) for o in rows_out)
 
     def pairs(ref, rows):
         if len(rows.pieces) == 1:
@@ -473,37 +514,42 @@
         return found
 
     def inner(*refs):
-        n_in, n_out = len(moved), len(outs)
+        n_in, n_out = len(loads), len(outs)
         vmem_in, vmem_out = refs[:n_in], refs[n_in : n_in + n_out]
         in_sem, out_sem = refs[n_in + n_out : n_in + n_out + 2]
         extra = refs[n_in + n_out + 2 :]
-        loads, at = [], 0
-        for ref, rows in zip(vmem_in, moved):
+        coming, at = [], 0
+        for ref, rows in zip(vmem_in, loads):
             copies = []
             for hbm, vmem in pairs(ref, rows):
                 copies.append(pltpu.make_async_copy(hbm, vmem, in_sem.at[at]))
                 at += 1
-            loads.append((id(ref), copies))
-        stores, at = [], 0
-        for ref, rows in zip(vmem_out, outs):
+            coming.append((id(ref), copies))
+        going, at = [], 0
+        for ref, rows, store in zip(vmem_out, rows_out, stored):
             copies = []
-            for hbm, vmem in pairs(ref, rows):
+            for hbm, vmem in pairs(ref, rows) if store else ():
                 copies.append(pltpu.make_async_copy(vmem, hbm, out_sem.at[at]))
                 at += 1
-            stores.append((id(ref), copies))
-        moves = Moves(loads, stores)
-        left = list(vmem_in)
-        ins = [o.ref if isinstance(o, Held) else left.pop(0) for o in operands]
-        kernel(moves, *ins, *vmem_out, *extra)
+            going.append((id(ref), copies))
+        moves = Moves(coming, going)
+        for plan in plans:
+            if callable(plan):
+                plan()
+                continue
+            kernel, ins, results, scratch, moves.hook = plan
+            given = [(None, vmem_in, vmem_out)[kind][at] if kind else at for kind, at in ins]
+            kernel(moves, *given, *[vmem_out[i] for i in results], *[extra[i] for i in scratch])
+            moves.done(*[vmem_out[i] for i in results])
         moves.finish(vmem_in, vmem_out)
 
     pl.run_scoped(
         inner,
-        *[pltpu.VMEM(o.shape, o.dtype) for o in moved],
-        *[pltpu.VMEM(o.shape, o.dtype) for o in outs],
+        *[pltpu.VMEM(o.shape, o.dtype) for o in loads],
+        *[pltpu.VMEM(o.shape, o.dtype) for o in rows_out],
         pltpu.SemaphoreType.DMA((max(n_load, 1),)),
         pltpu.SemaphoreType.DMA((max(n_store, 1),)),
-        *scratch,
+        *scratches,
     )
 
 
@@ -515,6 +561,7 @@
     mid = enum.auto()
     d_final = enum.auto()
     norm_small = enum.auto()
+    part = enum.auto()
     ids = enum.auto()
     ids_all = enum.auto()
     ck = enum.auto()
@@ -532,7 +579,6 @@
     cross_q = enum.auto()
     cross_small = enum.auto()
     cross_sum = enum.auto()
-    cross_vec = enum.auto()
     cv = enum.auto()
     d_inner = enum.auto()
     d_memory = enum.auto()
@@ -602,7 +648,10 @@
     squares = enum.auto()
     summed = enum.auto()
     v = enum.auto()
-    vec = enum.auto()
+    bias = enum.auto()
+    gain = enum.auto()
+    cross_shift = enum.auto()
+    cross_scale = enum.auto()
     w_in = enum.auto()
     w_mix = enum.auto()
     w_out = enum.auto()
@@ -686,22 +735,27 @@
         return run
 
 
-def gather_start(wires, name, source, target):
-    wires.start((name, N.core), [(source, target.at[1], wires.twin)])
+def whole_block(target, i):
+    return target.at[i]
+
+
+def gather_start(wires, name, source, target, block=whole_block):
+    wires.start((name, N.core), [(source, block(target, 1), wires.twin)])
     for k in range(1, wires.chips):
-        wires.start((name, N.chip, k), [(source, target.at[2 * (wires.chips - k)], wires.chip(k))])
-
-
-def gather_pass(wires, name, target):
+        wires.start((name, N.chip, k), [(source, block(target, 2 * (wires.chips - k)), wires.chip(k))])
+
+
+def gather_pass(wires, name, target, block=whole_block):
     for k in range(1, wires.chips):
-        wires.arrived((name, N.chip, k), target.at[2 * (wires.chips - k)])
-        wires.start((name, N.hop, k), [(target.at[2 * (wires.chips - k)], target.at[2 * (wires.chips - k) + 1], wires.twin)])
-
-
-def gather_end(wires, name, target):
-    wires.arrived((name, N.core), target.at[1])
+        at = 2 * (wires.chips - k)
+        wires.arrived((name, N.chip, k), block(target, at))
+        wires.start((name, N.hop, k), [(block(target, at), block(target, at + 1), wires.twin)])
+
+
+def gather_end(wires, name, target, block=whole_block):
+    wires.arrived((name, N.core), block(target, 1))
     for k in range(1, wires.chips):
-        wires.arrived((name, N.hop, k), target.at[2 * (wires.chips - k) + 1])
+        wires.arrived((name, N.hop, k), block(target, 2 * (wires.chips - k) + 1))
 
 
 def gather_names(name, chips):
@@ -732,7 +786,10 @@
         own = Rows([self.block(i, w.core) for i in range(self.count)], (self.count * self.rows, self.columns))
         arrived = Rows([self.core_in.at[i] for i in range(self.count)], own.shape)
         sums = Rows([self.core_sum.at[i] for i in range(self.count)], own.shape)
-        step(add_kernel, [own, arrived], [sums])
+        return (add_kernel, [own, arrived], [sums], (), self.core_sent)
+
+    def core_sent(self):
+        w = self.wires
         if self.dp_first:
             moves = []
             for k in range(1, w.dp_size):
@@ -787,11 +844,12 @@
     pieces = []
     for unit, (rows, _) in units.items():
         rows //= devices
-        if unit is N.g_out and rows // 2 % 16 == 0:
-            pieces.append(((unit, 0), unit, 0, rows // 2, True))
-            pieces.append(((unit, 1), unit, rows // 2, rows // 2, False))
-        else:
-            pieces.append(((unit, 0), unit, 0, rows, unit is N.g_out))
+        parts = 2 if unit is N.g_out else 3 if unit is N.g_attn else 1
+        if rows // parts % 16:
+            parts = 1
+        for i in range(parts):
+            dp_first = i == 0 and unit is N.g_out
+            pieces.append(((unit, i), unit, i * (rows // parts), rows // parts, dp_first))
     return pieces
 
 
@@ -803,6 +861,7 @@
         (key, N.core_sum): shaped(dp_size * chips, *block, kind=BF16),
         (key, N.mid): shaped(chips if dp_first else dp_size, *block, kind=BF16),
         (key, N.chip_in): shaped(far_chips, *(block if dp_first else (dp_size, *block)), kind=BF16),
+        (key, N.part): shaped(*block, kind=BF16),
         (key, N.row_in): shaped(far_rows, *((chips, *block) if dp_first else block), kind=BF16),
     }
 
@@ -888,7 +947,7 @@
     refs = list(refs)
     hbm = {n: refs.pop(0) for n in in_names + out_names}
     held_refs = {n: refs.pop(0) for n in held_names}
-    send_sem, recv_sem, held_sem = refs
+    vec_ref, cross_vec_ref, send_sem, recv_sem, held_sem = refs
     wires = Wires(send_sem, recv_sem, wire_names, hbm.values())
     chips, dp_size = wires.chips, wires.dp_size
     length, width = hbm[N.x].shape[1:]
@@ -899,7 +958,7 @@
     for copy in held_copies.values():
         copy.start()
     held = {n: Held(r) for n, r in held_refs.items()}
-    vec, cross_vec = held[N.vec], held[N.cross_vec]
+    vec, cross_vec = Held(vec_ref), Held(cross_vec_ref)
     ticks, last = range(micro), micro - 1
     back_scratch = (pltpu.VMEM((length, width), BF16),)
 
@@ -915,51 +974,56 @@
         return Rows([arrived.at[i] for i in range(wires.seq_size)])
 
     def self_forward(m):
-        step(
+        return (
             self_kernel,
             [inputs(m), held[N.w_qkv], held[N.w_mix], vec, b(N.self_bias, m)],
             [b(n, m) for n in (N.q, N.k, N.v, N.mixed, N.lse, N.summed, N.hidden, N.squares)],
+            (),
         )
 
     def ffn_forward(m, middle):
-        step(
+        return (
             ffn_kernel,
             [b(middle, m), vec, held[N.w_in], held[N.b_in], held[N.w_out]],
             [b(n, m) for n in (N.act, N.slope, N.final_sum, N.low_middle)] + [hbm[N.layer_out].at[m]],
+            (),
         )
 
     def ffn_back(m, grad):
-        step(
+        return (
             ffn_back_kernel,
             [grad, b(N.final_sum, m), vec, held[N.w_out], b(N.slope, m), held[N.w_in]],
             [b(n, m) for n in (N.dy3, N.d_inner, N.d_middle, N.ffn_small)],
+            (),
         )
 
     def cross_forward(m):
-        step(
+        return (
             cross_kernel,
             [b(N.hidden, m), held[N.cross_q], cross_vec, memory(m), held[N.cross_kv], b(N.cross_bias, m), held[N.cross_out]],
             [b(n, m) for n in (N.cq, N.ck, N.cv, N.cross_mixed, N.cross_lse, N.cross_sum, N.middle, N.low_hidden)],
+            (),
         )
 
     def cross_back(m):
-        step(
+        return (
             cross_back_kernel,
             [b(N.d_middle, m), b(N.cross_sum, m), cross_vec, held[N.cross_out], b(N.cross_mixed, m), b(N.cq, m), b(N.ck, m),
              b(N.cross_bias, m), b(N.cross_lse, m), b(N.cv, m), held[N.cross_q], held[N.cross_kv]],
             [b(n, m) for n in (N.dyc, N.dcq, N.dckv, N.d_middle, N.dm_keep, N.dm_send, N.cross_small)],
             back_scratch,
+            lambda: wires.start((N.dm_core, m), [(b(N.dm_send, m), b(N.dm_core_in, m), wires.twin)]),
         )
 
     def self_back(m):
-        step(
+        return (
             self_back_kernel,
             [b(N.d_middle, m), b(N.summed, m), vec, held[N.w_mix], b(N.mixed, m), b(N.q, m), b(N.k, m), b(N.self_bias, m),
              b(N.lse, m), b(N.v, m), held[N.w_qkv]],
             [b(n, m) for n in (N.dy, N.dq, N.dkv, N.dx_own, N.dx_keep, N.dx_send, N.self_small)],
             back_scratch,
+            lambda: wires.start((N.dx_core, m), [(b(N.dx_send, m), b(N.dx_core_in, m), wires.twin)]),
         )
-        wires.start((N.dx_core, m), [(b(N.dx_send, m), b(N.dx_core_in, m), wires.twin)])
 
     def dx_core(m):
         wires.arrived((N.dx_core, m), b(N.dx_core_in, m))
@@ -975,26 +1039,53 @@
             wires.arrived((N.dx_chip, k, m), b(N.dx_chip_in, m).at[k - 1])
         step(add_lead_kernel, [b(N.dx_sum, m), b(N.dx_chip_in, m)], [hbm[N.input_grad].at[m]])
 
-    def dm_start(m):
-        wires.start((N.dm_core, m), [(b(N.dm_send, m), b(N.dm_core_in, m), wires.twin)])
+    part_rows = length // 2
+
+    def part(h):
+        return pl.ds(h * part_rows, part_rows)
 
     def dm_core(m):
         wires.arrived((N.dm_core, m), b(N.dm_core_in, m))
         step(add_kernel, [b(N.dm_keep, m), b(N.dm_core_in, m)], [b(N.dm_sum, m)])
-        for k in range(1, chips):
-            source = b(N.dm_sum, m).at[pl.ds(k * length, length)]
-            wires.start((N.dm_chip, k, m), [(source, b(N.dm_chip_in, m).at[k - 1], wires.chip(k))])
+        for h in range(2):
+            for k in range(1, chips):
+                source = b(N.dm_sum, m).at[pl.ds(k * length + h * part_rows, part_rows)]
+                wires.start((N.dm_chip, k, m, h), [(source, b(N.dm_chip_in, m).at[k - 1, part(h)], wires.chip(k))])
 
     def dm_chip(m):
-        for k in range(1, chips):
-            wires.arrived((N.dm_chip, k, m), b(N.dm_chip_in, m).at[k - 1])
-        step(add_lead_kernel, [b(N.dm_sum, m).at[0:length], b(N.dm_chip_in, m)], [b(N.dm, m)])
-        wires.start((N.dm, m), [(b(N.dm, m), b(N.d_memory, m), wires.across)])
+        for h in range(2):
+            terms = [b(N.dm_sum, m).at[part(h)]]
+            for k in range(1, chips):
+                terms.append(b(N.dm_chip_in, m).at[k - 1, part(h)])
+                wires.arrived((N.dm_chip, k, m, h), terms[-1])
+            step(add_kernel, terms, [b(N.dm, m).at[part(h)]])
+            wires.start((N.dm, m, h), [(b(N.dm, m).at[part(h)], b(N.d_memory, m).at[part(h)], wires.across)])
+
+    def dm_end(m):
+        for h in range(2):
+            wires.arrived((N.dm, m, h), b(N.d_memory, m).at[part(h)])
+
+    def memory_send(m):
+        for h in range(2):
+            source, target = hbm[N.layer_out].at[m, part(h)], b(N.memory, m).at[0, part(h)]
+            wires.start((N.m, m, h), [(source, target, wires.across)])
+
+    def memory_block(h):
+        return lambda target, i: target.at[i, part(h)]
 
     def memory_start(m):
         arrived = b(N.memory, m)
-        wires.arrived((N.m, m), arrived.at[0])
-        gather_start(wires, (N.m, m), arrived.at[0], arrived)
+        for h in range(2):
+            wires.arrived((N.m, m, h), arrived.at[0, part(h)])
+            gather_start(wires, ((N.m, m), h), arrived.at[0, part(h)], arrived, memory_block(h))
+
+    def memory_pass(m):
+        for h in range(2):
+            gather_pass(wires, ((N.m, m), h), b(N.memory, m), memory_block(h))
+
+    def memory_end(m):
+        for h in range(2):
+            gather_end(wires, ((N.m, m), h), b(N.memory, m), memory_block(h))
 
     def weights(products, out, regroup=0):
         operands, plan = [], []
@@ -1003,14 +1094,14 @@
             operands += list(lefts) + list(rights)
             plan.append((tuple(range(n, n + count)), tuple(range(n + count, n + 2 * count)), column))
         scratch = (pltpu.VMEM(out.shape, F32),) if regroup else ()
-        step(functools.partial(weight_kernel, plan, regroup), operands, [out], scratch)
+        return (functools.partial(weight_kernel, plan, regroup), operands, [out], scratch)
 
     def all_b(name):
         return [b(name, m) for m in ticks]
 
     def cross_weights():
         regroup = width // 2 // (dp_size * wires.seq_size) if pieces else 0
-        weights(
+        return weights(
             [
                 (all_b(N.low_hidden), all_b(N.dcq), 0),
                 ([memory(m) for m in ticks], all_b(N.dckv), width),
@@ -1021,13 +1112,13 @@
         )
 
     def out_weights():
-        weights([(all_b(N.act), all_b(N.dy3), 0)], hbm[N.g_out])
+        return weights([(all_b(N.act), all_b(N.dy3), 0)], hbm[N.g_out])
 
     def in_weights():
-        weights([(all_b(N.low_middle), all_b(N.d_inner), 0)], hbm[N.g_in])
+        return weights([(all_b(N.low_middle), all_b(N.d_inner), 0)], hbm[N.g_in])
 
     def attn_weights():
-        weights(
+        return weights(
             [
                 ([hbm[N.x].at[m] for m in ticks], all_b(N.dq), 0),
                 ([inputs(m) for m in ticks], all_b(N.dkv), width),
@@ -1043,6 +1134,15 @@
     def stage(unit, which):
         for sums in units.get(unit, ()):
             which(sums)
+
+    def second_adds(unit, dp_first):
+        for sums in units.get(unit, ()):
+            if sums.dp_first == dp_first:
+                sums.second_add()
+
+    def core_adds(unit):
+        if unit in units:
+            group(*[sums.core_add() for sums in units[unit]])
 
     wires.barrier()
     gather_start(wires, N.i, hbm[N.ids], hbm[N.ids_all])
@@ -1057,111 +1157,126 @@
     gather_pass(wires, (N.x, 0), b(N.x_all, 0))
     for m in range(1, micro):
         gather_start(wires, (N.x, m), hbm[N.x].at[m], b(N.x_all, m))
-    for n in (N.vec, N.w_qkv, N.w_mix):
+    for n in (N.bias, N.gain, N.w_qkv, N.w_mix):
         held_copies[n].wait()
+    vec_ref[0:6, :] = held_refs[N.bias][...]
+    vec_ref[6:8, :] = held_refs[N.gain][...]
     gather_end(wires, (N.x, 0), b(N.x_all, 0))
-    self_forward(0)
+    group(self_forward(0))
     for n in held_names:
-        if n not in (N.vec, N.w_qkv, N.w_mix):
+        if n not in (N.bias, N.gain, N.w_qkv, N.w_mix):
             held_copies[n].wait()
+    cross_vec_ref[0:4, :] = held_refs[N.cross_shift][...]
+    cross_vec_ref[4:5, :] = held_refs[N.cross_scale][...]
     for m in range(1, micro):
         gather_pass(wires, (N.x, m), b(N.x_all, m))
 
     @wires.only(0)
     def _():
         for m in ticks:
-            ffn_forward(m, N.hidden)
-            wires.start((N.m, m), [(hbm[N.layer_out].at[m], b(N.memory, m).at[0], wires.across)])
+            group(ffn_forward(m, N.hidden))
+            memory_send(m)
             if m < last:
                 gather_end(wires, (N.x, m + 1), b(N.x_all, m + 1))
-                self_forward(m + 1)
-        for m in ticks:
-            wires.arrived((N.dm, m), b(N.d_memory, m))
-            if m < last:
-                ffn_back(m, b(N.d_memory, m))
-                self_back(m)
-                dx_core(m)
-        step(
-            ffn_norm_kernel,
-            [b(N.d_memory, last), b(N.final_sum, last), vec],
-            [b(N.dy3, last), hbm[N.d_final], hbm[N.norm_small]],
+                group(self_forward(m + 1))
+        for m in range(last):
+            dm_end(m)
+            group(ffn_back(m, b(N.d_memory, m)), self_back(m))
+            dx_core(m)
+        dm_end(last)
+        group(
+            (
+                ffn_norm_kernel,
+                [b(N.d_memory, last), b(N.final_sum, last), vec],
+                [b(N.dy3, last), hbm[N.d_final], hbm[N.norm_small]],
+                (),
+            ),
+            out_weights(),
         )
+        stage(N.g_out, Sums.core_start)
+        group(
+            (
+                ffn_rest_kernel,
+                [b(N.dy3, last), hbm[N.d_final], hbm[N.norm_small], held[N.w_out], b(N.slope, last), held[N.w_in]],
+                [b(N.d_inner, last), b(N.d_middle, last), b(N.ffn_small, last)],
+                (),
+            )
+        )
+        core_adds(N.g_out)
 
     @wires.only(1)
     def _():
         for m in range(1, micro):
             gather_end(wires, (N.x, m), b(N.x_all, m))
-            self_forward(m)
+            group(self_forward(m))
         memory_start(0)
-        gather_pass(wires, (N.m, 0), b(N.memory, 0))
+        memory_pass(0)
         for m in ticks:
-            gather_end(wires, (N.m, m), b(N.memory, m))
-            cross_forward(m)
-            if m < last:
-                memory_start(m + 1)
-            if m > 0:
-                dm_core(m - 1)
-            ffn_forward(m, N.middle)
-            if m < last:
-                gather_pass(wires, (N.m, m + 1), b(N.memory, m + 1))
-            ffn_back(m, hbm[N.cotangent].at[m])
-            if m > 0:
-                dm_chip(m - 1)
-            cross_back(m)
-            dm_start(m)
+            memory_end(m)
+
+            def between_forward(m=m):
+                if m < last:
+                    memory_start(m + 1)
+                if m > 0:
+                    dm_core(m - 1)
+
+            def between_back(m=m):
+                if m < last:
+                    memory_pass(m + 1)
+                if m > 0:
+                    dm_chip(m - 1)
+
+            group(cross_forward(m), between_forward, ffn_forward(m, N.middle))
+            group(ffn_back(m, hbm[N.cotangent].at[m]), between_back, cross_back(m))
         dm_core(last)
-        cross_weights()
+        group(out_weights())
+        stage(N.g_out, Sums.core_start)
         dm_chip(last)
+        core_adds(N.g_out)
+        group(cross_weights())
         stage(N.g_cross, Sums.core_start)
-
-    out_weights()
-    stage(N.g_out, Sums.core_start)
-
-    @wires.only(0)
-    def _():
-        step(
-            ffn_rest_kernel,
-            [b(N.dy3, last), hbm[N.d_final], hbm[N.norm_small], held[N.w_out], b(N.slope, last), held[N.w_in]],
-            [b(N.d_inner, last), b(N.d_middle, last), b(N.ffn_small, last)],
-        )
-
-    @wires.only(1)
-    def _():
-        stage(N.g_cross, Sums.core_add)
-
-    stage(N.g_out, Sums.core_add)
-    in_weights()
+        second_adds(N.g_out, False)
+        core_adds(N.g_cross)
+
+    group(in_weights())
     stage(N.g_in, Sums.core_start)
 
     @wires.only(1)
     def _():
         for m in range(last):
-            self_back(m)
-
-    stage(N.g_in, Sums.core_add)
+            group(self_back(m))
+
+    core_adds(N.g_in)
 
     @wires.only(1)
     def _():
+        stage(N.g_cross, Sums.second_add)
+        second_adds(N.g_out, True)
         for m in range(last):
             dx_core(m)
-        stage(N.g_cross, Sums.second_add)
-
-    self_back(last)
-    attn_weights()
-    stage(N.g_attn, Sums.core_start)
+
+    group(self_back(last))
     step(
         functools.partial(small_kernel, micro),
         all_b(N.self_small) + all_b(N.ffn_small) + all_b(N.squares) + all_b(N.cross_small),
         [hbm[N.small]],
     )
     wires.start(N.small_core, [(hbm[N.small], hbm[N.small_core_in], wires.twin)])
-    stage(N.g_attn, Sums.core_add)
-    stage(N.g_out, Sums.second_add)
-    dx_core(last)
+
+    @wires.only(0)
+    def _():
+        second_adds(N.g_out, False)
+        second_adds(N.g_out, True)
+
+    group(attn_weights())
+    stage(N.g_attn, Sums.core_start)
     wires.arrived(N.small_core, hbm[N.small_core_in])
     step(add_kernel, [hbm[N.small], hbm[N.small_core_in]], [hbm[N.small_core_sum]])
     for k in range(1, chips):
         wires.start((N.small_chip, k), [(hbm[N.small_core_sum], hbm[N.small_chip_in].at[k - 1], wires.chip(k))])
+    stage(N.g_in, Sums.second_add)
+    core_adds(N.g_attn)
+    dx_core(last)
 
     @wires.only(1)
     def _():
@@ -1170,17 +1285,15 @@
             half = width // 2 // (dp_size * wires.seq_size)
             wires.start(N.cross_half, [(hbm[N.g_cross, N.out].at[0:half], hbm[N.cross_half], wires.across)])
 
-    stage(N.g_in, Sums.second_add)
     for k in range(1, chips):
         wires.arrived((N.small_chip, k), hbm[N.small_chip_in].at[k - 1])
     step(add_lead_kernel, [hbm[N.small_core_sum], hbm[N.small_chip_in]], [hbm[N.small_chip_sum]])
     moves = [(hbm[N.small_chip_sum], hbm[N.small_row_in].at[k - 1], wires.row(k)) for k in range(1, dp_size)]
     wires.start(N.small_row, moves, hbm[N.small_row_in])
+    stage(N.g_out, Sums.third_add)
     for m in range(last):
         dx_end(m)
-    stage(N.g_out, Sums.third_add)
     stage(N.g_attn, Sums.second_add)
-    dx_end(last)
     wires.arrived(N.small_row, hbm[N.small_row_in])
     step(add_lead_kernel, [hbm[N.small_chip_sum], hbm[N.small_row_in]], [hbm[N.small_sum]])
 
@@ -1188,6 +1301,7 @@
     def _():
         wires.start(N.small_half, [(hbm[N.small_sum].at[16:24], hbm[N.small_half], wires.across)])
 
+    dx_end(last)
     stage(N.g_in, Sums.third_add)
     stage(N.g_attn, Sums.third_add)
 
@@ -1300,11 +1414,8 @@
     fused = width // devices % 16 == 0
     ticks = range(micro)
     x = x_in[0, :, 0]
-    vec = jnp.concatenate([attn_bias[0], gains[0]], 0)
-    cross_vec = jnp.concatenate([cross_bias, cross_gain[None], jnp.zeros((3, width), F32)], 0)
-
-    ids = segments[:, :, 0].reshape(2 * micro, length)
-    ids = jnp.concatenate([ids, jnp.zeros((-2 * micro % 8, length), ids.dtype)], 0)
+
+    ids = segments.reshape(2 * micro, length)
     arrays = {
         N.x: x,
         N.ids: ids,
@@ -1314,11 +1425,13 @@
         N.w_in: ffn_in[0],
         N.w_out: ffn_out[0],
         N.b_in: ffn_bias,
-        N.vec: vec,
+        N.bias: attn_bias[0],
+        N.gain: gains[0],
         N.cross_q: cross_q,
         N.cross_kv: cross_kv,
         N.cross_out: cross_out,
-        N.cross_vec: cross_vec,
+        N.cross_shift: cross_bias,
+        N.cross_scale: cross_gain[None],
     }
     lw, lw_low = shaped(length, width), shaped(length, width, kind=BF16)
     tw_low = shaped(tokens, width, kind=BF16)
@@ -1347,6 +1460,7 @@
         outs[n] = shaped(micro, length, width, kind=BF16)
     outs[N.ids_all] = shaped(seq_size, *ids.shape, kind=ids.dtype)
     outs[N.d_final], outs[N.norm_small] = lw, few
+    outs[N.part] = shaped(length // 2, width, kind=BF16)
     small_shape = shaped(24, width)
     for n in (N.small, N.small_core_in, N.small_core_sum, N.small_chip_sum, N.small_sum):
         outs[n] = small_shape
@@ -1358,9 +1472,11 @@
     }
     wire_names = [N.small_core, N.small_row, N.small_half] + [(N.small_chip, k) for k in range(1, chips)]
     for m in ticks:
-        wire_names += gather_names((N.m, m), chips) + gather_names((N.x, m), chips)
-        wire_names += [(N.m, m), (N.dm, m), (N.dm_core, m), (N.dx_core, m)]
-        wire_names += [(n, k, m) for n in (N.dm_chip, N.dx_chip) for k in range(1, chips)]
+        wire_names += gather_names((N.x, m), chips) + [(N.dm_core, m), (N.dx_core, m)]
+        wire_names += [(N.dx_chip, k, m) for k in range(1, chips)]
+        for h in range(2):
+            wire_names += gather_names(((N.m, m), h), chips) + [(N.m, m, h), (N.dm, m, h)]
+            wire_names += [(N.dm_chip, k, m, h) for k in range(1, chips)]
     pieces = sum_pieces(totals, devices) if fused else []
     for n, total in totals.items():
         outs[n] = shaped(*total, kind=BF16)
@@ -1373,8 +1489,9 @@
         outs[N.cross_half] = shaped(width // 2 // devices, 4 * width)
         wire_names.append(N.cross_half)
     wire_names += gather_names(N.i, chips)
-    held_names = [N.vec, N.w_qkv, N.w_mix, N.w_in, N.b_in, N.w_out, N.cross_vec, N.cross_q, N.cross_kv, N.cross_out]
+    held_names = [N.bias, N.gain, N.w_qkv, N.w_mix, N.w_in, N.b_in, N.w_out, N.cross_shift, N.cross_scale, N.cross_q, N.cross_kv, N.cross_out]
     scratch = [pltpu.VMEM(arrays[n].shape, arrays[n].dtype) for n in held_names]
+    scratch += [pltpu.VMEM((8, width), F32)] * 2
     scratch += [pltpu.SemaphoreType.DMA((len(wire_names),))] * 2 + [pltpu.SemaphoreType.DMA((len(held_names),))]
     results = kernel_call(
         functools.partial(main_body, micro, pieces, list(arrays), list(outs), wire_names, held_names),

time: 369 us -> 333 us (0.902)
  the two profiles are of different devices: /device:TPU:8 before, /device:TPU:10 now
where the time goes in v4:
time: 333 us; the launch traced here: 327 us
  Pallas kernels  321 us (96%)
  local copies, waits for them, and re-layouts  4.46 us (1%)
    pallas_call x1, Pallas kernels, kernel_call(): pl.pallas_call(body, out_shape=list(outs), in_specs=[anywhere] * len(oper...  318 us

profile of v4, /device:TPU:10, one launch (start us, length us, event | category | flops | bytes accessed | tf_op | source)
XLA Modules:
  0.0 327.4 jit_solution(14737429749205070543)
XLA Ops:
  0.6 1.3 broadcast_in_dim.27.refs_14_
  1.9 0.7 reduce
  2.6 0.6 reshape.33.refs_1_
  3.2 1.3 copy.36
  4.6 317.6 %layers.1 = (bf16[256,768]{1,0:T(8,128)(2,1)}, bf16[1024,768]{1,0:T(8,128)(2,1)}, bf16[1024,768]{1,0:T(8,128)(2,1)}, bf16[256,768]{1,0:T(8,128)(2,1)}, f32[6,256...) custom-call(bf16[2,256,768]{2,1,0:T(8,128)(2,1)} %bitcast.29, ...), custom_call_target="tpu_custom_call" | custom-call | flops 36238786560 | bytes 161872896 | tf_op jit(solution)/shard_map/layers/pallas_call | solution.py:1389
  322.1 3.8 %shard_map.262 = (bf16[2,256,768]{2,1,0:T(8,128)(2,1)}, bf16[2,256,768]{2,1,0:T(8,128)(2,1)}, f32[48,2304]{1,0:T(8,128)}, f32[48,768]{1,0:T(8,128)}, f32[48,3072...) custom-call(bf16[2,256,768]{2,1,0:T(8,128)(2,1)} %get-tuple-element., ...), custom_call_target="tpu_custom_call" | custom-call | tf_op jit(solution)/shard_map/pallas_call | solution.py:1545
  325.9 1.3 copy.32

commit v5 on v4

--- a/solution.py
+++ b/solution.py
@@ -410,6 +410,7 @@
         out[8:16, :] += ref[...]
     for ref in crosses:
         out[16:24, :] += jnp.where(lax.axis_index("section") == 1, ref[...], 0.0)
+    io.sent(out)
 
 
 class Moves:
@@ -1028,8 +1029,10 @@
     def dx_core(m):
         wires.arrived((N.dx_core, m), b(N.dx_core_in, m))
         arrived, rest = b(N.dx_core_in, m), (chips - 1) * length
-        step(add_kernel, [b(N.dx_own, m), arrived.at[0:length]], [b(N.dx_sum, m)])
-        step(add_kernel, [b(N.dx_keep, m), arrived.at[pl.ds(length, rest)]], [b(N.dx_rest, m)])
+        group(
+            (add_kernel, [b(N.dx_keep, m), arrived.at[pl.ds(length, rest)]], [b(N.dx_rest, m)], ()),
+            (add_kernel, [b(N.dx_own, m), arrived.at[0:length]], [b(N.dx_sum, m)], ()),
+        )
         for k in range(1, chips):
             source = b(N.dx_rest, m).at[pl.ds((k - 1) * length, length)]
             wires.start((N.dx_chip, k, m), [(source, b(N.dx_chip_in, m).at[k - 1], wires.chip(k))])
@@ -1159,8 +1162,8 @@
         gather_start(wires, (N.x, m), hbm[N.x].at[m], b(N.x_all, m))
     for n in (N.bias, N.gain, N.w_qkv, N.w_mix):
         held_copies[n].wait()
-    vec_ref[0:6, :] = held_refs[N.bias][...]
-    vec_ref[6:8, :] = held_refs[N.gain][...]
+    vec_ref[0:6, :] = held_refs[N.bias][0]
+    vec_ref[6:8, :] = held_refs[N.gain][0]
     gather_end(wires, (N.x, 0), b(N.x_all, 0))
     group(self_forward(0))
     for n in held_names:
@@ -1255,13 +1258,16 @@
         for m in range(last):
             dx_core(m)
 
-    group(self_back(last))
-    step(
-        functools.partial(small_kernel, micro),
-        all_b(N.self_small) + all_b(N.ffn_small) + all_b(N.squares) + all_b(N.cross_small),
-        [hbm[N.small]],
+    group(
+        self_back(last),
+        (
+            functools.partial(small_kernel, micro),
+            all_b(N.self_small) + all_b(N.ffn_small) + all_b(N.squares) + all_b(N.cross_small),
+            [hbm[N.small]],
+            (),
+            lambda: wires.start(N.small_core, [(hbm[N.small], hbm[N.small_core_in], wires.twin)]),
+        ),
     )
-    wires.start(N.small_core, [(hbm[N.small], hbm[N.small_core_in], wires.twin)])
 
     @wires.only(0)
     def _():
@@ -1425,8 +1431,8 @@
         N.w_in: ffn_in[0],
         N.w_out: ffn_out[0],
         N.b_in: ffn_bias,
-        N.bias: attn_bias[0],
-        N.gain: gains[0],
+        N.bias: attn_bias,
+        N.gain: gains,
         N.cross_q: cross_q,
         N.cross_kv: cross_kv,
         N.cross_out: cross_out,

time: 333 us -> 330 us (level)
  the two profiles are of different devices: /device:TPU:10 before, /device:TPU:0 now
where the time goes in v5:
time: 330 us; the launch traced here: 324 us
  Pallas kernels  318 us (96%)
  local copies, waits for them, and re-layouts  4.46 us (1%)
    pallas_call x1, Pallas kernels, kernel_call(): pl.pallas_call(body, out_shape=list(outs), in_specs=[anywhere] * len(oper...  314 us

profile of v5, /device:TPU:0, one launch (start us, length us, event | category | flops | bytes accessed | tf_op | source)
XLA Modules:
  0.0 324.2 jit_solution(3273904161085074548)
XLA Ops:
  0.6 1.3 broadcast_in_dim.27.refs_14_
  1.9 0.7 reduce
  2.6 0.6 reshape.33.refs_1_
  3.2 1.3 copy.30.refs_8_
  4.6 314.3 %layers.1 = (bf16[256,768]{1,0:T(8,128)(2,1)}, bf16[1024,768]{1,0:T(8,128)(2,1)}, bf16[1024,768]{1,0:T(8,128)(2,1)}, bf16[256,768]{1,0:T(8,128)(2,1)}, f32[6,256...) custom-call(bf16[2,256,768]{2,1,0:T(8,128)(2,1)} %bitcast.24, ...), custom_call_target="tpu_custom_call" | custom-call | flops 36238786560 | bytes 161872896 | tf_op jit(solution)/shard_map/layers/pallas_call | solution.py:1395
  318.8 3.8 %shard_map.262 = (bf16[2,256,768]{2,1,0:T(8,128)(2,1)}, bf16[2,256,768]{2,1,0:T(8,128)(2,1)}, f32[48,2304]{1,0:T(8,128)}, f32[48,768]{1,0:T(8,128)}, f32[48,3072...) custom-call(bf16[2,256,768]{2,1,0:T(8,128)(2,1)} %get-tuple-element., ...), custom_call_target="tpu_custom_call" | custom-call | tf_op jit(solution)/shard_map/pallas_call | solution.py:1551
  322.7 1.3 copy.33
